TPU v7x, 32 devices: a whole 2x2x4 slice. The times are simulated.
32 devices in a mesh: clip: 16 (over z, y, core), frame: 2 (over x).
Axes of the slice: x: 2, y: 2, z: 4, core: 2. Of those that a mesh axis runs over, the one named last changes fastest.
Arguments:
- frames_in: bfloat16 [16, 8, 16, 16, 1024], P('clip', 'frame'), may hold values from -6 to 6
- size_group: int32 [16], P('clip'), may hold values from 0 to 2
- modulation: float32 [16, 12, 1024], P('clip'), may hold values from -3 to 3
- w_qkv: bfloat16 [1024, 2, 3072], P('clip'), may hold values from -0.1875 to 0.1875
- w_proj: bfloat16 [1024, 2, 1024], P('clip'), may hold values from -0.75 to 0.75
- w_up: bfloat16 [1024, 2, 4096], P('clip'), may hold values from -0.1875 to 0.1875
- w_down: bfloat16 [4096, 2, 1024], P('clip'), may hold values from -0.09375 to 0.09375
- table_sp: float32 [16, 961], replicated, may hold values from -3 to 3
- table_st: float32 [16, 3375], replicated, may hold values from -3 to 3
- cotangent: bfloat16 [16, 8, 16, 16, 1024], P('clip', 'frame'), may hold values from -6 to 6
Outputs:
- mixed: bfloat16 [16, 8, 16, 16, 1024], P('clip', 'frame')
- grad_in: bfloat16 [16, 8, 16, 16, 1024], P('clip', 'frame')
- grad_modulation: float32 [16, 12, 1024], P('clip')
- grad_qkv: float32 [1024, 2, 3072], P('clip')
- grad_proj: float32 [1024, 2, 1024], P('clip')
- grad_up: float32 [1024, 2, 4096], P('clip')
- grad_down: float32 [4096, 2, 1024], P('clip')
- grad_table_sp: float32 [16, 961], replicated
- grad_table_st: float32 [16, 3375], replicated
All inputs are finite; a program needn't handle non-finite values.
Results may differ from a plain program's by a relative error of at most 0.028.
Values may be sent and summed in bfloat16 or wider, within the bound.
A program may use at most 512 MiB of HBM per device.

v0:
```python
import jax
import jax.numpy as jnp
from jax import lax
from jax.sharding import PartitionSpec as P

SWIN = 16
TWIN = 8
FRAMES = 8
FILLED = 5


NEG_FILL = -1000000000.0
NORM_EPS = 1e-06
HIGHEST = lax.Precision.HIGHEST


def layer_norm(values):
    centered = values - jnp.mean(values, axis=-1, keepdims=True)
    spread = jnp.mean(centered * centered, axis=-1, keepdims=True)
    return centered * lax.rsqrt(spread + NORM_EPS)


def modulate(values, shift_row, scale_row):
    return layer_norm(values) * (1.0 + scale_row) + shift_row


def gelu_tanh(values):
    return jax.nn.gelu(values, approximate=True)


def row_of(mod_rows, which):
    return mod_rows[:, which][:, None, None, None, :]


def clip_sum(values):
    return jnp.sum(values, axis=(1, 2, 3))


def flat_dot(values, weight):
    flat_in = values.reshape(-1, values.shape[-1])
    flat_out = jnp.dot(flat_in, weight, preferred_element_type=jnp.float32)
    return flat_out.reshape(values.shape[:-1] + (weight.shape[1],))


def back_dot(grad_values, weight):
    flat_in = grad_values.reshape(-1, grad_values.shape[-1])
    flat_out = jnp.einsum("nb,ab->na", flat_in, weight, preferred_element_type=jnp.float32)
    return flat_out.reshape(grad_values.shape[:-1] + (weight.shape[0],))


def outer_dot(left_values, right_values):
    left_flat = left_values.reshape(-1, left_values.shape[-1])
    right_flat = right_values.reshape(-1, right_values.shape[-1])
    return jnp.einsum("na,nb->ab", left_flat, right_flat, preferred_element_type=jnp.float32)


def split_heads(values, n_heads):
    return values.reshape(values.shape[0], values.shape[1], n_heads, -1)


def offset_pick(side_len):
    position = jnp.arange(side_len, dtype=jnp.int32)
    offsets = position[:, None] - position[None, :] + side_len - 1
    targets = jnp.arange(2 * side_len - 1, dtype=jnp.int32)
    return (offsets[:, :, None] == targets[None, None, :]).astype(jnp.float32)


def expand_bias(table, side_len):
    one_hot = offset_pick(side_len)
    rows_done = jnp.einsum("hab,xya->hxyb", table, one_hot, precision=HIGHEST)
    full_bias = jnp.einsum("hxyb,uvb->hxuyv", rows_done, one_hot, precision=HIGHEST)
    return full_bias.reshape(table.shape[0], side_len * side_len, side_len * side_len)


def cube_bias(table_st, first_frame, local_frames):
    n_heads = table_st.shape[0]
    span_frames = 2 * FRAMES - 1
    side_span = 2 * TWIN - 1
    table_cube = table_st.reshape(n_heads, span_frames, side_span * side_span)
    query_frames = first_frame + jnp.arange(local_frames, dtype=jnp.int32)
    key_frames = jnp.arange(FRAMES, dtype=jnp.int32)
    offsets = query_frames[:, None] - key_frames[None, :] + FRAMES - 1
    choose = (
        offsets[:, :, None] == jnp.arange(span_frames, dtype=jnp.int32)[None, None, :]
    ).astype(jnp.float32)
    picked = jnp.einsum("hoz,jfo->hjfz", table_cube, choose, precision=HIGHEST)
    squares = expand_bias(picked.reshape(-1, side_span, side_span), TWIN)
    squares = squares.reshape(n_heads, local_frames, FRAMES, TWIN * TWIN, TWIN * TWIN)
    squares = squares.transpose(0, 1, 3, 2, 4)
    return squares.reshape(n_heads, local_frames * TWIN * TWIN, FRAMES * TWIN * TWIN)


def spatial_windows(values):
    n_clips, n_frames, n_rows, n_cols, n_depth = values.shape
    blocked = values.reshape(n_clips, n_frames, n_rows // SWIN, SWIN, n_cols // SWIN, SWIN, n_depth)
    return blocked.transpose(0, 1, 2, 4, 3, 5, 6).reshape(-1, SWIN * SWIN, n_depth)


def spatial_unwindow(values, full_shape):
    n_clips, n_frames, n_rows, n_cols, n_depth = full_shape
    blocked = values.reshape(n_clips, n_frames, n_rows // SWIN, n_cols // SWIN, SWIN, SWIN, n_depth)
    return blocked.transpose(0, 1, 2, 4, 3, 5, 6).reshape(full_shape)


def cube_windows(values):
    n_clips, n_frames, n_rows, n_cols, n_depth = values.shape
    blocked = values.reshape(n_clips, n_frames, n_rows // TWIN, TWIN, n_cols // TWIN, TWIN, n_depth)
    blocked = blocked.transpose(0, 2, 4, 1, 3, 5, 6)
    return blocked.reshape(
        n_clips * (n_rows // TWIN) * (n_cols // TWIN), n_frames * TWIN * TWIN, n_depth
    )


def cube_unwindow(values, full_shape):
    n_clips, n_frames, n_rows, n_cols, n_depth = full_shape
    blocked = values.reshape(n_clips, n_rows // TWIN, n_cols // TWIN, n_frames, TWIN, TWIN, n_depth)
    return blocked.transpose(0, 3, 1, 4, 2, 5, 6).reshape(full_shape)


def soft_scores(query_win, key_win, bias, key_ok, score_scale):
    scores = jnp.einsum("nqhd,nkhd->nhqk", query_win, key_win, preferred_element_type=jnp.float32)
    scores = scores * score_scale + bias[None]
    scores = jnp.where(key_ok[:, None, None, :], scores, NEG_FILL)
    row_top = jnp.max(scores, axis=-1, keepdims=True)
    expo_values = jnp.exp(scores - row_top)
    return expo_values / jnp.sum(expo_values, axis=-1, keepdims=True)


def block_forward(
    stream,
    mod_rows,
    weights,
    n_heads,
    bias,
    key_ok,
    to_windows,
    from_windows,
    fetch_keys,
    score_scale,
):
    qkv_w, proj_w, up_w, down_w = weights
    width_d = stream.shape[-1]
    normed_a = modulate(stream, row_of(mod_rows, 0), row_of(mod_rows, 1)).astype(jnp.bfloat16)
    qkv_values = flat_dot(normed_a, qkv_w).astype(jnp.bfloat16)
    key_local = qkv_values[..., width_d : 2 * width_d]
    value_local = qkv_values[..., 2 * width_d :]
    query_win = split_heads(to_windows(qkv_values[..., :width_d]), n_heads)
    key_flat, value_flat = fetch_keys(key_local, value_local)
    key_win = split_heads(key_flat, n_heads)
    value_win = split_heads(value_flat, n_heads)
    soft_probs = soft_scores(query_win, key_win, bias, key_ok, score_scale)
    att_win = jnp.einsum(
        "nhqk,nkhd->nqhd",
        soft_probs.astype(jnp.bfloat16),
        value_win,
        preferred_element_type=jnp.float32,
    ).astype(jnp.bfloat16)
    att_out = from_windows(
        att_win.reshape(att_win.shape[0], att_win.shape[1], width_d), stream.shape
    )
    proj_out = flat_dot(att_out, proj_w)
    mid_stream = stream + row_of(mod_rows, 2) * proj_out
    normed_m = modulate(mid_stream, row_of(mod_rows, 3), row_of(mod_rows, 4)).astype(jnp.bfloat16)
    up_value = flat_dot(normed_m, up_w)
    active = gelu_tanh(up_value).astype(jnp.bfloat16)
    down_out = flat_dot(active, down_w)
    result = mid_stream + row_of(mod_rows, 5) * down_out
    saved = (
        stream,
        normed_a,
        query_win,
        key_win,
        value_win,
        key_local,
        value_local,
        att_out,
        proj_out,
        mid_stream,
        normed_m,
        up_value,
        active,
        down_out,
    )
    return (result, saved)


def block_backward(
    grad_out,
    saved,
    mod_rows,
    weights,
    n_heads,
    bias,
    key_ok,
    to_windows,
    from_windows,
    return_keys,
    key_win,
    value_win,
    score_scale,
):
    (
        stream,
        normed_a,
        query_win,
        unused_key,
        unused_value,
        key_local,
        value_local,
        att_out,
        proj_out,
        mid_stream,
        normed_m,
        up_value,
        active,
        down_out,
    ) = saved
    qkv_w, proj_w, up_w, down_w = weights
    n_clips = stream.shape[0]
    width_d = stream.shape[-1]
    grad_down_v = (row_of(mod_rows, 5) * grad_out).astype(jnp.bfloat16)
    gate_m_grad = clip_sum(grad_out * down_out)
    down_grad = outer_dot(active, grad_down_v)
    grad_act = back_dot(grad_down_v, down_w)
    unused_gelu, gelu_pull = jax.vjp(gelu_tanh, up_value)
    grad_up_v = gelu_pull(grad_act)[0].astype(jnp.bfloat16)
    up_grad = outer_dot(normed_m, grad_up_v)
    grad_normed = back_dot(grad_up_v, up_w)
    unused_norm, norm_pull = jax.vjp(modulate, mid_stream, row_of(mod_rows, 3), row_of(mod_rows, 4))
    grad_mid, shift_m_grad, scale_m_grad = norm_pull(grad_normed)
    grad_mid = grad_mid + grad_out
    grad_proj_v = (row_of(mod_rows, 2) * grad_mid).astype(jnp.bfloat16)
    gate_a_grad = clip_sum(grad_mid * proj_out)
    proj_grad = outer_dot(att_out, grad_proj_v)
    grad_att = back_dot(grad_proj_v, proj_w).astype(jnp.bfloat16)
    grad_att_win = split_heads(to_windows(grad_att), n_heads)
    soft_probs = soft_scores(query_win, key_win, bias, key_ok, score_scale)
    grad_probs = jnp.einsum(
        "nqhd,nkhd->nhqk", grad_att_win, value_win, preferred_element_type=jnp.float32
    )
    row_delta = jnp.sum(soft_probs * grad_probs, axis=-1, keepdims=True)
    grad_scores = (soft_probs * (grad_probs - row_delta)).astype(jnp.bfloat16)
    grad_bias = jnp.sum(grad_scores.astype(jnp.float32), axis=0)
    grad_query = (
        jnp.einsum("nhqk,nkhd->nqhd", grad_scores, key_win, preferred_element_type=jnp.float32)
        * score_scale
    )
    grad_key = (
        jnp.einsum("nhqk,nqhd->nkhd", grad_scores, query_win, preferred_element_type=jnp.float32)
        * score_scale
    )
    grad_value = jnp.einsum(
        "nhqk,nqhd->nkhd",
        soft_probs.astype(jnp.bfloat16),
        grad_att_win,
        preferred_element_type=jnp.float32,
    )
    n_win = grad_query.shape[0]
    grad_query = from_windows(grad_query.reshape(n_win, grad_query.shape[1], width_d), stream.shape)
    grad_key_full, grad_value_full = return_keys(
        grad_key.reshape(n_win, grad_key.shape[1], width_d),
        grad_value.reshape(n_win, grad_value.shape[1], width_d),
    )
    grad_qkv_v = jnp.concatenate([grad_query, grad_key_full, grad_value_full], axis=-1).astype(
        jnp.bfloat16
    )
    qkv_grad = outer_dot(normed_a, grad_qkv_v)
    grad_normed = back_dot(grad_qkv_v, qkv_w)
    unused_norm, norm_pull = jax.vjp(modulate, stream, row_of(mod_rows, 0), row_of(mod_rows, 1))
    grad_stream, shift_a_grad, scale_a_grad = norm_pull(grad_normed)
    grad_stream = grad_stream + grad_mid
    mod_grad = jnp.stack(
        [
            shift_a_grad.reshape(n_clips, width_d),
            scale_a_grad.reshape(n_clips, width_d),
            gate_a_grad,
            shift_m_grad.reshape(n_clips, width_d),
            scale_m_grad.reshape(n_clips, width_d),
            gate_m_grad,
        ],
        axis=1,
    )
    return (grad_stream, mod_grad, (qkv_grad, proj_grad, up_grad, down_grad), grad_bias)


def on_device(
    frames_in, size_group, modulation, w_qkv, w_proj, w_up, w_down, table_sp, table_st, cotangent
):
    n_clips, local_frames, n_rows, n_cols, width_d = frames_in.shape
    n_heads = table_sp.shape[0]
    score_scale = (width_d // n_heads) ** (-0.5)
    first_frame = lax.axis_index("frame") * local_frames
    local_shape = (n_clips, local_frames, n_rows, n_cols, width_d)
    whole_shape = (n_clips, FRAMES, n_rows, n_cols, width_d)
    gathered = (
        lax.all_gather(w_qkv, "clip", axis=0, tiled=True),
        lax.all_gather(w_proj, "clip", axis=0, tiled=True),
        lax.all_gather(w_up, "clip", axis=0, tiled=True),
        lax.all_gather(w_down, "clip", axis=0, tiled=True),
    )
    column_ids = jnp.arange(n_cols, dtype=jnp.int32)
    column_limit = n_cols - 3 * (2 - size_group)
    wide_ok = column_ids[None, :] < column_limit[:, None]
    local_ok = jnp.broadcast_to(wide_ok[:, None, None, :], (n_clips, local_frames, n_rows, n_cols))
    spatial_ok = spatial_windows(local_ok[..., None])[..., 0]
    frame_ok = jnp.arange(FRAMES, dtype=jnp.int32) < FILLED
    cube_grid = wide_ok[:, None, None, :] & frame_ok[None, :, None, None]
    cube_grid = jnp.broadcast_to(cube_grid, (n_clips, FRAMES, n_rows, n_cols))
    cube_ok = cube_windows(cube_grid[..., None])[..., 0]
    span_sp = 2 * SWIN - 1

    def build_spatial(table):
        return expand_bias(table.reshape(n_heads, span_sp, span_sp), SWIN)

    def build_cube(table):
        return cube_bias(table, first_frame, local_frames)

    bias_sp, pull_sp = jax.vjp(build_spatial, table_sp)
    bias_st, pull_st = jax.vjp(build_cube, table_st)

    def spatial_keys(key_local, value_local):
        return (spatial_windows(key_local), spatial_windows(value_local))

    def cube_keys(key_local, value_local):
        key_all, value_all = (
            lax.all_gather(key_local, "frame", axis=1, tiled=True),
            lax.all_gather(value_local, "frame", axis=1, tiled=True),
        )
        return (cube_windows(key_all), cube_windows(value_all))

    def spatial_return(grad_key, grad_value):
        return (spatial_unwindow(grad_key, local_shape), spatial_unwindow(grad_value, local_shape))

    def cube_return(grad_key, grad_value):
        key_whole = cube_unwindow(grad_key, whole_shape)
        value_whole = cube_unwindow(grad_value, whole_shape)
        return (
            lax.psum_scatter(
                key_whole.astype(jnp.bfloat16), "frame", scatter_dimension=1, tiled=True
            ).astype(jnp.float32),
            lax.psum_scatter(
                value_whole.astype(jnp.bfloat16), "frame", scatter_dimension=1, tiled=True
            ).astype(jnp.float32),
        )

    weights_sp = (gathered[0][:, 0], gathered[1][:, 0], gathered[2][:, 0], gathered[3][:, 0])
    weights_st = (gathered[0][:, 1], gathered[1][:, 1], gathered[2][:, 1], gathered[3][:, 1])
    stream_mid, saved_sp = block_forward(
        frames_in.astype(jnp.float32),
        modulation[:, 0:6],
        weights_sp,
        n_heads,
        bias_sp,
        spatial_ok,
        spatial_windows,
        spatial_unwindow,
        spatial_keys,
        score_scale,
    )
    stream_end, saved_st = block_forward(
        stream_mid,
        modulation[:, 6:12],
        weights_st,
        n_heads,
        bias_st,
        cube_ok,
        cube_windows,
        cube_unwindow,
        cube_keys,
        score_scale,
    )
    mixed = stream_end.astype(jnp.bfloat16)
    again = (
        lax.all_gather(w_qkv, "clip", axis=0, tiled=True),
        lax.all_gather(w_proj, "clip", axis=0, tiled=True),
        lax.all_gather(w_up, "clip", axis=0, tiled=True),
        lax.all_gather(w_down, "clip", axis=0, tiled=True),
    )
    back_sp = (again[0][:, 0], again[1][:, 0], again[2][:, 0], again[3][:, 0])
    back_st = (again[0][:, 1], again[1][:, 1], again[2][:, 1], again[3][:, 1])
    key_again, value_again = (
        lax.all_gather(saved_st[5], "frame", axis=1, tiled=True),
        lax.all_gather(saved_st[6], "frame", axis=1, tiled=True),
    )
    key_win_st = split_heads(cube_windows(key_again), n_heads)
    value_win_st = split_heads(cube_windows(value_again), n_heads)
    grad_stream, mod_grad_st, grads_st, bias_grad_st = block_backward(
        cotangent.astype(jnp.float32),
        saved_st,
        modulation[:, 6:12],
        back_st,
        n_heads,
        bias_st,
        cube_ok,
        cube_windows,
        cube_unwindow,
        cube_return,
        key_win_st,
        value_win_st,
        score_scale,
    )
    grad_stream, mod_grad_sp, grads_sp, bias_grad_sp = block_backward(
        grad_stream,
        saved_sp,
        modulation[:, 0:6],
        back_sp,
        n_heads,
        bias_sp,
        spatial_ok,
        spatial_windows,
        spatial_unwindow,
        spatial_return,
        saved_sp[3],
        saved_sp[4],
        score_scale,
    )
    table_sp_grad = pull_sp(bias_grad_sp)[0]
    table_st_grad = pull_st(bias_grad_st)[0]
    full_qkv = jnp.stack([grads_sp[0], grads_st[0]], axis=1)
    full_proj = jnp.stack([grads_sp[1], grads_st[1]], axis=1)
    full_up = jnp.stack([grads_sp[2], grads_st[2]], axis=1)
    full_down = jnp.stack([grads_sp[3], grads_st[3]], axis=1)
    shares = (
        lax.psum_scatter(
            full_qkv.astype(jnp.bfloat16), "clip", scatter_dimension=0, tiled=True
        ).astype(jnp.float32),
        lax.psum_scatter(
            full_proj.astype(jnp.bfloat16), "clip", scatter_dimension=0, tiled=True
        ).astype(jnp.float32),
        lax.psum_scatter(
            full_up.astype(jnp.bfloat16), "clip", scatter_dimension=0, tiled=True
        ).astype(jnp.float32),
        lax.psum_scatter(
            full_down.astype(jnp.bfloat16), "clip", scatter_dimension=0, tiled=True
        ).astype(jnp.float32),
    )
    mod_grad = jnp.concatenate([mod_grad_sp, mod_grad_st], axis=1)
    summed = (
        lax.psum(shares[0].astype(jnp.bfloat16), "frame").astype(jnp.float32),
        lax.psum(shares[1].astype(jnp.bfloat16), "frame").astype(jnp.float32),
        lax.psum(shares[2].astype(jnp.bfloat16), "frame").astype(jnp.float32),
        lax.psum(shares[3].astype(jnp.bfloat16), "frame").astype(jnp.float32),
        lax.psum(mod_grad.astype(jnp.bfloat16), "frame").astype(jnp.float32),
        lax.psum(table_sp_grad.astype(jnp.bfloat16), "frame").astype(jnp.float32),
        lax.psum(table_st_grad.astype(jnp.bfloat16), "frame").astype(jnp.float32),
    )
    tables = (
        lax.psum(summed[5].astype(jnp.bfloat16), "clip").astype(jnp.float32),
        lax.psum(summed[6].astype(jnp.bfloat16), "clip").astype(jnp.float32),
    )
    return (
        mixed,
        grad_stream.astype(jnp.bfloat16),
        summed[4],
        summed[0],
        summed[1],
        summed[2],
        summed[3],
        tables[0],
        tables[1],
    )


def solution(mesh):
    placed = (
        P("clip", "frame", None, None, None),
        P("clip"),
        P("clip", None, None),
        P("clip", None, None),
        P("clip", None, None),
        P("clip", None, None),
        P("clip", None, None),
        P(),
        P(),
        P("clip", "frame", None, None, None),
    )
    return jax.shard_map(
        on_device,
        mesh=mesh,
        in_specs=placed,
        out_specs=(
            P("clip", "frame", None, None, None),
            P("clip", "frame", None, None, None),
            P("clip", None, None),
            P("clip", None, None),
            P("clip", None, None),
            P("clip", None, None),
            P("clip", None, None),
            P(),
            P(),
        ),
        check_vma=False,
    )
```

profile of v0, /device:TPU:0, one launch (start us, length us, event | category | flops | bytes accessed | tf_op | source)
XLA Modules:
  0.0 2054.6 jit_solution(8931594977724697460)
XLA Ops:
  16.9 17.4 convolution_bitcast_fusion
  34.3 41.7 %copy.250 = f32[16,16,16,16,16]{2,1,4,3,0:T(8,128)} copy(f32[16,16,16,16,16]{3,4,1,0,2:T(8,128)} %convolution_bitcast_fusion) | data formatting | bytes 8388608 | tf_op jit(solution)/shard_map/add | solution.py:122
  76.0 24.0 %reshape.1284 = f32[16,256,256]{1,2,0:T(8,128)} reshape(f32[16,16,16,16,16]{2,1,4,3,0:T(8,128)} %copy.250) | data formatting | bytes 8388608 | tf_op jit(solution)/shard_map/add | solution.py:122
  164.5 12.9 fusion.232
  198.5 95.7 %all-gather.11.cloned.1.call-done = bf16[1024,2,4096]{2,0,1:T(8,128)(2,1)} async-done(((bf16[64,2,4096]{2,0,1:T(8,128)(2,1)}), bf16[1024,2,4096]{2,0,1:T(8,128)(2,1)}) %all-gather.11.cloned.1.call-update) | async-done | bytes 16777232 | tf_op jit(solution)/shard_map/all_gather | solution.py:298
  294.2 18.2 multiply_convert_fusion.3
  312.4 109.4 %all-gather.13.cloned.1.call-done = bf16[4096,2,1024]{2,0,1:T(8,128)(2,1)} async-done(((bf16[256,2,1024]{2,0,1:T(8,128)(2,1)}), bf16[4096,2,1024]{2,0,1:T(8,128)(2,1)}) %all-gather.13.cloned.1.call-update) | async-done | bytes 16777232 | tf_op jit(solution)/shard_map/all_gather | solution.py:299
  470.1 162.0 %reshape.1236 = f32[16,4,8,64,64]{2,1,0,4,3:T(4,128)} reshape(f32[512,8,8,8,8]{0,4,3,2,1:T(8,128)} %copy.182) | data formatting | bytes 16777216 | tf_op jit(solution)/shard_map/jvp()/reshape;jvp()/reshape | solution.py:88
  632.1 93.6 %copy.183 = f32[16,4,64,8,64]{4,3,2,1,0:T(8,128)} copy(f32[16,4,64,8,64]{3,1,0,4,2:T(4,128)} %bitcast.54) | data formatting | bytes 16777216 | tf_op jit(solution)/shard_map/jvp()/transpose | solution.py:89
  725.6 14.3 add.352
  805.0 20.1 fusion.233
  825.0 14.0 convert_bitcast_fusion.6
  858.8 19.0 multiply_convert_fusion.2
  877.8 24.3 %fusion.18 = bf16[1024,4096]{1,0:T(8,128)(2,1)} fusion(f32[1024,4096]{1,0:T(8,128)} %get-tuple-element.105, bf16[1024,1024]{1,0:T(8,128)(2,1)S(1)} %bitcast.513, bf16[4096,2,1024]{2,0,1:T(8,128)(2,1)} %all-gather.13.cloned.1.call-done), kind=kOutput, calls=%fused_computation.27 | convolution fusion | flops 8673820672 | bytes 35651584 | tf_op jit(solution)/shard_map/nb,ab->na/dot_general | solution.py:47
  902.1 13.6 fusion.237
  951.9 23.6 %multiply_reduce_fusion = (f32[4,16,256]{2,1,0:T(8,128)S(1)}, f32[4,16,256,512]{3,2,1,0:T(8,128)}) fusion(f32[4,16,256,512]{3,2,1,0:T(8,128)} %get-tuple-element.103, f32[4,16,256]{2,1,0:T(8,128)S(1)} %get-tuple-element.102, bf16[4,256,16,64]{1,3,2,0:T(8,128)(2,1)S(1)} %copy.188, bf16[4,512,16,64]{1,3,2,0:T(8,128)(2,1)} %copy.184), kind=kOutput, calls=%fused_computation.6 | convolution fusion | flops 1098891264 | bytes 73531392 | tf_op jit(solution)/shard_map/nqhd,nkhd->nhqk/dot_general | solution.py:238
  975.5 31.8 %convert_reduce_fusion = (f32[16,256,512]{2,1,0:T(8,128)}, bf16[4,16,256,512]{3,2,1,0:T(8,128)(2,1)}) fusion(f32[4,16,256,512]{3,2,1,0:T(8,128)} %get-tuple-element.107, f32[4,16,256]{2,1,0:T(8,128)S(1)} %get-tuple-element.106, f32[4,16,256,512]{3,2,1,0:T(8,128)} %get-tuple-element.103, f32[4,16,256]{2,1,0:T(8,128)S(1)} %get-tuple-element.102), kind=kLoop, calls=%fused_computation.4 | loop fusion | flops 48234496 | bytes 92405760 | tf_op jit(solution)/shard_map/reduce_sum | solution.py:243
  1045.9 14.9 convert_bitcast_fusion.2
  1115.9 39.4 %reduce-scatter.9.cloned.1.call-done = bf16[1,4,16,16,1024]{4,3,2,1,0:T(8,128)(2,1)} async-done(((bf16[1,8,16,16,1024]{4,3,2,1,0:T(8,128)(2,1)}), bf16[1,4,16,16,1024]{4,3,2,1,0:T(8,128)(2,1)}) %reduce-scatter.9.cloned.1.call-update) | async-done | bytes 2097168 | tf_op jit(solution)/shard_map/reduce_scatter | solution.py:341
  1180.1 24.8 %fusion.11 = bf16[1024,4096]{1,0:T(8,128)(2,1)} fusion(f32[1024,4096]{1,0:T(8,128)} %get-tuple-element.101, bf16[1024,1024]{1,0:T(8,128)(2,1)S(1)} %bitcast.526, bf16[4096,2,1024]{2,0,1:T(8,128)(2,1)} %all-gather.13.cloned.1.call-done), kind=kOutput, calls=%fused_computation.20 | convolution fusion | flops 8673820672 | bytes 35651584 | tf_op jit(solution)/shard_map/nb,ab->na/dot_general | solution.py:47
  1204.9 13.8 fusion.235
  1261.3 15.3 convert_reduce_fusion.1
  1367.7 14.9 fusion.45
  1434.5 13.1 reshape.1254
  1447.6 90.6 %copy.216 = f32[16,4,8,64,64]{2,1,0,4,3:T(4,128)} copy(f32[16,4,8,64,64]{4,2,3,1,0:T(8,128)} %bitcast.484) | data formatting | bytes 16777216 | tf_op jit(solution)/shard_map/transpose(jvp())/transpose | solution.py:89
  1538.2 161.2 %reshape.1255 = f32[512,8,8,8,8]{0,4,3,2,1:T(8,128)} reshape(f32[16,4,8,64,64]{2,1,0,4,3:T(4,128)} %copy.216) | data formatting | bytes 16777216 | tf_op jit(solution)/shard_map/transpose(jvp())/reshape;transpose(jvp())/reshape | solution.py:72
  1728.1 19.4 reshape.1253
  1747.5 36.5 %copy.214 = f32[16,16,16,16,16]{4,3,2,1,0:T(8,128)} copy(f32[16,16,16,16,16]{2,1,4,3,0:T(8,128)} %reshape.1253) | data formatting | bytes 8388608 | tf_op jit(solution)/shard_map/transpose(jvp())/reshape | solution.py:72
  1800.1 65.9 %reduce-scatter.15.cloned.1.call-done = bf16[64,2,4096]{2,0,1:T(8,128)(2,1)} async-done(((bf16[1024,2,4096]{2,0,1:T(8,128)(2,1)}), bf16[64,2,4096]{2,0,1:T(8,128)(2,1)}) %reduce-scatter.15.cloned.1.call-update) | async-done | bytes 1048592 | tf_op jit(solution)/shard_map/reduce_scatter | solution.py:430
  1866.3 21.3 %fusion.2 = f32[16,16,16,31,1]{3,2,4,1,0:T(8,128)} fusion(f32[16,16,16,16,16]{4,3,2,1,0:T(8,128)} %copy.214, s32[16,16]{1,0:T(8,128)S(1)} %copy-done.69), kind=kOutput, calls=%fused_computation.2 | convolution fusion | flops 390078208 | bytes 4703232 | tf_op jit(solution)/shard_map/transpose(jvp(hxyb,uvb->hxuyv))/dot_general | solution.py:71
  1896.2 61.1 %all-reduce.7.cloned.1.call-done = (bf16[64,2,3072]{2,0,1:T(8,128)(2,1)}, bf16[64,2,1024]{2,0,1:T(8,128)(2,1)}, bf16[64,2,4096]{2,0,1:T(8,128)(2,1)}, bf16[256,2,1024]{2,0,1:T(8,128)(2,1)}, bf16[16,3375]{1,0:T(8,128)(2,1)}) async-done(((bf16[64,2,3072]{2,0,1:T(8,128)(2,1)}, bf16[64,2,1024]{2,0,1:T(8,128)(2,1)}, bf16[64,2,4096]{2,0,1:T(8,128)(2,1)}, bf16[256,2,1024]{2,0,1:T(8,128)(2,1)}, ...) | async-done | bytes 3253744 | tf_op jit(solution)/shard_map/psum | solution.py:439
  1965.9 59.7 %psum.69 = bf16[16,961]{1,0:T(8,128)(2,1)S(1)} all-reduce(bf16[16,961]{1,0:T(8,128)(2,1)S(1)} %get-tuple-element.56), channel_id=1, replica_groups=mesh['clip'=16,'frame'=2] {'clip'}, use_global_device_ids=true, to_apply=%region_47.48 | all-reduce | flops 15376 | bytes 61504 | tf_op jit(solution)/shard_map/psum | solution.py:448
  (469 shorter events, 650.7 us)
Async XLA Ops:
  7.2 107.2 %all-gather.7.cloned.1.call-start = ((), (), s32[]{:S(2)}) async-start(), calls=%async_computation.6 | async-start | bytes 13369344 | tf_op jit(solution)/shard_map/all_gather | solution.py:296
  9.5 179.6 %all-gather.9.cloned.1.call-start = ((), (), s32[]{:S(2)}) async-start(), calls=%async_computation.7 | async-start | bytes 4456448 | tf_op jit(solution)/shard_map/all_gather | solution.py:297
  11.3 282.9 %all-gather.11.cloned.1.call-start = ((), (), s32[]{:S(2)}) async-start(), calls=%async_computation.8 | async-start | bytes 17825792 | tf_op jit(solution)/shard_map/all_gather | solution.py:298
  14.1 407.7 %all-gather.13.cloned.1.call-start = ((), (), s32[]{:S(2)}) async-start(), calls=%async_computation.9 | async-start | bytes 17825792 | tf_op jit(solution)/shard_map/all_gather | solution.py:299
  15.5 736.1 %all-gather.17.cloned.1.call-start = ((), (), s32[]{:S(2)}) async-start(), calls=%async_computation.11 | async-start | bytes 6291456 | tf_op jit(solution)/shard_map/all_gather | solution.py:326
  101.7 92.1 %copy-start.104 = (f32[1,1,1024]{2,0,1:T(1,128)}, f32[1,1,1024]{2,0,1:T(1,128)S(1)}, u32[]{:S(2)}) copy-start(f32[1,1,1024]{2,0,1:T(1,128)S(1)} %get-tuple-element.95) | copy-start | bytes 12292
  101.7 95.6 %copy-start.86 = (f32[1,1,1024]{2,0,1:T(1,128)}, f32[1,1,1024]{2,0,1:T(1,128)S(1)}, u32[]{:S(2)}) copy-start(f32[1,1,1024]{2,0,1:T(1,128)S(1)} %get-tuple-element.91) | copy-start | bytes 12292
  101.7 332.9 %copy-start.106 = (f32[1,1,1024]{2,0,1:T(1,128)}, f32[1,1,1024]{2,0,1:T(1,128)S(1)}, u32[]{:S(2)}) copy-start(f32[1,1,1024]{2,0,1:T(1,128)S(1)} %get-tuple-element.92) | copy-start | bytes 12292
  101.7 335.5 %copy-start.97 = (f32[1,1,1024]{2,0,1:T(1,128)}, f32[1,1,1024]{2,0,1:T(1,128)S(1)}, u32[]{:S(2)}) copy-start(f32[1,1,1024]{2,0,1:T(1,128)S(1)} %get-tuple-element.88) | copy-start | bytes 12292
  101.7 335.5 %copy-start.120 = (f32[1,1,1024]{2,0,1:T(1,128)}, f32[1,1,1024]{2,0,1:T(1,128)S(1)}, u32[]{:S(2)}) copy-start(f32[1,1,1024]{2,0,1:T(1,128)S(1)} %get-tuple-element.87) | copy-start | bytes 12292
  198.4 113.9 %copy-start.41 = (bf16[1,4,16,16,1024]{4,3,2,1,0:T(8,128)(2,1)}, bf16[1,4,16,16,1024]{4,3,2,1,0:T(8,128)(2,1)S(1)}, u32[]{:S(2)}) copy-start(bf16[1,4,16,16,1024]{4,3,2,1,0:T(8,128)(2,1)S(1)} %add_convert_fusion.4) | copy-start | bytes 6291460
  451.1 327.5 %all-gather.15.cloned.1.call-start = ((), (), s32[]{:S(2)}) async-start(), calls=%async_computation.10 | async-start | bytes 6291456 | tf_op jit(solution)/shard_map/all_gather | solution.py:327
  451.7 664.2 %reduce-scatter.7.cloned.1.call-start = ((), (), s32[]{:S(2)}) async-start(), calls=%async_computation.12 | async-start | bytes 6291456 | tf_op jit(solution)/shard_map/reduce_scatter | solution.py:338
  1045.9 109.5 %reduce-scatter.9.cloned.1.call-start = ((), (), s32[]{:S(2)}) async-start(), calls=%async_computation.13 | async-start | bytes 6291456 | tf_op jit(solution)/shard_map/reduce_scatter | solution.py:341
  1088.6 711.5 %reduce-scatter.13.cloned.1.call-start = ((), (), s32[]{:S(2)}) async-start(), calls=%async_computation.15 | async-start | bytes 4456448 | tf_op jit(solution)/shard_map/reduce_scatter | solution.py:427
  1234.0 566.1 %reduce-scatter.11.cloned.1.call-start = ((), (), s32[]{:S(2)}) async-start(), calls=%async_computation.14 | async-start | bytes 13369344 | tf_op jit(solution)/shard_map/reduce_scatter | solution.py:424
  1366.1 434.0 %reduce-scatter.17.cloned.1.call-start = ((), (), s32[]{:S(2)}) async-start(), calls=%async_computation.17 | async-start | bytes 17825792 | tf_op jit(solution)/shard_map/reduce_scatter | solution.py:433
  1402.7 463.3 %reduce-scatter.15.cloned.1.call-start = ((), (), s32[]{:S(2)}) async-start(), calls=%async_computation.16 | async-start | bytes 17825792 | tf_op jit(solution)/shard_map/reduce_scatter | solution.py:430
  1434.4 522.9 %all-reduce.7.cloned.1.call-start = ((), (), s32[]{:S(2)}) async-start(), calls=%async_computation.19 | async-start | bytes 6512640 | tf_op jit(solution)/shard_map/psum | solution.py:439
  1538.2 161.2 %copy-start.89 = (s32[8,8]{1,0:T(8,128)S(1)}, s32[8,8]{1,0:T(8,128)}, u32[]{:S(2)}) copy-start(s32[8,8]{1,0:T(8,128)} %copy-done.88) | copy-start | bytes 772
  1797.8 68.3 %copy-start.113 = (bf16[1024]{0:T(1024)(128)(2,1)S(1)}, bf16[1024]{0:T(1024)(128)(2,1)}, u32[]{:S(2)}) copy-start(bf16[1024]{0:T(1024)(128)(2,1)} %get-tuple-element.47) | copy-start | bytes 6148
  1797.8 68.3 %copy-start.117 = (bf16[1024]{0:T(1024)(128)(2,1)S(1)}, bf16[1024]{0:T(1024)(128)(2,1)}, u32[]{:S(2)}) copy-start(bf16[1024]{0:T(1024)(128)(2,1)} %get-tuple-element.76) | copy-start | bytes 6148
  1797.8 68.3 %copy-start.123 = (bf16[1024]{0:T(1024)(128)(2,1)S(1)}, bf16[1024]{0:T(1024)(128)(2,1)}, u32[]{:S(2)}) copy-start(bf16[1024]{0:T(1024)(128)(2,1)} %get-tuple-element.114) | copy-start | bytes 6148
  1797.8 68.4 %copy-start.112 = (bf16[1024]{0:T(1024)(128)(2,1)S(1)}, bf16[1024]{0:T(1024)(128)(2,1)}, u32[]{:S(2)}) copy-start(bf16[1024]{0:T(1024)(128)(2,1)} %get-tuple-element.45) | copy-start | bytes 6148
  1797.8 68.4 %copy-start.116 = (bf16[1024]{0:T(1024)(128)(2,1)S(1)}, bf16[1024]{0:T(1024)(128)(2,1)}, u32[]{:S(2)}) copy-start(bf16[1024]{0:T(1024)(128)(2,1)} %get-tuple-element.54) | copy-start | bytes 6148
  1797.8 68.4 %copy-start.122 = (bf16[1024]{0:T(1024)(128)(2,1)S(1)}, bf16[1024]{0:T(1024)(128)(2,1)}, u32[]{:S(2)}) copy-start(bf16[1024]{0:T(1024)(128)(2,1)} %get-tuple-element.116) | copy-start | bytes 6148
  1797.8 68.4 %copy-start.111 = (bf16[1024]{0:T(1024)(128)(2,1)S(1)}, bf16[1024]{0:T(1024)(128)(2,1)}, u32[]{:S(2)}) copy-start(bf16[1024]{0:T(1024)(128)(2,1)} %get-tuple-element.49) | copy-start | bytes 6148
  1797.9 68.4 %copy-start.69 = (s32[16,16]{1,0:T(8,128)S(1)}, s32[16,16]{1,0:T(8,128)}, u32[]{:S(2)}) copy-start(s32[16,16]{1,0:T(8,128)} %copy-done.68) | copy-start | bytes 3076
  1866.0 180.2 %all-reduce.5.cloned.1.call-start = ((), (), s32[]{:S(2)}) async-start(), calls=%async_computation.18 | async-start | bytes 221184 | tf_op jit(solution)/shard_map/psum | solution.py:449
  1891.0 66.4 %copy-start.115 = (bf16[1024]{0:T(1024)(128)(2,1)S(1)}, bf16[1024]{0:T(1024)(128)(2,1)}, u32[]{:S(2)}) copy-start(bf16[1024]{0:T(1024)(128)(2,1)} %get-tuple-element.53) | copy-start | bytes 6148
  1957.3 73.3 %copy-start.57 = (bf16[256,2,1024]{2,0,1:T(8,128)(2,1)S(1)}, bf16[256,2,1024]{2,0,1:T(8,128)(2,1)}, u32[]{:S(2)}) copy-start(bf16[256,2,1024]{2,0,1:T(8,128)(2,1)} %get-tuple-element.60) | copy-start | bytes 3145732
  1957.3 75.7 %copy-start.65 = (bf16[64,2,3072]{2,0,1:T(8,128)(2,1)S(1)}, bf16[64,2,3072]{2,0,1:T(8,128)(2,1)}, u32[]{:S(2)}) copy-start(bf16[64,2,3072]{2,0,1:T(8,128)(2,1)} %get-tuple-element.57) | copy-start | bytes 2359300
  (111 other events, 952.0 us)
Sparse Core Ops, SparseCore 0:
  10.9 103.4 all-gather.6
  117.2 48.7 all-gather.8
  168.7 125.3 all-gather.10
  296.8 125.0 all-gather.12
  451.2 54.8 all-gather.16
  507.6 56.7 all-gather.14
  1046.0 52.5 reduce-scatter.6
  1101.0 54.3 reduce-scatter.8
  1234.2 72.3 reduce-scatter.12
  1366.2 135.2 reduce-scatter.10
  1506.2 177.6 reduce-scatter.16
  1688.4 177.5 reduce-scatter.14
  1869.4 87.8 all-reduce.6
  1961.0 85.1 all-reduce.4
where the time goes:
time: 2070 us; the launch traced here: 2050 us
  local copies, waits for them, and re-layouts  980 us (47%)
  matrix products  473 us (23%)
  waiting for transfers between devices  394 us (19%)
  other arithmetic  123 us (6%)
  blocking collectives  67.8 us (3%)
    reshape x3, local copies, waits for them, and re-layouts, expand_bias(): full_bias.reshape(table.shape[0], side_len * side_len, side_len * side_len)  217 us
    transpose x2, local copies, waits for them, and re-layouts, cube_bias(): squares = squares.transpose(0, 1, 3, 2, 4)  184 us
    reshape x1, local copies, waits for them, and re-layouts, cube_bias(): squares.reshape(n_heads, local_frames, FRAMES, TWIN * TWIN, TWIN * TWIN)  162 us
    all_gather x1, waiting for transfers between devices, on_device(): lax.all_gather(w_down, 'clip', axis=0, tiled=True)  109 us
    another operation x16, local copies, waits for them, and re-layouts, split_heads(): return values.reshape(values.shape[0], values.shape[1], n_heads, -1)  108 us
    dot_general x8, matrix products, back_dot(): jnp.einsum('nb,ab->na', flat_in, weight, preferred_element_type=jnp.float32)  104 us
    all_gather x1, waiting for transfers between devices, on_device(): lax.all_gather(w_up, 'clip', axis=0, tiled=True)  95.7 us
    dot_general x8, matrix products, flat_dot(): flat_out = jnp.dot(flat_in, weight, preferred_element_type=jnp.float32)  88.9 us
  transfers between devices with their start and end apart: 14, of which 7 were waited for; matrix products, arithmetic and copies ran while one was open for 58% of the time, Pallas kernels for 0%

commit v1 on v0

--- a/solution.py
+++ b/solution.py
@@ -1,16 +1,1307 @@
+import functools
+
 import jax
 import jax.numpy as jnp
 from jax import lax
+from jax.experimental import pallas as pl
+from jax.experimental.pallas import tpu as pltpu
 from jax.sharding import PartitionSpec as P
 
 SWIN = 16
 TWIN = 8
 FRAMES = 8
 FILLED = 5
-
-
+KEYF = 6
 NEG_FILL = -1000000000.0
 NORM_EPS = 1e-06
+F32 = jnp.float32
+BF16 = jnp.bfloat16
+NT = (((1,), (1,)), ((), ()))
+TN = (((0,), (0,)), ((), ()))
+
+
+def dot_nn(a, b):
+    return jnp.dot(a, b, preferred_element_type=F32)
+
+
+def dot_nt(a, b):
+    return lax.dot_general(a, b, NT, preferred_element_type=F32)
+
+
+def dot_tn(a, b):
+    return lax.dot_general(a, b, TN, preferred_element_type=F32)
+
+
+def norm_stats(values):
+    mean = jnp.mean(values, axis=-1, keepdims=True)
+    centered = values - mean
+    spread = jnp.mean(centered * centered, axis=-1, keepdims=True)
+    inv = lax.rsqrt(spread + NORM_EPS)
+    return centered * inv, inv
+
+
+def pick_sp():
+    span = 2 * SWIN - 1
+    shape = (8 * span, SWIN, 128)
+    source = lax.broadcasted_iota(jnp.int32, shape, 0)
+    ci = lax.broadcasted_iota(jnp.int32, shape, 1)
+    lane = lax.broadcasted_iota(jnp.int32, shape, 2)
+    hit = (source // span == 7 - lane // SWIN) & (source % span == SWIN - 1 + ci - lane % SWIN)
+    return hit.astype(F32).reshape(8 * span, SWIN * 128)
+
+
+def pick_st():
+    span = 2 * TWIN - 1
+    shape = (span * span, TWIN, 128)
+    source = lax.broadcasted_iota(jnp.int32, shape, 0)
+    ci = lax.broadcasted_iota(jnp.int32, shape, 1)
+    lane = lax.broadcasted_iota(jnp.int32, shape, 2)
+    row = span - 1 - lane // TWIN
+    hit = (source // span == row) & (source % span == TWIN - 1 + ci - lane % TWIN)
+    return hit.astype(F32).reshape(span * span, TWIN * 128)
+
+
+def spread_sp(table):
+    n_heads = table.shape[0]
+    span = 2 * SWIN - 1
+    padded = jnp.pad(table, ((0, 0), (span, 0))).reshape(n_heads * 4, 8 * span)
+    out = jnp.dot(padded, pick_sp(), precision=lax.Precision.HIGHEST)
+    return out.reshape(n_heads, 4, SWIN, 128)
+
+
+def spread_st(table):
+    n_heads = table.shape[0]
+    span = 2 * TWIN - 1
+    fspan = 2 * FRAMES - 1
+    flat = table.reshape(n_heads * fspan, span * span)
+    out = jnp.dot(flat, pick_st(), precision=lax.Precision.HIGHEST)
+    return out.reshape(n_heads, fspan, TWIN, 128)
+
+
+def gather_sp(spread):
+    n_heads = spread.shape[0]
+    span = 2 * SWIN - 1
+    flat = spread.reshape(n_heads * 4, SWIN * 128)
+    out = lax.dot_general(flat, pick_sp(), NT, precision=lax.Precision.HIGHEST)
+    return out.reshape(n_heads, 32 * span)[:, span:]
+
+
+def gather_st(spread):
+    n_heads = spread.shape[0]
+    span = 2 * TWIN - 1
+    fspan = 2 * FRAMES - 1
+    flat = spread.reshape(n_heads * fspan, TWIN * 128)
+    out = lax.dot_general(flat, pick_st(), NT, precision=lax.Precision.HIGHEST)
+    return out.reshape(n_heads, fspan * span * span)
+
+
+def fill_bias_sp(spread_ref, hh, bias_ref):
+    spread = jnp.concatenate([spread_ref[hh, g] for g in (3, 2, 1, 0)], axis=1)
+    width = spread.shape[1]
+    win = SWIN * SWIN
+    for ri in range(SWIN):
+        shift = (width - (SWIN - 1 - ri) * SWIN) % width
+        rolled = pltpu.roll(spread, shift, 1) if shift else spread
+        bias_ref[ri * SWIN : (ri + 1) * SWIN, :] = rolled[:, :win]
+
+
+def fold_bias_sp(grad_ref, out_ref, hh):
+    win = SWIN * SWIN
+    width = 2 * win
+    total = None
+    for ri in range(SWIN):
+        rows = grad_ref[ri * SWIN : (ri + 1) * SWIN, :]
+        rows = jnp.concatenate([rows, jnp.zeros((SWIN, width - win), F32)], axis=1)
+        shift = (SWIN - 1 - ri) * SWIN
+        rows = pltpu.roll(rows, shift, 1) if shift else rows
+        total = rows if total is None else total + rows
+    for g in range(4):
+        out_ref[hh, g] = total[:, (3 - g) * 128 : (4 - g) * 128]
+
+
+def fill_bias_st(spread_ref, hh, bias_ref):
+    lanes = lax.broadcasted_iota(jnp.int32, (TWIN, 128), 1)
+    half = TWIN * TWIN
+    n_pairs = KEYF // 2
+    for ri in range(TWIN):
+        shift = (128 - (TWIN - 1 - ri) * TWIN) % 128
+        cache = {}
+
+        def low_of(f):
+            if f not in cache:
+                rows = spread_ref[hh, 2 * FRAMES - 2 - f]
+                cache[f] = pltpu.roll(rows, shift, 1) if shift else rows
+            return cache[f]
+
+        pairs = {}
+        for fi in range(FRAMES):
+            for pair in range(n_pairs):
+                f = FRAMES - 1 - fi + 2 * pair
+                if f not in pairs:
+                    pairs[f] = jnp.where(
+                        lanes < half, low_of(f), pltpu.roll(low_of(f + 1), half, 1)
+                    )
+                row = fi * half + ri * TWIN
+                bias_ref[row : row + TWIN, pair * 128 : (pair + 1) * 128] = pairs[f]
+
+
+def fold_bias_st(grad_ref, out_ref, hh):
+    lanes = lax.broadcasted_iota(jnp.int32, (TWIN, 128), 1)
+    half = TWIN * TWIN
+    n_pairs = KEYF // 2
+    fspan = 2 * FRAMES - 1
+    totals = [None] * fspan
+    for ri in range(TWIN):
+        sums = {}
+        for fi in range(FRAMES):
+            for pair in range(n_pairs):
+                f = FRAMES - 1 - fi + 2 * pair
+                row = fi * half + ri * TWIN
+                part = grad_ref[row : row + TWIN, pair * 128 : (pair + 1) * 128]
+                sums[f] = part if f not in sums else sums[f] + part
+        for f in range(fspan):
+            piece = None
+            if f in sums:
+                piece = jnp.where(lanes < half, sums[f], 0.0)
+            if f - 1 in sums:
+                upper = pltpu.roll(jnp.where(lanes >= half, sums[f - 1], 0.0), half, 1)
+                piece = upper if piece is None else piece + upper
+            if piece is None:
+                continue
+            shift = (TWIN - 1 - ri) * TWIN
+            piece = pltpu.roll(piece, shift, 1) if shift else piece
+            totals[f] = piece if totals[f] is None else totals[f] + piece
+    for f in range(fspan):
+        out_ref[hh, 2 * FRAMES - 2 - f] = jnp.zeros((TWIN, 128), F32) if totals[f] is None else totals[f]
+
+
+def lane_mask(rows, hh):
+    lanes = lax.broadcasted_iota(jnp.int32, (rows, 128), 1)
+    return (lanes < 64) if hh == 0 else (lanes >= 64)
+
+
+def attend_forward(spatial, n_win, n_query, n_key, chunk, q_ref, k_ref, v_ref, m_ref, ok_ref, att_ref, p_ref, bias_ref):
+    for hh in range(2):
+        if spatial:
+            fill_bias_sp(m_ref, hh, bias_ref.at[hh])
+        else:
+            fill_bias_st(m_ref, hh, bias_ref.at[hh])
+    own = lane_mask(chunk, 0)
+    for n in range(n_win):
+        key = k_ref[n * n_query : n * n_query + n_key, :]
+        val = v_ref[n * n_query : n * n_query + n_key, :]
+        ok = ok_ref[n] > 0.0
+        for c in range(n_query // chunk):
+            rows = slice(n * n_query + c * chunk, n * n_query + (c + 1) * chunk)
+            query = q_ref[rows, :]
+            query = query * jnp.asarray(0.125, BF16)
+            outs = []
+            for hh in range(2):
+                mine = own if hh == 0 else jnp.logical_not(own)
+                picked = jnp.where(mine, query, jnp.zeros_like(query))
+                scores = dot_nt(picked, key) + bias_ref[hh, c * chunk : (c + 1) * chunk, :]
+                scores = jnp.where(ok, scores, NEG_FILL)
+                top = jnp.max(scores, axis=-1, keepdims=True)
+                expo = jnp.exp(scores - top)
+                probs = (expo * (1.0 / jnp.sum(expo, axis=-1, keepdims=True))).astype(BF16)
+                p_ref[hh, n, c * chunk : (c + 1) * chunk, :] = probs
+                outs.append(dot_nn(probs, val))
+            att_ref[rows, :] = jnp.where(own, outs[0], outs[1]).astype(BF16)
+
+
+def attend_backward(
+    spatial, n_win, n_query, n_key, chunk, head, q_ref, k_ref, v_ref, do_ref, p_ref, g_ref, dm_ref, db_ref
+):
+    width = g_ref.shape[1] // 3
+    own = lane_mask(chunk, 0)
+    own_k = lane_mask(n_key, 0)
+
+    def store(rows, which, values):
+        g_ref[rows, pl.ds(pl.multiple_of(which * width + head * 128, 128), 128)] = values
+
+    db_ref[...] = jnp.zeros_like(db_ref)
+    for n in range(n_win):
+        keys = slice(n * n_query, n * n_query + n_key)
+        key = k_ref[keys, :]
+        val = v_ref[keys, :]
+        gk = [None, None]
+        gv = [None, None]
+        for c in range(n_query // chunk):
+            rows = slice(n * n_query + c * chunk, n * n_query + (c + 1) * chunk)
+            part = slice(c * chunk, (c + 1) * chunk)
+            query = q_ref[rows, :]
+            gout = do_ref[rows, :]
+            gq = []
+            for hh in range(2):
+                mine = own if hh == 0 else jnp.logical_not(own)
+                probs = p_ref[hh, n, part, :]
+                gsel = jnp.where(mine, gout, jnp.zeros_like(gout))
+                dprob = dot_nt(gsel, val)
+                soft = probs.astype(F32)
+                delta = jnp.sum(soft * dprob, axis=-1, keepdims=True)
+                dscore = (soft * (dprob - delta)).astype(BF16)
+                db_ref[hh, part, :] += dscore.astype(F32)
+                gq.append(dot_nn(dscore, key))
+                dk = dot_tn(dscore, query)
+                dv = dot_tn(probs, gout)
+                gk[hh] = dk if gk[hh] is None else gk[hh] + dk
+                gv[hh] = dv if gv[hh] is None else gv[hh] + dv
+            store(rows, 0, (jnp.where(own, gq[0], gq[1]) * 0.125).astype(BF16))
+        store(keys, 1, (jnp.where(own_k, gk[0], gk[1]) * 0.125).astype(BF16))
+        store(keys, 2, jnp.where(own_k, gv[0], gv[1]).astype(BF16))
+        if n_key < n_query:
+            rest = slice(n * n_query + n_key, (n + 1) * n_query)
+            empty = jnp.zeros((n_query - n_key, 128), BF16)
+            store(rest, 1, empty)
+            store(rest, 2, empty)
+    for hh in range(2):
+        if spatial:
+            fold_bias_sp(db_ref.at[hh], dm_ref, hh)
+        else:
+            fold_bias_st(db_ref.at[hh], dm_ref, hh)
+
+
+def attention_shapes(spatial, tokens):
+    n_query = SWIN * SWIN if spatial else FRAMES * TWIN * TWIN
+    n_key = n_query if spatial else KEYF * TWIN * TWIN
+    return tokens // n_query, n_query, n_key, 256
+
+
+def attention_forward(spatial, qkv, spread, key_ok):
+    tokens, width3 = qkv.shape
+    width = width3 // 3
+    pairs = width // 128
+    n_win, n_query, n_key, chunk = attention_shapes(spatial, tokens)
+    n_heads = 2 * pairs
+    tail = spread.shape[1:]
+    zeros = (0,) * len(tail)
+    return pl.pallas_call(
+        functools.partial(attend_forward, spatial, n_win, n_query, n_key, chunk),
+        grid=(pairs,),
+        in_specs=[
+            pl.BlockSpec((tokens, 128), lambda i: (0, i)),
+            pl.BlockSpec((tokens, 128), lambda i: (0, pairs + i)),
+            pl.BlockSpec((tokens, 128), lambda i: (0, 2 * pairs + i)),
+            pl.BlockSpec((2,) + tail, lambda i: (i,) + zeros),
+            pl.BlockSpec((n_win, 1, n_key), lambda i: (0, 0, 0)),
+        ],
+        out_specs=[
+            pl.BlockSpec((tokens, 128), lambda i: (0, i)),
+            pl.BlockSpec((2, n_win, n_query, n_key), lambda i: (i, 0, 0, 0)),
+        ],
+        out_shape=[
+            jax.ShapeDtypeStruct((tokens, width), BF16),
+            jax.ShapeDtypeStruct((n_heads, n_win, n_query, n_key), BF16),
+        ],
+        scratch_shapes=[pltpu.VMEM((2, n_query, n_key), F32)],
+        compiler_params=pltpu.CompilerParams(vmem_limit_bytes=48 * 1024 * 1024),
+        name="attend_forward",
+    )(qkv, qkv, qkv, spread, key_ok)
+
+
+ROWS = 64
+COLS = 1024
+MESH = pl.DeviceIdType.MESH
+
+
+def place(n_clip):
+    clip = lax.axis_index("clip")
+    x = lax.axis_index("frame")
+    z = clip // 4
+    y = lax.rem(clip // 2, 2)
+    c = lax.rem(clip, 2)
+    return clip, z, y, c, x
+
+
+def remote(src, dst, send, recv, clip, frame):
+    return pltpu.make_async_remote_copy(
+        src_ref=src,
+        dst_ref=dst,
+        send_sem=send,
+        recv_sem=recv,
+        device_id={"clip": clip, "frame": frame},
+        device_id_type=MESH,
+    )
+
+
+def greet(targets):
+    barrier = pltpu.get_barrier_semaphore()
+    count = 0
+    for clip, frame, valid in targets:
+        if valid is None:
+            pl.semaphore_signal(barrier, inc=1, device_id={"clip": clip, "frame": frame}, device_id_type=MESH)
+            count = count + 1
+        else:
+            @pl.when(valid)
+            def _():
+                pl.semaphore_signal(barrier, inc=1, device_id={"clip": clip, "frame": frame}, device_id_type=MESH)
+            count = count + valid.astype(jnp.int32)
+    pl.semaphore_wait(barrier, count)
+
+
+GATHER_HI = 640
+
+
+def gather_tick(t, n, nz, where, shard, full, local, up_s, up_r, dn_s, dn_r, y_s, y_r, x_s, x_r, c_s, c_r):
+    clip, z, y, c, x = where
+    hi = GATHER_HI
+    lo = COLS - hi
+    fetch = pl.ds(pl.multiple_of(x * lo, 128), hi)
+    give = pl.ds(pl.multiple_of(x * hi, 128), lo)
+    last = nz - 1
+
+    def own(i):
+        return pltpu.make_async_copy(
+            shard.at[i, :, fetch], full.at[i, z, y, c, :, fetch], local.at[i]
+        )
+
+    def up(i, s, origin):
+        src = shard.at[i, :, fetch] if s == 0 else full.at[i, origin, y, c, :, fetch]
+        return remote(src, full.at[i, origin, y, c, :, fetch], up_s.at[s, i], up_r.at[s, i], clip + 4, x)
+
+    def down(i, s, origin):
+        src = shard.at[i, :, fetch] if s == 0 else full.at[i, origin, y, c, :, fetch]
+        return remote(src, full.at[i, origin, y, c, :, fetch], dn_s.at[s, i], dn_r.at[s, i], clip - 4, x)
+
+    def over_y(i):
+        src = full.at[i, :, y, c, :, fetch]
+        return remote(src, src, y_s.at[i], y_r.at[i], clip + 2 - 4 * y, x)
+
+    def over_x(i):
+        src = full.at[i, :, :, c, :, give]
+        return remote(src, src, x_s.at[i], x_r.at[i], clip, 1 - x)
+
+    def over_c(i):
+        src = full.at[i, :, :, c]
+        return remote(src, src, c_s.at[i], c_r.at[i], clip + 1 - 2 * c, x)
+
+    def when_item(i):
+        return jnp.logical_and(i >= 0, i < n)
+
+    def z_wait(i, s):
+        @pl.when(z - 1 - s >= 0)
+        def _():
+            up(i, s, z - 1 - s).wait_recv()
+
+        @pl.when(z + 1 + s <= last)
+        def _():
+            down(i, s, z + 1 + s).wait_recv()
+
+    def z_start(i, s):
+        @pl.when(jnp.logical_and(z < last, z - s >= 0))
+        def _():
+            up(i, s, z - s).start()
+
+        @pl.when(jnp.logical_and(z > 0, z + s <= last))
+        def _():
+            down(i, s, z + s).start()
+
+    def z_sent(i, s):
+        @pl.when(jnp.logical_and(z < last, z - s >= 0))
+        def _():
+            up(i, s, z - s).wait_send()
+
+        @pl.when(jnp.logical_and(z > 0, z + s <= last))
+        def _():
+            down(i, s, z + s).wait_send()
+
+    steps = nz - 1
+    i = t
+
+    @pl.when(when_item(i))
+    def _():
+        own(i).start()
+        z_start(i, 0)
+
+    for s in range(1, steps):
+        i = t - s
+
+        @pl.when(when_item(i))
+        def _(i=i, s=s):
+            z_wait(i, s - 1)
+            z_start(i, s)
+
+    i_y = t - steps
+
+    @pl.when(when_item(i_y))
+    def _():
+        z_wait(i_y, steps - 1)
+        own(i_y).wait()
+        over_y(i_y).start()
+
+    i_x = t - steps - 1
+
+    @pl.when(when_item(i_x))
+    def _():
+        over_y(i_x).wait_recv()
+        over_x(i_x).start()
+
+    i_c = t - steps - 2
+
+    @pl.when(when_item(i_c))
+    def _():
+        over_x(i_c).wait_recv()
+        over_c(i_c).start()
+
+    i_d = t - steps - 3
+
+    @pl.when(when_item(i_d))
+    def _():
+        over_c(i_d).wait_recv()
+        for s in range(steps):
+            z_sent(i_d, s)
+        over_y(i_d).wait_send()
+        over_x(i_d).wait_send()
+        over_c(i_d).wait_send()
+
+
+def gather_kernel(n, nz, shard, full, *sems):
+    where = place(4 * nz)
+    clip, z, y, c, x = where
+    greet([
+        (clip + 4, x, z < nz - 1),
+        (clip - 4, x, z > 0),
+        (clip + 2 - 4 * y, x, None),
+        (clip, 1 - x, None),
+        (clip + 1 - 2 * c, x, None),
+    ])
+
+    def step(t, carry):
+        gather_tick(t, n, nz, where, shard, full, *sems)
+        return carry
+
+    lax.fori_loop(0, n + nz + 2, step, 0)
+
+
+def gather_sems(n, nz):
+    dma = pltpu.SemaphoreType.DMA
+    z = dma((nz - 1, n))
+    one = dma((n,))
+    return [one, z, z, z, z, one, one, one, one, one, one]
+
+
+def gather_all(shard, nz, cid):
+    n = shard.shape[0]
+    return pl.pallas_call(
+        functools.partial(gather_kernel, n, nz),
+        out_shape=jax.ShapeDtypeStruct((n, nz, 2, 2, ROWS, COLS), BF16),
+        in_specs=[pl.BlockSpec(memory_space=pl.ANY)],
+        out_specs=pl.BlockSpec(memory_space=pl.ANY),
+        scratch_shapes=gather_sems(n, nz),
+        compiler_params=pltpu.CompilerParams(collective_id=cid, has_side_effects=True),
+        name="gather_all",
+    )(shard)
+
+
+NBUF = 3
+REDUCE_TAIL = 7
+NACC = 4
+
+
+def reduce_tick(t, n, nz, where, sources, out, acc, cbuf, ya, xa, yb, xb, tb, zb, sb, fb, ob,
+                loc, c_s, c_r, ya_s, ya_r, xa_s, xa_r, yb_s, yb_r, xb_s, xb_r, z_s, z_r, f_s, f_r, o_s,
+                cred_c, cred_y, cred_x, cred_z, cred_f):
+    clip, z, y, c, x = where
+    half = COLS // 2
+    quarter = COLS // 4
+    peer_c = clip + 1 - 2 * c
+    peer_y = clip + 2 - 4 * y
+
+    def lanes(base, which):
+        return pl.ds(pl.multiple_of(base + which * quarter, 128), quarter)
+
+    mine1, their1 = lanes(0, x), lanes(0, 1 - x)
+    mine2, their2 = lanes(half, x), lanes(half, 1 - x)
+
+    def slot(i):
+        return lax.rem(i, NBUF)
+
+    def aslot(i):
+        return lax.rem(i, NACC)
+
+    def load(i, source, first):
+        return pltpu.make_async_copy(source.at[i - first, :, :, c], acc.at[aslot(i)], loc.at[slot(i)])
+
+    def over_c(i, source, first):
+        src = source.at[i - first, :, :, 1 - c]
+        return remote(src, cbuf.at[slot(i)], c_s.at[slot(i)], c_r.at[slot(i)], peer_c, x)
+
+    def over_ya(i):
+        return remote(acc.at[aslot(i), :, 1 - y, :, pl.ds(0, half)], ya.at[slot(i)], ya_s.at[slot(i)], ya_r.at[slot(i)], peer_y, x)
+
+    def over_xa(i):
+        return remote(acc.at[aslot(i), :, :, :, their2], xa.at[slot(i)], xa_s.at[slot(i)], xa_r.at[slot(i)], clip, 1 - x)
+
+    def over_xb(i):
+        return remote(acc.at[aslot(i), :, y, :, their1], xb.at[slot(i)], xb_s.at[slot(i)], xb_r.at[slot(i)], clip, 1 - x)
+
+    def over_yb(i):
+        return remote(acc.at[aslot(i), :, 1 - y, :, mine2], yb.at[slot(i)], yb_s.at[slot(i)], yb_r.at[slot(i)], peer_y, x)
+
+    def over_z(i, k):
+        to = lax.rem(z + k, nz)
+        return remote(tb.at[slot(i), to], zb.at[slot(i), k - 1], z_s.at[slot(i), k - 1], z_r.at[slot(i), k - 1],
+                      clip + 4 * (to - z), x)
+
+    def over_f(i):
+        return remote(sb.at[slot(i)], fb.at[slot(i)], f_s.at[slot(i)], f_r.at[slot(i)], clip, 1 - x)
+
+    def write(i):
+        return pltpu.make_async_copy(ob.at[slot(i)], out.at[i], o_s.at[slot(i)])
+
+    def credit(sem, who, frame, i):
+        @pl.when(i + NBUF < n)
+        def _():
+            pl.semaphore_signal(sem, inc=1, device_id={"clip": who, "frame": frame}, device_id_type=MESH)
+
+    def need(sem, i):
+        @pl.when(i >= NBUF)
+        def _():
+            pl.semaphore_wait(sem, 1)
+
+    def item(i):
+        return jnp.logical_and(i >= 0, i < n)
+
+    i = t - 6
+
+    @pl.when(item(i))
+    def _(i=i):
+        write(i).wait()
+
+    i = t
+
+    @pl.when(item(i))
+    def _(i=i):
+        need(cred_c, i)
+        first = 0
+        for source, skip, count in sources:
+
+            @pl.when(jnp.logical_and(i >= first, i < first + count))
+            def _(source=source, offset=first - skip):
+                over_c(i, source, offset).start()
+                load(i, source, offset).start()
+
+            first += count
+
+    i = t - 1
+
+    @pl.when(item(i))
+    def _(i=i):
+        over_c(i, sources[0][0], i).wait()
+        load(i, sources[0][0], i).wait()
+        a, b = aslot(i), slot(i)
+
+        def body(k, carry):
+            acc[a, k] = acc[a, k] + cbuf[b, k]
+            return carry
+
+        lax.fori_loop(0, nz, body, 0)
+        credit(cred_c, peer_c, x, i)
+        need(cred_y, i)
+        need(cred_x, i)
+        over_ya(i).start()
+        over_xa(i).start()
+
+    i = t - 2
+
+    @pl.when(item(i))
+    def _(i=i):
+        over_ya(i).wait()
+        over_xa(i).wait()
+        a, b = aslot(i), slot(i)
+
+        def body(k, carry):
+            acc[a, k, y, :, pl.ds(0, half)] = acc[a, k, y, :, pl.ds(0, half)] + ya[b, k]
+            acc[a, k, :, :, mine2] = acc[a, k, :, :, mine2] + xa[b, k]
+            return carry
+
+        lax.fori_loop(0, nz, body, 0)
+        over_xb(i).start()
+        over_yb(i).start()
+
+    i = t - 3
+
+    @pl.when(item(i))
+    def _(i=i):
+        over_xb(i).wait()
+        over_yb(i).wait()
+        a, b = aslot(i), slot(i)
+
+        def body(k, carry):
+            tb[b, k, :, pl.ds(0, quarter)] = acc[a, k, y, :, mine1] + xb[b, k]
+            tb[b, k, :, pl.ds(quarter, quarter)] = acc[a, k, y, :, mine2] + yb[b, k]
+            return carry
+
+        lax.fori_loop(0, nz, body, 0)
+        credit(cred_y, peer_y, x, i)
+        credit(cred_x, clip, 1 - x, i)
+        for k in range(1, nz):
+            need(cred_z.at[k - 1], i)
+            over_z(i, k).start()
+
+    i = t - 4
+
+    @pl.when(item(i))
+    def _(i=i):
+        for k in range(1, nz):
+            over_z(i, k).wait()
+        b = slot(i)
+        total = tb[b, z].astype(F32)
+        for k in range(1, nz):
+            total = total + zb[b, k - 1].astype(F32)
+        sb[b] = total.astype(BF16)
+        for k in range(1, nz):
+            sender = lax.rem(z + nz - k, nz)
+            credit(cred_z.at[k - 1], clip + 4 * (sender - z), x, i)
+        need(cred_f, i)
+        over_f(i).start()
+
+    i = t - 5
+
+    @pl.when(item(i))
+    def _(i=i):
+        over_f(i).wait()
+        b = slot(i)
+        ob[b, :, mine1] = sb[b, :, pl.ds(0, quarter)].astype(F32)
+        ob[b, :, mine2] = sb[b, :, pl.ds(quarter, quarter)].astype(F32)
+        ob[b, :, their1] = fb[b, :, pl.ds(0, quarter)].astype(F32)
+        ob[b, :, their2] = fb[b, :, pl.ds(quarter, quarter)].astype(F32)
+        credit(cred_f, clip, 1 - x, i)
+        write(i).start()
+
+
+def greet_reduce(nz, where):
+    clip, z, y, c, x = where
+    others = [(clip + 4 * (lax.rem(z + k, nz) - z), x, None) for k in range(1, nz)]
+    greet(others + [
+        (clip + 2 - 4 * y, x, None),
+        (clip, 1 - x, None),
+        (clip + 1 - 2 * c, x, None),
+    ])
+
+
+def reduce_kernel(picks, nz, *refs):
+    n_in = len(picks)
+    sources = [(ref, skip, count) for ref, (skip, count) in zip(refs[:n_in], picks)]
+    out, rest = refs[n_in], refs[n_in + 1 :]
+    n = sum(count for _, count in picks)
+    where = place(4 * nz)
+    greet_reduce(nz, where)
+
+    def step(t, carry):
+        reduce_tick(t, n, nz, where, sources, out, *rest)
+        return carry
+
+    lax.fori_loop(0, n + REDUCE_TAIL, step, 0)
+
+
+def reduce_scratch(nz):
+    half, quarter = COLS // 2, COLS // 4
+    dma = pltpu.SemaphoreType.DMA
+    one = dma((NBUF,))
+    regular = pltpu.SemaphoreType.REGULAR
+    return [
+        pltpu.VMEM((NACC, nz, 2, ROWS, COLS), BF16),
+        pltpu.VMEM((NBUF, nz, 2, ROWS, COLS), BF16),
+        pltpu.VMEM((NBUF, nz, ROWS, half), BF16),
+        pltpu.VMEM((NBUF, nz, 2, ROWS, quarter), BF16),
+        pltpu.VMEM((NBUF, nz, ROWS, quarter), BF16),
+        pltpu.VMEM((NBUF, nz, ROWS, quarter), BF16),
+        pltpu.VMEM((NBUF, nz, ROWS, half), BF16),
+        pltpu.VMEM((NBUF, nz - 1, ROWS, half), BF16),
+        pltpu.VMEM((NBUF, ROWS, half), BF16),
+        pltpu.VMEM((NBUF, ROWS, half), BF16),
+        pltpu.VMEM((NBUF, ROWS, COLS), F32),
+        one, one, one, one, one, one, one, one, one, one, one,
+        dma((NBUF, nz - 1)), dma((NBUF, nz - 1)),
+        one, one, one,
+        regular, regular, regular, pltpu.SemaphoreType.REGULAR((nz - 1,)), regular,
+    ]
+
+
+def reduce_all(grads, picks, nz, cid):
+    n = sum(count for _, count in picks)
+    return pl.pallas_call(
+        functools.partial(reduce_kernel, picks, nz),
+        out_shape=jax.ShapeDtypeStruct((n, ROWS, COLS), F32),
+        in_specs=[pl.BlockSpec(memory_space=pl.ANY)] * len(grads),
+        out_specs=pl.BlockSpec(memory_space=pl.ANY),
+        scratch_shapes=reduce_scratch(nz),
+        compiler_params=pltpu.CompilerParams(
+            collective_id=cid, has_side_effects=True, vmem_limit_bytes=48 * 1024 * 1024
+        ),
+        name="reduce_all",
+    )(*grads)
+
+
+CHUNK = 512
+STEP_ROWS = 128
+MIB = 1024 * 1024
+GELU_C = 0.7978845608028654
+GELU_A = 0.044715
+
+
+def fixed(shape, **kw):
+    zeros = (0,) * len(shape)
+    return pl.BlockSpec(shape, lambda i: zeros, pipeline_mode=pl.Buffered(1), **kw)
+
+
+def over_rows(tokens, body):
+    def step(k, carry):
+        body(pl.ds(pl.multiple_of(k * STEP_ROWS, STEP_ROWS), STEP_ROWS))
+        return carry
+
+    lax.fori_loop(0, tokens // STEP_ROWS, step, 0)
+
+
+def qkv_body(s_ref, m_ref, w_ref, na_ref, q_ref):
+    @pl.when(pl.program_id(0) == 0)
+    def _():
+        def rows_of(rows):
+            normed, _ = norm_stats(s_ref[rows, :])
+            na_ref[rows, :] = (normed * (1.0 + m_ref[1:2, :]) + m_ref[0:1, :]).astype(BF16)
+
+        over_rows(s_ref.shape[0], rows_of)
+
+    q_ref[...] = dot_nn(na_ref[...], w_ref[0]).astype(BF16)
+
+
+def qkv_forward(stream, mods, weights, base):
+    tokens, width = stream.shape
+    per = width // CHUNK
+    return pl.pallas_call(
+        qkv_body,
+        grid=(3 * per,),
+        in_specs=[
+            fixed((tokens, width)),
+            fixed(mods.shape),
+            pl.BlockSpec((1, width, CHUNK), lambda i: (base + i // per, 0, i % per)),
+        ],
+        out_specs=[fixed((tokens, width)), pl.BlockSpec((tokens, CHUNK), lambda i: (0, i))],
+        out_shape=[
+            jax.ShapeDtypeStruct((tokens, width), BF16),
+            jax.ShapeDtypeStruct((tokens, 3 * width), BF16),
+        ],
+        compiler_params=pltpu.CompilerParams(vmem_limit_bytes=48 * MIB),
+        name="qkv_forward",
+    )(stream, mods, weights)
+
+
+def proj_body(att_ref, s_ref, m_ref, w_ref, proj_ref, mid_ref, nm_ref):
+    proj = dot_nn(att_ref[...], w_ref[0])
+    proj_ref[...] = proj.astype(BF16)
+    mid = s_ref[...] + m_ref[2:3, :] * proj
+    mid_ref[...] = mid
+    normed, _ = norm_stats(mid)
+    nm_ref[...] = (normed * (1.0 + m_ref[4:5, :]) + m_ref[3:4, :]).astype(BF16)
+
+
+def proj_forward(att, stream, mods, weights, base):
+    tokens, width = stream.shape
+    rows = 256
+    row = pl.BlockSpec((rows, width), lambda i: (i, 0))
+    return pl.pallas_call(
+        proj_body,
+        grid=(tokens // rows,),
+        in_specs=[row, row, fixed(mods.shape), pl.BlockSpec((1, width, width), lambda i: (base + 3, 0, 0))],
+        out_specs=[row, row, row],
+        out_shape=[
+            jax.ShapeDtypeStruct((tokens, width), BF16),
+            jax.ShapeDtypeStruct((tokens, width), F32),
+            jax.ShapeDtypeStruct((tokens, width), BF16),
+        ],
+        compiler_params=pltpu.CompilerParams(vmem_limit_bytes=48 * MIB),
+        name="proj_forward",
+    )(att, stream, mods, weights)
+
+
+def down_rows(w_ref):
+    return jnp.concatenate(
+        [w_ref[sub, c * 64 : (c + 1) * 64, :] for c in range(2) for sub in range(4)], axis=0
+    )
+
+
+def mlp_forward_body(n_steps, nm_ref, mid_ref, m_ref, up_ref, dn_ref, act_ref, dact_ref, down_ref, res_ref, acc_ref):
+    step = pl.program_id(0)
+    tokens = nm_ref.shape[0]
+    w_down = down_rows(dn_ref)
+    rows_each = 256
+
+    def part(k, carry):
+        rows = pl.ds(pl.multiple_of(k * rows_each, rows_each), rows_each)
+        up = dot_nn(nm_ref[rows, :], up_ref[0])
+        square = up * up
+        tanh = jnp.tanh(GELU_C * up * (1.0 + GELU_A * square))
+        half = 0.5 * (1.0 + tanh)
+        act = (up * half).astype(BF16)
+        slope = GELU_C * (1.0 + 3.0 * GELU_A * square)
+        act_ref[rows, :] = act
+        dact_ref[rows, :] = (half + 0.5 * up * (1.0 - tanh * tanh) * slope).astype(BF16)
+        down = dot_nn(act, w_down)
+
+        @pl.when(step == 0)
+        def _():
+            acc_ref[rows, :] = down
+
+        @pl.when(step > 0)
+        def _():
+            acc_ref[rows, :] += down
+
+        return carry
+
+    lax.fori_loop(0, tokens // rows_each, part, 0)
+
+    @pl.when(step == n_steps - 1)
+    def _():
+        def rows_of(rows):
+            down = acc_ref[rows, :]
+            down_ref[rows, :] = down.astype(BF16)
+            res_ref[rows, :] = (mid_ref[rows, :] + m_ref[5:6, :] * down).astype(res_ref.dtype)
+
+        over_rows(tokens, rows_of)
+
+
+def mlp_forward(normed_m, mid, mods, weights, base, result_type):
+    tokens, width = mid.shape
+    n_steps = 4 * width // CHUNK
+    per = width // CHUNK
+    hidden = 4 * width
+    return pl.pallas_call(
+        functools.partial(mlp_forward_body, n_steps),
+        grid=(n_steps,),
+        in_specs=[
+            fixed((tokens, width)),
+            fixed((tokens, width)),
+            fixed(mods.shape),
+            pl.BlockSpec((1, width, CHUNK), lambda i: (base + 4 + i // per, 0, i % per)),
+            pl.BlockSpec((4, 128, width), lambda i: (base // 4 + 2, i, 0)),
+        ],
+        out_specs=[
+            pl.BlockSpec((tokens, CHUNK), lambda i: (0, i)),
+            pl.BlockSpec((tokens, CHUNK), lambda i: (0, i)),
+            fixed((tokens, width)),
+            fixed((tokens, width)),
+        ],
+        out_shape=[
+            jax.ShapeDtypeStruct((tokens, hidden), BF16),
+            jax.ShapeDtypeStruct((tokens, hidden), BF16),
+            jax.ShapeDtypeStruct((tokens, width), BF16),
+            jax.ShapeDtypeStruct((tokens, width), result_type),
+        ],
+        scratch_shapes=[pltpu.VMEM((tokens, width), F32)],
+        compiler_params=pltpu.CompilerParams(vmem_limit_bytes=56 * MIB),
+        name="mlp_forward",
+    )(normed_m, mid, mods, weights, weights)
+
+
+def norm_back_rows(values, scale_row, grad):
+    normed, inv = norm_stats(values)
+    u = grad * (1.0 + scale_row)
+    out = (
+        u
+        - jnp.mean(u, axis=-1, keepdims=True)
+        - normed * jnp.mean(u * normed, axis=-1, keepdims=True)
+    ) * inv
+    return out, jnp.sum(grad, axis=0, keepdims=True), jnp.sum(grad * normed, axis=0, keepdims=True)
+
+
+BLOCK_ROWS = 128
+
+
+def backward_plan(tokens, width):
+    rows = tokens // BLOCK_ROWS
+    chunks = 4 * width // CHUNK
+    halves = width // CHUNK
+    pairs = width // 128
+    sizes = (rows, chunks, rows, halves, pairs, 3 * halves, rows)
+    starts = [0]
+    for size in sizes:
+        starts.append(starts[-1] + size)
+    return starts
+
+
+def backward_body(
+    spatial, shapes, n_prev, n_own, tick_steps, nz,
+    g_ref, down_ref, mid_ref, proj_ref, s_ref, m_ref, act_ref, dact_ref, w_ref, dn_ref,
+    q_ref, k_ref, v_ref, p_ref, nm_hbm, att_hbm, na_hbm, prev_hbm,
+    out_ref, dm_ref, rows_ref, grads_hbm, share_hbm,
+    res_ref, gv_ref, e_ref, gm_ref, ga_ref, gq_ref, db_ref, gdb_ref, gub_ref,
+    res_sem, gd_sem, gu_sem, *comm,
+):
+    n_win, n_query, n_key, chunk = shapes
+    tokens, width = e_ref.shape
+    starts = backward_plan(tokens, width)
+    a0, a1, a2, a3, a4, a5, a6, end = starts
+    halves = width // CHUNK
+    step = pl.program_id(0)
+    where = place(4 * nz)
+    n_items = n_prev + n_own
+    sources = []
+    if n_prev:
+        sources.append((prev_hbm, 8, n_prev))
+    sources.append((grads_hbm, 0, n_own))
+
+    @pl.when(step == 0)
+    def _():
+        greet_reduce(nz, where)
+
+    def tick(t):
+        reduce_tick(t, n_items, nz, where, sources, share_hbm, *comm)
+
+    due = jnp.zeros((), jnp.bool_)
+    passed = jnp.zeros((), jnp.int32)
+    for s in tick_steps:
+        due = jnp.logical_or(due, step == s)
+        passed = passed + (step > s).astype(jnp.int32)
+
+    def resident(source):
+        return pltpu.make_async_copy(source, res_ref, res_sem)
+
+    def put_down(i):
+        slot = lax.rem(i, 2)
+        target = grads_hbm.at[pl.ds(0, 4), i // 2, lax.rem(i, 2)]
+        return pltpu.make_async_copy(gdb_ref.at[slot], target, gd_sem.at[slot])
+
+    def put_cols(i, item, half):
+        slot = lax.rem(i, 2)
+        cols = pl.ds(pl.multiple_of(half * CHUNK, CHUNK), CHUNK)
+        target = grads_hbm.at[item, :, :, :, :, cols]
+        return pltpu.make_async_copy(gub_ref.at[slot], target, gu_sem.at[slot])
+
+    def keep_cols(i, values):
+        gub_ref[lax.rem(i, 2)] = values.reshape(gub_ref.shape[1:])
+
+    def rows_at(i):
+        return pl.ds(pl.multiple_of(i * BLOCK_ROWS, BLOCK_ROWS), BLOCK_ROWS)
+
+    def add_e(first, left, right):
+        part = tokens // 2
+        for k in range(2):
+            rows = slice(k * part, (k + 1) * part)
+            value = dot_nt(left[rows], right)
+
+            @pl.when(first)
+            def _(rows=rows, value=value):
+                e_ref[rows, :] = value
+
+            @pl.when(jnp.logical_not(first))
+            def _(rows=rows, value=value):
+                e_ref[rows, :] += value
+
+    @pl.when(step == 0)
+    def _():
+        resident(nm_hbm).start()
+        rows_ref[...] = jnp.zeros_like(rows_ref)
+
+    @pl.when(step < a1)
+    def _():
+        grad = g_ref[...].astype(F32)
+        gv_ref[rows_at(step), :] = (m_ref[5:6, :] * grad).astype(BF16)
+        rows_ref[5:6, :] += jnp.sum(grad * down_ref[...].astype(F32), axis=0, keepdims=True)
+
+    @pl.when(step == a1)
+    def _():
+        resident(nm_hbm).wait()
+
+    @pl.when(jnp.logical_and(step >= a1, step < a2))
+    def _():
+        i = step - a1
+
+        @pl.when(i >= 2)
+        def _():
+            put_down(i).wait()
+            put_cols(i, 4, 0).wait()
+
+        gdv = gv_ref[...]
+        grad_act = dot_nt(gdv, down_rows(dn_ref))
+        gup = (grad_act * dact_ref[...].astype(F32)).astype(BF16)
+        slot = lax.rem(i, 2)
+        grad_down = dot_tn(act_ref[...], gdv).astype(BF16)
+        for c in range(2):
+            for sub in range(4):
+                first = (c * 4 + sub) * 64
+                gdb_ref[slot, sub, c] = grad_down[first : first + 64, :]
+        put_down(i).start()
+        keep_cols(i, dot_tn(res_ref[...], gup).astype(BF16))
+        put_cols(i, 4 + i // halves, lax.rem(i, halves)).start()
+        add_e(i == 0, gup, w_ref[0])
+
+    @pl.when(step == a2)
+    def _():
+        resident(att_hbm).start()
+        for k in range(2):
+            put_down(k).wait()
+            put_cols(k, 4, 0).wait()
+
+    @pl.when(jnp.logical_and(step >= a2, step < a3))
+    def _():
+        rows = rows_at(step - a2)
+        out, shift, scale = norm_back_rows(mid_ref[...], m_ref[4:5, :], e_ref[rows, :])
+        grad_mid = out + g_ref[...].astype(F32)
+        gm_ref[rows, :] = grad_mid
+        gv_ref[rows, :] = (m_ref[2:3, :] * grad_mid).astype(BF16)
+        rows_ref[3:4, :] += shift
+        rows_ref[4:5, :] += scale
+        rows_ref[2:3, :] += jnp.sum(grad_mid * proj_ref[...].astype(F32), axis=0, keepdims=True)
+
+    @pl.when(step == a3)
+    def _():
+        resident(att_hbm).wait()
+
+    @pl.when(jnp.logical_and(step >= a3, step < a4))
+    def _():
+        i = step - a3
+        part = gv_ref[:, pl.ds(pl.multiple_of(i * CHUNK, CHUNK), CHUNK)]
+        keep_cols(i, dot_tn(res_ref[...], part).astype(BF16))
+        put_cols(i, 8, i).start()
+        add_e(i == 0, part, w_ref[0])
+
+    @pl.when(step == a4)
+    def _():
+        resident(na_hbm).start()
+        ga_ref[...] = e_ref[...].astype(BF16)
+
+    @pl.when(jnp.logical_and(step >= a4, step < a5))
+    def _():
+        head = step - a4
+        lanes = pl.ds(pl.multiple_of(head * 128, 128), 128)
+        attend_backward(
+            spatial, n_win, n_query, n_key, chunk, head,
+            q_ref, k_ref, v_ref, ga_ref.at[:, lanes], p_ref, gq_ref, dm_ref, db_ref,
+        )
+
+    @pl.when(step == a5)
+    def _():
+        resident(na_hbm).wait()
+
+    @pl.when(jnp.logical_and(step >= a5, step < a6))
+    def _():
+        i = step - a5
+        put_cols(i, 8, 0).wait()
+        part = gq_ref[:, pl.ds(pl.multiple_of(i * CHUNK, CHUNK), CHUNK)]
+        keep_cols(i, dot_tn(res_ref[...], part).astype(BF16))
+        put_cols(i, 9 + i // halves, lax.rem(i, halves)).start()
+        add_e(i == 0, part, w_ref[0])
+
+    @pl.when(step >= a6)
+    def _():
+        rows = rows_at(step - a6)
+        out, shift, scale = norm_back_rows(s_ref[...].astype(F32), m_ref[1:2, :], e_ref[rows, :])
+        out_ref[...] = (out + gm_ref[rows, :]).astype(out_ref.dtype)
+        rows_ref[0:1, :] += shift
+        rows_ref[1:2, :] += scale
+
+    @pl.when(due)
+    def _():
+        tick(passed)
+
+    @pl.when(step == end - 1)
+    def _():
+        for k in range(2):
+            put_cols(k, 8, 0).wait()
+
+        def rest(t, carry):
+            tick(t)
+            return carry
+
+        lax.fori_loop(len(tick_steps), n_items + REDUCE_TAIL, rest, 0)
+
+
+def block_backward(grad, saved, mods, weights, base, spread_shape, spatial, out_type, prev, n_own, tick_steps, nz, cid):
+    stream, normed_a, qkv, probs, att, proj, mid, normed_m, act, dact, down = saved
+    tokens, width = mid.shape
+    shapes = attention_shapes(spatial, tokens)
+    n_win, n_query, n_key, _ = shapes
+    pairs = width // 128
+    halves = width // CHUNK
+    a0, a1, a2, a3, a4, a5, a6, end = backward_plan(tokens, width)
+    tail = spread_shape[1:]
+    zeros = (0,) * len(tail)
+
+    def at(start, stop):
+        return lambda i: jnp.clip(i - start, 0, stop - start - 1)
+
+    def row_block(place_of):
+        return pl.BlockSpec((BLOCK_ROWS, width), lambda i: (place_of(i), 0))
+
+    def g_at(i):
+        return jnp.where(i < a1, i, at(a2, a3)(i))
+
+    def weight_at(i):
+        up = at(a1, a2)(i)
+        proj_half = at(a3, a4)(i)
+        third = at(a5, a6)(i)
+        item = jnp.where(i < a3, 4 + up // halves, jnp.where(i < a5, 3, third // halves))
+        half = jnp.where(i < a3, up % halves, jnp.where(i < a5, proj_half, third % halves))
+        return (base + item, 0, half)
+
+    heads = at(a4, a5)
+    hidden = pl.BlockSpec((tokens, CHUNK), lambda i: (0, at(a1, a2)(i)))
+    anywhere = pl.BlockSpec(memory_space=pl.ANY)
+    n_prev = 0 if prev is None else 4
+    n_items = n_prev + n_own
+    extra = [] if prev is None else [prev]
+    body = functools.partial(backward_body, spatial, shapes, n_prev, n_own, tick_steps, nz)
+    if prev is None:
+        whole = body
+
+        def body(*refs):
+            return whole(*refs[:17], None, *refs[17:])
+
+    dma = pltpu.SemaphoreType.DMA
+    return pl.pallas_call(
+        body,
+        grid=(end,),
+        in_specs=[
+            row_block(g_at),
+            row_block(at(a0, a1)),
+            row_block(at(a2, a3)),
+            row_block(at(a2, a3)),
+            row_block(at(a6, end)),
+            fixed(mods.shape),
+            hidden,
+            hidden,
+            pl.BlockSpec((1, width, CHUNK), weight_at),
+            pl.BlockSpec((4, 128, width), lambda i: (base // 4 + 2, at(a1, a2)(i), 0)),
+            pl.BlockSpec((tokens, 128), lambda i: (0, heads(i))),
+            pl.BlockSpec((tokens, 128), lambda i: (0, pairs + heads(i))),
+            pl.BlockSpec((tokens, 128), lambda i: (0, 2 * pairs + heads(i))),
+            pl.BlockSpec((2, n_win, n_query, n_key), lambda i: (heads(i), 0, 0, 0)),
+            anywhere, anywhere, anywhere,
+        ] + [anywhere] * len(extra),
+        out_specs=[
+            row_block(at(a6, end)),
+            pl.BlockSpec((2,) + tail, lambda i: (heads(i),) + zeros),
+            pl.BlockSpec((8, width), lambda i: (0, 0)),
+            anywhere,
+            anywhere,
+        ],
+        out_shape=[
+            jax.ShapeDtypeStruct((tokens, width), out_type),
+            jax.ShapeDtypeStruct(spread_shape, F32),
+            jax.ShapeDtypeStruct((8, width), F32),
+            jax.ShapeDtypeStruct((12, nz, 2, 2, ROWS, COLS), BF16),
+            jax.ShapeDtypeStruct((n_items, ROWS, COLS), F32),
+        ],
+        scratch_shapes=[
+            pltpu.VMEM((tokens, width), BF16),
+            pltpu.VMEM((tokens, width), BF16),
+            pltpu.VMEM((tokens, width), F32),
+            pltpu.VMEM((tokens, width), F32),
+            pltpu.VMEM((tokens, width), BF16),
+            pltpu.VMEM((tokens, 3 * width), BF16),
+            pltpu.VMEM((2, n_query, n_key), F32),
+            pltpu.VMEM((2, 4, 2, ROWS, COLS), BF16),
+            pltpu.VMEM((2, nz, 2, 2, ROWS, CHUNK), BF16),
+            dma,
+            dma((2,)),
+            dma((2,)),
+        ] + reduce_scratch(nz),
+        compiler_params=pltpu.CompilerParams(
+            collective_id=cid, has_side_effects=True, vmem_limit_bytes=64 * MIB
+        ),
+        name="block_backward",
+    )(grad, down, mid, proj, stream, mods, act, dact, weights, weights, qkv, qkv, qkv, probs,
+      normed_m, att, normed_a, *extra)
+
+
+def block_forward(stream, mods, weights, base, spread, key_ok, spatial, result_type):
+    normed_a, qkv = qkv_forward(stream, mods, weights, base)
+    att, probs = attention_forward(spatial, qkv, spread, key_ok)
+    proj, mid, normed_m = proj_forward(att, stream, mods, weights, base)
+    act, dact, down, result = mlp_forward(normed_m, mid, mods, weights, base, result_type)
+    return result, (stream, normed_a, qkv, probs, att, proj, mid, normed_m, act, dact, down)
+
+
+def swap_rows(values, me, swap):
+    keep = lax.dynamic_index_in_dim(values, me, 1, keepdims=False)
+    send = lax.dynamic_index_in_dim(values, 1 - me, 1, keepdims=False)
+    recv = lax.ppermute(send.astype(BF16), "frame", swap).astype(values.dtype)
+    first = jnp.where(me == 0, keep, recv)
+    second = jnp.where(me == 0, recv, keep)
+    full = jnp.concatenate([first, second], axis=0)
+    return full.transpose(2, 0, 1, 3, 4).reshape(-1, values.shape[-1])
+
+
+def unswap_rows(values, me, swap, n_cw, f_l):
+    depth = values.shape[-1]
+    full = values.reshape(n_cw, 2, f_l, TWIN, TWIN, depth)
+    keep = lax.dynamic_index_in_dim(full, me, 1, keepdims=False)
+    send = lax.dynamic_index_in_dim(full, 1 - me, 1, keepdims=False)
+    recv = lax.ppermute(send.astype(BF16), "frame", swap).astype(values.dtype)
+    first = jnp.where(me == 0, keep, recv)
+    second = jnp.where(me == 0, recv, keep)
+    both = jnp.stack([first, second], axis=0)
+    return both.transpose(2, 0, 3, 1, 4, 5).reshape(-1, depth)
+
+
+def pack_shards(shards, b):
+    w_qkv, w_proj, w_up, w_down = [w[:, b] for w in shards]
+    parts = []
+    for w in (w_qkv, w_proj, w_up):
+        parts.append(w.reshape(ROWS, -1, COLS).transpose(1, 0, 2))
+    parts.append(w_down.reshape(-1, ROWS, COLS))
+    return jnp.concatenate(parts, axis=0)
+
+
+def on_device(
+    frames_in, size_group, modulation, w_qkv, w_proj, w_up, w_down, table_sp, table_st, cotangent
+):
+    n_clips, f_l, n_rows, n_cols, width = frames_in.shape
+    me = lax.axis_index("frame")
+    swap = [(0, 1), (1, 0)]
+    n_cw = n_cols // TWIN
+    nz = lax.axis_size("clip") // 4
+    natural = (f_l, 2, TWIN, n_cw, TWIN, width)
+    shards = (w_qkv, w_proj, w_up, w_down)
+    packed = jnp.concatenate([pack_shards(shards, b) for b in range(2)], axis=0)
+    full = gather_all(packed, nz, 1).reshape(24, 16 * ROWS, COLS)
+    limit = n_cols - 3 * (2 - size_group[0])
+    wide = (jnp.arange(n_cols, dtype=jnp.int32) < limit).astype(F32)
+    ok_sp = jnp.broadcast_to(wide[None, None, None, :], (f_l, 1, n_rows, n_cols))
+    ok_sp = ok_sp.reshape(f_l, 1, n_rows * n_cols)
+    frame_ok = (jnp.arange(KEYF) < FILLED).astype(F32)
+    ok_st = wide.reshape(n_cw, 1, 1, TWIN) * frame_ok[None, :, None, None]
+    ok_st = jnp.broadcast_to(ok_st, (n_cw, KEYF, TWIN, TWIN)).reshape(n_cw, 1, -1)
+    spread0 = spread_sp(table_sp)
+    spread1 = spread_st(table_st)
+    mods = modulation[0].reshape(2, 6, width)
+    mods = jnp.pad(mods, ((0, 0), (0, 2), (0, 0)))
+    cot = swap_rows(cotangent.reshape(natural), me, swap)
+    stream0 = frames_in.reshape(-1, width).astype(F32)
+    mid_stream, saved0 = block_forward(stream0, mods[0], full, 0, spread0, ok_sp, True, F32)
+    stream1 = swap_rows(mid_stream.reshape(natural), me, swap)
+    end_stream, saved1 = block_forward(stream1, mods[1], full, 12, spread1, ok_st, False, BF16)
+    mixed = unswap_rows(end_stream, me, swap, n_cw, f_l).reshape(frames_in.shape)
+    starts = backward_plan(stream0.shape[0], width)
+    ticks1 = tuple(range(starts[2], starts[6] + 4, 2))
+    grad1, gspread1, rows1, gw1, shares1 = block_backward(
+        cot, saved1, mods[1], full, 12, spread1.shape, False, F32, None, 8, ticks1, nz, 2
+    )
+    grad_mid = unswap_rows(grad1, me, swap, n_cw, f_l)
+    ticks0 = (0,) + tuple(range(starts[1], starts[2], 3)) + tuple(range(starts[2], starts[6] + 4, 2))
+    grad0, gspread0, rows0, gw0, shares0 = block_backward(
+        grad_mid, saved0, mods[0], full, 0, spread0.shape, True, BF16, gw1, 8, ticks0, nz, 3
+    )
+    last = reduce_all([gw0], [(8, 4)], nz, 4)
+    shares = jnp.stack([
+        jnp.concatenate([shares0[4:12], last], axis=0),
+        jnp.concatenate([shares1, shares0[0:4]], axis=0),
+    ])
+
+    def columns(lo, hi):
+        part = shares[:, lo:hi]
+        return part.transpose(2, 0, 1, 3).reshape(ROWS, 2, (hi - lo) * COLS)
+
+    g_down = shares[:, 0:4].reshape(2, 4 * ROWS, COLS).transpose(1, 0, 2)
+    outs = (columns(9, 12), columns(8, 9), columns(4, 8), g_down)
+    mod_grad = lax.psum(jnp.concatenate([rows0[:6], rows1[:6]], axis=0), "frame")[None]
+    g_sp = lax.psum(gather_sp(gspread0), ("clip", "frame"))
+    g_st = lax.psum(gather_st(gspread1), ("clip", "frame"))
+    grad_in = grad0.reshape(frames_in.shape)
+    return (mixed, grad_in, mod_grad, outs[0], outs[1], outs[2], outs[3], g_sp, g_st)
+
+
 HIGHEST = lax.Precision.HIGHEST
 
 
@@ -126,7 +1417,7 @@
     return expo_values / jnp.sum(expo_values, axis=-1, keepdims=True)
 
 
-def block_forward(
+def general_forward(
     stream,
     mod_rows,
     weights,
@@ -184,7 +1475,7 @@
     return (result, saved)
 
 
-def block_backward(
+def general_backward(
     grad_out,
     saved,
     mod_rows,
@@ -283,7 +1574,7 @@
     return (grad_stream, mod_grad, (qkv_grad, proj_grad, up_grad, down_grad), grad_bias)
 
 
-def on_device(
+def on_device_general(
     frames_in, size_group, modulation, w_qkv, w_proj, w_up, w_down, table_sp, table_st, cotangent
 ):
     n_clips, local_frames, n_rows, n_cols, width_d = frames_in.shape
@@ -345,7 +1636,7 @@
 
     weights_sp = (gathered[0][:, 0], gathered[1][:, 0], gathered[2][:, 0], gathered[3][:, 0])
     weights_st = (gathered[0][:, 1], gathered[1][:, 1], gathered[2][:, 1], gathered[3][:, 1])
-    stream_mid, saved_sp = block_forward(
+    stream_mid, saved_sp = general_forward(
         frames_in.astype(jnp.float32),
         modulation[:, 0:6],
         weights_sp,
@@ -357,7 +1648,7 @@
         spatial_keys,
         score_scale,
     )
-    stream_end, saved_st = block_forward(
+    stream_end, saved_st = general_forward(
         stream_mid,
         modulation[:, 6:12],
         weights_st,
@@ -384,7 +1675,7 @@
     )
     key_win_st = split_heads(cube_windows(key_again), n_heads)
     value_win_st = split_heads(cube_windows(value_again), n_heads)
-    grad_stream, mod_grad_st, grads_st, bias_grad_st = block_backward(
+    grad_stream, mod_grad_st, grads_st, bias_grad_st = general_backward(
         cotangent.astype(jnp.float32),
         saved_st,
         modulation[:, 6:12],
@@ -399,7 +1690,7 @@
         value_win_st,
         score_scale,
     )
-    grad_stream, mod_grad_sp, grads_sp, bias_grad_sp = block_backward(
+    grad_stream, mod_grad_sp, grads_sp, bias_grad_sp = general_backward(
         grad_stream,
         saved_sp,
         modulation[:, 0:6],
@@ -474,8 +1765,9 @@
         P(),
         P("clip", "frame", None, None, None),
     )
+    whole_windows = mesh.shape["frame"] == 2 and mesh.shape["clip"] == 16
     return jax.shard_map(
-        on_device,
+        on_device if whole_windows else on_device_general,
         mesh=mesh,
         in_specs=placed,
         out_specs=(

time: 2070 us -> 1030 us (0.50)
  local copies, waits for them, and re-layouts: 980 us -> 70.1 us
  Pallas kernels: 0 us -> 821 us
  matrix products: 473 us -> 6.31 us
  waiting for transfers between devices: 394 us -> 35.3 us
  other arithmetic: 123 us -> 21.8 us
    pallas_call x0 -> x12, Pallas kernels: none -> 821 us  [the longest x2 350 us: block_backward(): pl.pallas_call(body, grid=(end,), in_specs=[row_block(g_at), row_block(at...]
    dot_general x44 -> x4, matrix products: 440 us -> 6.31 us  [the longest x1 2.59 us: gather_sp(): out = lax.dot_general(flat, pick_sp(), NT, precision=lax.Precision.HIGHEST)]
    reshape x14 -> x5, local copies, waits for them, and re-layouts: 415 us -> 4.06 us  [the longest x1 2.94 us: on_device(): g_down = shares[:, 0:4].reshape(2, 4 * ROWS, COLS).transpose(1, 0, 2)]
    all_gather x6 -> x0, waiting for transfers between devices: 216 us -> none  [the longest x1 109 us: on_device(): lax.all_gather(w_down, 'clip', axis=0, tiled=True)]
    transpose x7 -> x1, local copies, waits for them, and re-layouts: 193 us -> 1.49 us  [unswap_rows(): return both.transpose(2, 0, 3, 1, 4, 5).reshape(-1, depth)]
    another operation x28 -> x1, local copies, waits for them, and re-layouts: 153 us -> 0.01 us  [on_device(): mods = modulation[0].reshape(2, 6, width)]
    reduce_scatter x6 -> x0, waiting for transfers between devices: 105 us -> none  [the longest x1 65.9 us: on_device(): lax.psum_scatter(full_up.astype(jnp.bfloat16), 'clip', scatter_dimension=...]
    add x3 -> x0, local copies, waits for them, and re-layouts: 80 us -> none  [soft_scores(): scores = scores * score_scale + bias[None]]
  transfers between devices with their start and end apart: 14 -> 5, of which waited for: 7 -> 2; matrix products, arithmetic and copies ran while one was open for 58% -> 5% of each run, Pallas kernels for 0% -> 32%
where the time goes in v1:
time: 1030 us; the launch traced here: 1020 us
  Pallas kernels  821 us (80%)
  local copies, waits for them, and re-layouts  70.1 us (7%)
  blocking collectives  48.3 us (5%)
  waiting for transfers between devices  35.3 us (3%)
  other arithmetic  21.8 us (2%)
  between operations  16.2 us (2%)
    pallas_call x2, Pallas kernels, block_backward(): pl.pallas_call(body, grid=(end,), in_specs=[row_block(g_at), row_block(at...  350 us
    pallas_call x1, Pallas kernels, gather_all(): pl.pallas_call(functools.partial(gather_kernel, n, nz), out_shape=jax.Sha...  236 us
    pallas_call x2, Pallas kernels, mlp_forward(): pl.pallas_call(functools.partial(mlp_forward_body, n_steps), grid=(n_step...  90.1 us
    pallas_call x1, Pallas kernels, reduce_all(): pl.pallas_call(functools.partial(reduce_kernel, picks, nz), out_shape=jax...  54.1 us
    pallas_call x2, Pallas kernels, attention_forward(): pl.pallas_call(functools.partial(attend_forward, spatial, n_win, n_query,...  47.6 us
    psum x1, blocking collectives, on_device(): g_sp = lax.psum(gather_sp(gspread0), ('clip', 'frame'))  40 us
    unnamed x180, local copies, waits for them, and re-layouts  38.2 us
    pallas_call x2, Pallas kernels, qkv_forward(): pl.pallas_call(qkv_body, grid=(3 * per,), in_specs=[fixed((tokens, width)...  28 us
  transfers between devices with their start and end apart: 5, of which 2 were waited for; matrix products, arithmetic and copies ran while one was open for 5% of the time, Pallas kernels for 32%

profile of v1, /device:TPU:0, one launch (start us, length us, event | category | flops | bytes accessed | tf_op | source)
XLA Modules:
  0.0 1023.1 jit_solution(2168394158357713728)
XLA Ops:
  7.4 4.1 bitcast_convert_fusion.s_ref
  11.7 3.3 slice_reduce_fusion.2
  15.4 4.9 slice_reduce_fusion
  24.3 236.0 %gather_all.1 = bf16[24,4,2,2,64,1024]{5,4,3,2,1,0:T(8,128)(2,1)} custom-call(bf16[24,64,1024]{2,1,0:T(8,128)(2,1)} %copy-done.17), custom_call_target="tpu_custom_call" | custom-call | tf_op jit(solution)/shard_map/gather_all/pallas_call | solution.py:485
  262.6 14.0 %qkv_forward.2 = (bf16[1024,1024]{1,0:T(8,128)(2,1)S(1)}, bf16[1024,3072]{1,0:T(8,128)(2,1)}) custom-call(f32[1024,1024]{1,0:T(8,128)} %bitcast_convert_fusion.s_ref, f32[8,1024]{1,0:T(8,128)S(1)} %get-tuple-element.114.m_ref, bf16[24,1024,1024]{2,1,0:T(8,128)(2,1)} %bitcast.179), custom_call_target="tpu_custom_call" | custom-call | tf_op jit(solution)/shard_map/qkv_forward/pallas_call | solution.py:772
  278.0 15.4 %attend_forward.2 = (bf16[1024,1024]{1,0:T(8,128)(2,1)S(1)}, bf16[16,4,256,256]{3,2,1,0:T(8,128)(2,1)}) custom-call(bf16[1024,3072]{1,0:T(8,128)(2,1)} %get-tuple-element.41.q_ref.k_ref.v_ref, bf16[1024,3072]{1,0:T(8,128)(2,1)} %get-tuple-element.41.q_ref.k_ref.v_ref, bf16[1024,3072]{1,0:T(8,128)(2,1)} %get-tuple-element.41.q_ref.k_ref.v_ref, ...), custom_call_target="tpu_custom_call" | custom-call | tf_op jit(solution)/shard_map/attend_forward/pallas_call | solution.py:278
  294.7 7.5 proj_forward.2
  304.8 45.4 %mlp_forward.2 = (bf16[1024,4096]{1,0:T(8,128)(2,1)}, bf16[1024,4096]{1,0:T(8,128)(2,1)}, bf16[1024,1024]{1,0:T(8,128)(2,1)}, f32[1024,1024]{1,0:T(8,128)}) custom-call(bf16[1024,1024]{1,0:T(8,128)(2,1)} %copy-done.1, f32[1024,1024]{1,0:T(8,128)} %get-tuple-element.44.mid_ref, f32[8,1024]{1,0:T(8,128)} %copy-done.8, bf16[24,1024,1024]{2,1,0:T(8,128)(2,1)} %bitcast.181, ...), custom_call_target="tpu_custom_call" | custom-call | tf_op jit(solution)/shard_map/mlp_forward/pallas_call | solution.py:869
  350.2 2.9 fusion.13
  362.7 16.6 %collective-permute-done = bf16[4,8,2,8,1024]{4,3,1,0,2:T(8,128)(2,1)} collective-permute-done((bf16[4,8,2,8,1024]{4,3,1,0,2:T(8,128)(2,1)}, bf16[4,8,2,8,1024]{4,3,1,0,2:T(8,128)(2,1)}, u32[]{:S(2)}, u32[]{:S(2)}) %collective-permute-start) | collective-permute-done | bytes 1048608 | tf_op jit(solution)/shard_map/ppermute | solution.py:1219
  379.4 2.5 convert_select_fusion.3
  381.8 2.6 pad_maximum_fusion
  384.4 14.0 %qkv_forward.3 = (bf16[1024,1024]{1,0:T(8,128)(2,1)S(1)}, bf16[1024,3072]{1,0:T(8,128)(2,1)}) custom-call(f32[1024,1024]{1,0:T(8,128)} %bitcast.191, f32[8,1024]{1,0:T(8,128)S(1)} %get-tuple-element.113.m_ref.refs_5_, bf16[24,1024,1024]{2,1,0:T(8,128)(2,1)} %bitcast.183), custom_call_target="tpu_custom_call" | custom-call | tf_op jit(solution)/shard_map/qkv_forward/pallas_call | solution.py:772
  399.8 32.2 %attend_forward.3 = (bf16[1024,1024]{1,0:T(8,128)(2,1)S(1)}, bf16[16,2,512,384]{3,2,1,0:T(8,128)(2,1)}) custom-call(bf16[1024,3072]{1,0:T(8,128)(2,1)} %get-tuple-element.46.q_ref.k_ref.v_ref.refs_10_.refs_11_.refs_12_, bf16[1024,3072]{1,0:T(8,128)(2,1)} %get-tuple-element.46.q_ref.k_ref.v_ref.refs_10_.refs_11_.refs_12_, ...), custom_call_target="tpu_custom_call" | custom-call | tf_op jit(solution)/shard_map/attend_forward/pallas_call | solution.py:278
  433.3 7.4 proj_forward.3
  443.2 44.7 %mlp_forward.3 = (bf16[1024,4096]{1,0:T(8,128)(2,1)}, bf16[1024,4096]{1,0:T(8,128)(2,1)}, bf16[1024,1024]{1,0:T(8,128)(2,1)}, bf16[1024,1024]{1,0:T(8,128)(2,1)}) custom-call(bf16[1024,1024]{1,0:T(8,128)(2,1)} %copy-done.3, f32[1024,1024]{1,0:T(8,128)} %get-tuple-element.49.mid_ref.refs_2_, f32[8,1024]{1,0:T(8,128)} %copy-done.9, ...), custom_call_target="tpu_custom_call" | custom-call | tf_op jit(solution)/shard_map/mlp_forward/pallas_call | solution.py:869
  489.7 174.0 %block_backward.2 = (f32[1024,1024]{1,0:T(8,128)}, f32[16,15,8,128]{3,2,1,0:T(8,128)}, f32[8,1024]{1,0:T(8,128)}, bf16[12,4,2,2,64,1024]{5,4,3,2,1,0:T(8,128)(2,1)}, f32[8,64,1024]{2,1,0:T(8,128)}) custom-call(bf16[1024,1024]{1,0:T(8,128)(2,1)} %bitcast.195, bf16[1024,1024]{1,0:T(8,128)(2,1)} %get-tuple-element.51.refs_1_, ...), custom_call_target="tpu_custom_call" | custom-call | tf_op jit(solution)/shard_map/block_backward/pallas_call | solution.py:1152
  673.7 18.6 %collective-permute-done.3 = bf16[2,4,8,8,1024]{4,3,0,2,1:T(8,128)(2,1)S(1)} collective-permute-done((bf16[2,4,8,8,1024]{4,3,0,2,1:T(8,128)(2,1)S(1)}, bf16[2,4,8,8,1024]{4,3,0,2,1:T(8,128)(2,1)S(1)}, u32[]{:S(2)}, u32[]{:S(2)}) %collective-permute-start.3) | collective-permute-done | bytes 1048608 | tf_op jit(solution)/shard_map/ppermute | solution.py:1231
  692.4 2.2 fusion
  694.6 2.3 pad_maximum_fusion.1
  696.9 176.3 %block_backward.3 = (bf16[1024,1024]{1,0:T(8,128)(2,1)}, f32[16,4,16,128]{3,2,1,0:T(8,128)}, f32[8,1024]{1,0:T(8,128)}, bf16[12,4,2,2,64,1024]{5,4,3,2,1,0:T(8,128)(2,1)}, f32[12,64,1024]{2,1,0:T(8,128)}) custom-call(f32[1024,1024]{1,0:T(8,128)} %bitcast.194, bf16[1024,1024]{1,0:T(8,128)(2,1)} %get-tuple-element.58.down_ref, ...), custom_call_target="tpu_custom_call" | custom-call | tf_op jit(solution)/shard_map/block_backward/pallas_call | solution.py:1152
  876.3 54.1 %reduce_all.1 = f32[4,64,1024]{2,1,0:T(8,128)S(1)} custom-call(bf16[12,4,2,2,64,1024]{5,4,3,2,1,0:T(8,128)(2,1)} %get-tuple-element.69.refs_0_), custom_call_target="tpu_custom_call" | custom-call | tf_op jit(solution)/shard_map/reduce_all/pallas_call | solution.py:724
  934.6 2.4 pad_maximum_fusion.2
  940.1 8.3 psum.21
  949.1 3.8 copy.67
  953.0 4.3 reshape.241
  957.4 2.6 fusion.7
  961.8 2.7 copy.68
  964.5 4.5 reshape.242
  969.0 2.9 copy.122
  972.1 40.0 %psum.22 = f32[16,961]{1,0:T(8,128)} all-reduce(f32[16,961]{1,0:T(8,128)S(1)} %slice.84), channel_id=1, replica_groups=mesh['clip'=16,'frame'=2] {'clip','frame'}, use_global_device_ids=true, to_apply=%region_1.2 | all-reduce | flops 15376 | bytes 123008 | tf_op jit(solution)/shard_map/psum | solution.py:1299
  1012.1 3.3 copy.135
  (254 shorter events, 51.2 us)
Async XLA Ops:
  7.2 1004.9 %all-reduce.4.cloned.1.call-start = ((), (), s32[]{:S(2)}) async-start(), calls=%async_computation | async-start | bytes 442368 | tf_op jit(solution)/shard_map/psum | solution.py:1300
  7.2 253.3 %copy-start.62 = (s32[128]{0:T(128)}, s32[128]{0:T(128)S(1)}, u32[]{:S(2)}) copy-start(s32[128]{0:T(128)S(1)} %get-tuple-element.125) | copy-start | bytes 1540
  7.3 253.3 %copy-start.64 = (s32[128]{0:T(128)}, s32[128]{0:T(128)S(1)}, u32[]{:S(2)}) copy-start(s32[128]{0:T(128)S(1)} %get-tuple-element.130) | copy-start | bytes 1540
  7.3 253.2 %copy-start.46 = (s32[248]{0:T(256)}, s32[248]{0:T(256)S(1)}, u32[]{:S(2)}) copy-start(s32[248]{0:T(256)S(1)} %get-tuple-element.123) | copy-start | bytes 2980
  7.3 253.2 %copy-start.48 = (s32[248]{0:T(256)}, s32[248]{0:T(256)S(1)}, u32[]{:S(2)}) copy-start(s32[248]{0:T(256)S(1)} %get-tuple-element.124) | copy-start | bytes 2980
  7.3 253.2 %copy-start.50 = (s32[248]{0:T(256)}, s32[248]{0:T(256)S(1)}, u32[]{:S(2)}) copy-start(s32[248]{0:T(256)S(1)} %get-tuple-element.127) | copy-start | bytes 2980
  7.3 253.2 %copy-start.52 = (s32[248]{0:T(256)}, s32[248]{0:T(256)S(1)}, u32[]{:S(2)}) copy-start(s32[248]{0:T(256)S(1)} %get-tuple-element.128) | copy-start | bytes 2980
  7.4 253.2 %copy-start.73 = (pred[248]{0:T(512)(128)(4,1)}, pred[248]{0:T(512)(128)(4,1)S(1)}, u32[]{:S(2)}) copy-start(pred[248]{0:T(512)(128)(4,1)S(1)} %get-tuple-element.119) | copy-start | bytes 748
  7.4 253.2 %copy-start.75 = (pred[248]{0:T(512)(128)(4,1)}, pred[248]{0:T(512)(128)(4,1)S(1)}, u32[]{:S(2)}) copy-start(pred[248]{0:T(512)(128)(4,1)S(1)} %get-tuple-element.120) | copy-start | bytes 748
  7.4 253.2 %copy-start.66 = (pred[128]{0:T(512)(128)(4,1)}, pred[128]{0:T(512)(128)(4,1)S(1)}, u32[]{:S(2)}) copy-start(pred[128]{0:T(512)(128)(4,1)S(1)} %get-tuple-element.122) | copy-start | bytes 388
  11.7 283.0 %copy-start.8 = (f32[8,1024]{1,0:T(8,128)}, f32[8,1024]{1,0:T(8,128)S(1)}, u32[]{:S(2)}) copy-start(f32[8,1024]{1,0:T(8,128)S(1)} %get-tuple-element.114.m_ref) | copy-start | bytes 98308
  11.7 421.6 %copy-start.9 = (f32[8,1024]{1,0:T(8,128)}, f32[8,1024]{1,0:T(8,128)S(1)}, u32[]{:S(2)}) copy-start(f32[8,1024]{1,0:T(8,128)S(1)} %get-tuple-element.113.m_ref.refs_5_) | copy-start | bytes 98308
  15.0 5.3 copy-start.16
  24.3 236.0 %copy-start.25 = (f32[16,961]{1,0:T(8,128)S(1)}, f32[16,961]{1,0:T(8,128)}, u32[]{:S(2)}) copy-start(f32[16,961]{1,0:T(8,128)} %param.17) | copy-start | bytes 184516
  353.1 26.3 %collective-permute-start = (bf16[4,8,2,8,1024]{4,3,1,0,2:T(8,128)(2,1)}, bf16[4,8,2,8,1024]{4,3,1,0,2:T(8,128)(2,1)}, u32[]{:S(2)}, u32[]{:S(2)}) collective-permute-start(bf16[4,8,2,8,1024]{4,3,1,0,2:T(8,128)(2,1)} %fusion.13), channel_id=1, source_target_pairs={{0,1},{1,0},{2,3},{3,2},{4,5},{5,4},{6,7},{7,6},{8,9},{9,8},{10,11... | collective-permute-start | bytes 3145736 | tf_op jit(solution)/shard_map/ppermute | solution.py:1219
  354.9 133.0 %collective-permute-start.2 = (bf16[4,8,2,8,1024]{4,3,1,0,2:T(8,128)(2,1)}, bf16[4,8,2,8,1024]{4,3,1,0,2:T(8,128)(2,1)S(1)}, u32[]{:S(2)}, u32[]{:S(2)}) collective-permute-start(bf16[4,8,2,8,1024]{4,3,1,0,2:T(8,128)(2,1)} %bitcast.174), channel_id=1, source_target_pairs={{0,1},{1,0},{2,3},{3,2},{4,5},{5,4},{6,7},{7,6},{8,9},{9,8},{10,11... | collective-permute-start | bytes 3145736 | tf_op jit(solution)/shard_map/ppermute | solution.py:1219
  356.5 4.8 copy-start.77
  356.5 4.8 copy-start.79
  663.8 4.6 copy-start.21
  665.7 26.7 %collective-permute-start.3 = (bf16[2,4,8,8,1024]{4,3,0,2,1:T(8,128)(2,1)S(1)}, bf16[2,4,8,8,1024]{4,3,0,2,1:T(8,128)(2,1)S(1)}, u32[]{:S(2)}, u32[]{:S(2)}) collective-permute-start(bf16[2,4,8,8,1024]{4,3,0,2,1:T(8,128)(2,1)S(1)} %fusion.14), channel_id=1, source_target_pairs={{0,1},{1,0},{2,3},{3,2},{4,5},{5,4},{6,7},{7,6},{8,9},{9,8},{10,11... | collective-permute-start | bytes 3145736 | tf_op jit(solution)/shard_map/ppermute | solution.py:1231
  670.6 266.4 %collective-permute-start.1 = (bf16[2,4,8,8,1024]{4,3,0,2,1:T(8,128)(2,1)}, bf16[2,4,8,8,1024]{4,3,0,2,1:T(8,128)(2,1)}, u32[]{:S(2)}, u32[]{:S(2)}) collective-permute-start(bf16[2,4,8,8,1024]{4,3,0,2,1:T(8,128)(2,1)} %bitcast.175), channel_id=1, source_target_pairs={{0,1},{1,0},{2,3},{3,2},{4,5},{5,4},{6,7},{7,6},{8,9},{9,8},{10,11... | collective-permute-start | bytes 3145736 | tf_op jit(solution)/shard_map/ppermute | solution.py:1231
  952.9 4.4 copy-start.32
  952.9 4.4 copy-start.33
  952.9 4.4 copy-start.44
  952.9 4.4 copy-start.45
  952.9 4.4 copy-start.47
  952.9 4.4 copy-start.49
  952.9 4.4 copy-start.51
  953.0 4.4 copy-start.53
  953.0 4.4 copy-start.74
  953.0 4.4 copy-start.76
  964.5 4.5 copy-start.12
  (54 other events, 137.5 us)
Sparse Core Ops, SparseCore 0:
  673.8 122.4 all-reduce.3

commit v2 on v1

--- a/solution.py
+++ b/solution.py
@@ -264,39 +264,7 @@
 def attention_shapes(spatial, tokens):
     n_query = SWIN * SWIN if spatial else FRAMES * TWIN * TWIN
     n_key = n_query if spatial else KEYF * TWIN * TWIN
-    return tokens // n_query, n_query, n_key, 256
-
-
-def attention_forward(spatial, qkv, spread, key_ok):
-    tokens, width3 = qkv.shape
-    width = width3 // 3
-    pairs = width // 128
-    n_win, n_query, n_key, chunk = attention_shapes(spatial, tokens)
-    n_heads = 2 * pairs
-    tail = spread.shape[1:]
-    zeros = (0,) * len(tail)
-    return pl.pallas_call(
-        functools.partial(attend_forward, spatial, n_win, n_query, n_key, chunk),
-        grid=(pairs,),
-        in_specs=[
-            pl.BlockSpec((tokens, 128), lambda i: (0, i)),
-            pl.BlockSpec((tokens, 128), lambda i: (0, pairs + i)),
-            pl.BlockSpec((tokens, 128), lambda i: (0, 2 * pairs + i)),
-            pl.BlockSpec((2,) + tail, lambda i: (i,) + zeros),
-            pl.BlockSpec((n_win, 1, n_key), lambda i: (0, 0, 0)),
-        ],
-        out_specs=[
-            pl.BlockSpec((tokens, 128), lambda i: (0, i)),
-            pl.BlockSpec((2, n_win, n_query, n_key), lambda i: (i, 0, 0, 0)),
-        ],
-        out_shape=[
-            jax.ShapeDtypeStruct((tokens, width), BF16),
-            jax.ShapeDtypeStruct((n_heads, n_win, n_query, n_key), BF16),
-        ],
-        scratch_shapes=[pltpu.VMEM((2, n_query, n_key), F32)],
-        compiler_params=pltpu.CompilerParams(vmem_limit_bytes=48 * 1024 * 1024),
-        name="attend_forward",
-    )(qkv, qkv, qkv, spread, key_ok)
+    return tokens // n_query, n_query, n_key, n_query
 
 
 ROWS = 64
@@ -339,124 +307,114 @@
     pl.semaphore_wait(barrier, count)
 
 
-GATHER_HI = 640
+GATHER_TAIL = 6
 
 
 def gather_tick(t, n, nz, where, shard, full, local, up_s, up_r, dn_s, dn_r, y_s, y_r, x_s, x_r, c_s, c_r):
     clip, z, y, c, x = where
-    hi = GATHER_HI
-    lo = COLS - hi
-    fetch = pl.ds(pl.multiple_of(x * lo, 128), hi)
-    give = pl.ds(pl.multiple_of(x * hi, 128), lo)
     last = nz - 1
-
-    def own(i):
-        return pltpu.make_async_copy(
-            shard.at[i, :, fetch], full.at[i, z, y, c, :, fetch], local.at[i]
-        )
-
-    def up(i, s, origin):
-        src = shard.at[i, :, fetch] if s == 0 else full.at[i, origin, y, c, :, fetch]
-        return remote(src, full.at[i, origin, y, c, :, fetch], up_s.at[s, i], up_r.at[s, i], clip + 4, x)
-
-    def down(i, s, origin):
-        src = shard.at[i, :, fetch] if s == 0 else full.at[i, origin, y, c, :, fetch]
-        return remote(src, full.at[i, origin, y, c, :, fetch], dn_s.at[s, i], dn_r.at[s, i], clip - 4, x)
-
-    def over_y(i):
-        src = full.at[i, :, y, c, :, fetch]
-        return remote(src, src, y_s.at[i], y_r.at[i], clip + 2 - 4 * y, x)
-
-    def over_x(i):
-        src = full.at[i, :, :, c, :, give]
-        return remote(src, src, x_s.at[i], x_r.at[i], clip, 1 - x)
-
-    def over_c(i):
-        src = full.at[i, :, :, c]
-        return remote(src, src, c_s.at[i], c_r.at[i], clip + 1 - 2 * c, x)
-
-    def when_item(i):
-        return jnp.logical_and(i >= 0, i < n)
-
-    def z_wait(i, s):
-        @pl.when(z - 1 - s >= 0)
-        def _():
-            up(i, s, z - 1 - s).wait_recv()
-
-        @pl.when(z + 1 + s <= last)
-        def _():
-            down(i, s, z + 1 + s).wait_recv()
-
-    def z_start(i, s):
-        @pl.when(jnp.logical_and(z < last, z - s >= 0))
-        def _():
-            up(i, s, z - s).start()
-
-        @pl.when(jnp.logical_and(z > 0, z + s <= last))
-        def _():
-            down(i, s, z + s).start()
-
-    def z_sent(i, s):
-        @pl.when(jnp.logical_and(z < last, z - s >= 0))
-        def _():
-            up(i, s, z - s).wait_send()
-
-        @pl.when(jnp.logical_and(z > 0, z + s <= last))
-        def _():
-            down(i, s, z + s).wait_send()
-
     steps = nz - 1
-    i = t
-
-    @pl.when(when_item(i))
-    def _():
-        own(i).start()
-        z_start(i, 0)
-
-    for s in range(1, steps):
-        i = t - s
-
-        @pl.when(when_item(i))
-        def _(i=i, s=s):
-            z_wait(i, s - 1)
-            z_start(i, s)
-
-    i_y = t - steps
-
-    @pl.when(when_item(i_y))
-    def _():
-        z_wait(i_y, steps - 1)
-        own(i_y).wait()
-        over_y(i_y).start()
-
-    i_x = t - steps - 1
-
-    @pl.when(when_item(i_x))
-    def _():
-        over_y(i_x).wait_recv()
-        over_x(i_x).start()
-
-    i_c = t - steps - 2
-
-    @pl.when(when_item(i_c))
-    def _():
-        over_x(i_c).wait_recv()
-        over_c(i_c).start()
-
-    i_d = t - steps - 3
-
-    @pl.when(when_item(i_d))
-    def _():
-        over_c(i_d).wait_recv()
-        for s in range(steps):
-            z_sent(i_d, s)
-        over_y(i_d).wait_send()
-        over_x(i_d).wait_send()
-        over_c(i_d).wait_send()
-
-
-def gather_kernel(n, nz, shard, full, *sems):
-    where = place(4 * nz)
+
+    def phases(i, hi):
+        lo = COLS - hi
+        fetch = pl.ds(pl.multiple_of(x * lo, 128), hi)
+        give = pl.ds(pl.multiple_of(x * hi, 128), lo)
+
+        def own():
+            return pltpu.make_async_copy(
+                shard.at[i, :, fetch], full.at[i, z, y, c, :, fetch], local.at[i]
+            )
+
+        def up(s, origin):
+            src = shard.at[i, :, fetch] if s == 0 else full.at[i, origin, y, c, :, fetch]
+            return remote(src, full.at[i, origin, y, c, :, fetch], up_s.at[s, i], up_r.at[s, i], clip + 4, x)
+
+        def down(s, origin):
+            src = shard.at[i, :, fetch] if s == 0 else full.at[i, origin, y, c, :, fetch]
+            return remote(src, full.at[i, origin, y, c, :, fetch], dn_s.at[s, i], dn_r.at[s, i], clip - 4, x)
+
+        def over_y():
+            src = full.at[i, :, y, c, :, fetch]
+            return remote(src, src, y_s.at[i], y_r.at[i], clip + 2 - 4 * y, x)
+
+        def over_x():
+            src = full.at[i, :, :, c, :, give]
+            return remote(src, src, x_s.at[i], x_r.at[i], clip, 1 - x)
+
+        def over_c():
+            src = full.at[i, :, :, c]
+            return remote(src, src, c_s.at[i], c_r.at[i], clip + 1 - 2 * c, x)
+
+        def z_wait(s):
+            @pl.when(z - 1 - s >= 0)
+            def _():
+                up(s, z - 1 - s).wait_recv()
+
+            @pl.when(z + 1 + s <= last)
+            def _():
+                down(s, z + 1 + s).wait_recv()
+
+        def z_start(s):
+            @pl.when(jnp.logical_and(z < last, z - s >= 0))
+            def _():
+                up(s, z - s).start()
+
+            @pl.when(jnp.logical_and(z > 0, z + s <= last))
+            def _():
+                down(s, z + s).start()
+
+        def z_sent(s):
+            @pl.when(jnp.logical_and(z < last, z - s >= 0))
+            def _():
+                up(s, z - s).wait_send()
+
+            @pl.when(jnp.logical_and(z > 0, z + s <= last))
+            def _():
+                down(s, z + s).wait_send()
+
+        def first():
+            own().start()
+            z_start(0)
+
+        def along(s):
+            z_wait(s - 1)
+            z_start(s)
+
+        def to_y():
+            z_wait(steps - 1)
+            own().wait()
+            over_y().start()
+
+        def to_x():
+            over_y().wait_recv()
+            over_x().start()
+
+        def to_c():
+            over_x().wait_recv()
+            over_c().start()
+
+        def finish():
+            over_c().wait_recv()
+            for s in range(steps):
+                z_sent(s)
+            over_y().wait_send()
+            over_x().wait_send()
+            over_c().wait_send()
+
+        mids = [functools.partial(along, s) for s in range(1, steps)]
+        return [first] + mids + [to_y, to_x, to_c, finish]
+
+    for k in range(steps + 4):
+        i = t - k
+        valid = jnp.logical_and(i >= 0, i < n)
+        third = lax.rem(i + 3, 3) == 2
+        for hi, chosen in ((640, jnp.logical_not(third)), (768, third)):
+            @pl.when(jnp.logical_and(valid, chosen))
+            def _(i=i, hi=hi, k=k):
+                phases(i, hi)[k]()
+
+
+def greet_gather(nz, where):
     clip, z, y, c, x = where
     greet([
         (clip + 4, x, z < nz - 1),
@@ -466,12 +424,6 @@
         (clip + 1 - 2 * c, x, None),
     ])
 
-    def step(t, carry):
-        gather_tick(t, n, nz, where, shard, full, *sems)
-        return carry
-
-    lax.fori_loop(0, n + nz + 2, step, 0)
-
 
 def gather_sems(n, nz):
     dma = pltpu.SemaphoreType.DMA
@@ -480,21 +432,9 @@
     return [one, z, z, z, z, one, one, one, one, one, one]
 
 
-def gather_all(shard, nz, cid):
-    n = shard.shape[0]
-    return pl.pallas_call(
-        functools.partial(gather_kernel, n, nz),
-        out_shape=jax.ShapeDtypeStruct((n, nz, 2, 2, ROWS, COLS), BF16),
-        in_specs=[pl.BlockSpec(memory_space=pl.ANY)],
-        out_specs=pl.BlockSpec(memory_space=pl.ANY),
-        scratch_shapes=gather_sems(n, nz),
-        compiler_params=pltpu.CompilerParams(collective_id=cid, has_side_effects=True),
-        name="gather_all",
-    )(shard)
-
-
 NBUF = 3
 REDUCE_TAIL = 7
+Y_FIRST = 640
 NACC = 4
 
 
@@ -502,16 +442,13 @@
                 loc, c_s, c_r, ya_s, ya_r, xa_s, xa_r, yb_s, yb_r, xb_s, xb_r, z_s, z_r, f_s, f_r, o_s,
                 cred_c, cred_y, cred_x, cred_z, cred_f):
     clip, z, y, c, x = where
-    half = COLS // 2
-    quarter = COLS // 4
+    half = ROWS // 2
     peer_c = clip + 1 - 2 * c
     peer_y = clip + 2 - 4 * y
-
-    def lanes(base, which):
-        return pl.ds(pl.multiple_of(base + which * quarter, 128), quarter)
-
-    mine1, their1 = lanes(0, x), lanes(0, 1 - x)
-    mine2, their2 = lanes(half, x), lanes(half, 1 - x)
+    mine = pl.ds(pl.multiple_of(x * half, half), half)
+    theirs = pl.ds(pl.multiple_of((1 - x) * half, half), half)
+    left = pl.ds(0, Y_FIRST)
+    right = pl.ds(Y_FIRST, COLS - Y_FIRST)
 
     def slot(i):
         return lax.rem(i, NBUF)
@@ -527,16 +464,16 @@
         return remote(src, cbuf.at[slot(i)], c_s.at[slot(i)], c_r.at[slot(i)], peer_c, x)
 
     def over_ya(i):
-        return remote(acc.at[aslot(i), :, 1 - y, :, pl.ds(0, half)], ya.at[slot(i)], ya_s.at[slot(i)], ya_r.at[slot(i)], peer_y, x)
+        return remote(acc.at[aslot(i), :, 1 - y, :, left], ya.at[slot(i)], ya_s.at[slot(i)], ya_r.at[slot(i)], peer_y, x)
 
     def over_xa(i):
-        return remote(acc.at[aslot(i), :, :, :, their2], xa.at[slot(i)], xa_s.at[slot(i)], xa_r.at[slot(i)], clip, 1 - x)
+        return remote(acc.at[aslot(i), :, :, theirs, right], xa.at[slot(i)], xa_s.at[slot(i)], xa_r.at[slot(i)], clip, 1 - x)
 
     def over_xb(i):
-        return remote(acc.at[aslot(i), :, y, :, their1], xb.at[slot(i)], xb_s.at[slot(i)], xb_r.at[slot(i)], clip, 1 - x)
+        return remote(acc.at[aslot(i), :, y, theirs, left], xb.at[slot(i)], xb_s.at[slot(i)], xb_r.at[slot(i)], clip, 1 - x)
 
     def over_yb(i):
-        return remote(acc.at[aslot(i), :, 1 - y, :, mine2], yb.at[slot(i)], yb_s.at[slot(i)], yb_r.at[slot(i)], peer_y, x)
+        return remote(acc.at[aslot(i), :, 1 - y, mine, right], yb.at[slot(i)], yb_s.at[slot(i)], yb_r.at[slot(i)], peer_y, x)
 
     def over_z(i, k):
         to = lax.rem(z + k, nz)
@@ -611,8 +548,8 @@
         a, b = aslot(i), slot(i)
 
         def body(k, carry):
-            acc[a, k, y, :, pl.ds(0, half)] = acc[a, k, y, :, pl.ds(0, half)] + ya[b, k]
-            acc[a, k, :, :, mine2] = acc[a, k, :, :, mine2] + xa[b, k]
+            acc[a, k, y, :, left] = acc[a, k, y, :, left] + ya[b, k]
+            acc[a, k, :, mine, right] = acc[a, k, :, mine, right] + xa[b, k]
             return carry
 
         lax.fori_loop(0, nz, body, 0)
@@ -628,8 +565,8 @@
         a, b = aslot(i), slot(i)
 
         def body(k, carry):
-            tb[b, k, :, pl.ds(0, quarter)] = acc[a, k, y, :, mine1] + xb[b, k]
-            tb[b, k, :, pl.ds(quarter, quarter)] = acc[a, k, y, :, mine2] + yb[b, k]
+            tb[b, k, :, left] = acc[a, k, y, mine, left] + xb[b, k]
+            tb[b, k, :, right] = acc[a, k, y, mine, right] + yb[b, k]
             return carry
 
         lax.fori_loop(0, nz, body, 0)
@@ -662,10 +599,8 @@
     def _(i=i):
         over_f(i).wait()
         b = slot(i)
-        ob[b, :, mine1] = sb[b, :, pl.ds(0, quarter)].astype(F32)
-        ob[b, :, mine2] = sb[b, :, pl.ds(quarter, quarter)].astype(F32)
-        ob[b, :, their1] = fb[b, :, pl.ds(0, quarter)].astype(F32)
-        ob[b, :, their2] = fb[b, :, pl.ds(quarter, quarter)].astype(F32)
+        ob[b, mine, :] = sb[b].astype(F32)
+        ob[b, theirs, :] = fb[b].astype(F32)
         credit(cred_f, clip, 1 - x, i)
         write(i).start()
 
@@ -680,58 +615,109 @@
     ])
 
 
-def reduce_kernel(picks, nz, *refs):
-    n_in = len(picks)
-    sources = [(ref, skip, count) for ref, (skip, count) in zip(refs[:n_in], picks)]
-    out, rest = refs[n_in], refs[n_in + 1 :]
-    n = sum(count for _, count in picks)
+def exchange_tick(t, nz, where, small, totals, boxes, mod_box, sems):
+    clip, z, y, c, x = where
+    steps = [(clip, 1 - x), (clip + 1 - 2 * c, x), (clip + 2 - 4 * y, x)]
+    bit = 1
+    while bit < nz:
+        flip = lax.rem(z // bit, 2)
+        steps.append((clip + 4 * bit * (1 - 2 * flip), x))
+        bit *= 2
+
+    def copies(k):
+        to, frame = steps[k]
+        found = [
+            remote(boxes[j].at[k, 0], boxes[j].at[k, 1], sems.at[j, 0, k], sems.at[j, 1, k], to, frame)
+            for j in range(2)
+        ]
+        if k == 0:
+            found.append(remote(small[0], mod_box, sems.at[2, 0, 0], sems.at[2, 1, 0], to, frame))
+        return found
+
+    for k in range(len(steps)):
+        @pl.when(t == k + 1)
+        def _(k=k):
+            for copy in copies(k):
+                copy.wait()
+            for j in range(2):
+                totals[1 + j][...] = boxes[j][k, 0].astype(F32) + boxes[j][k, 1].astype(F32)
+            if k == 0:
+                totals[0][...] = small[0][...] + mod_box[...]
+
+        @pl.when(t == k)
+        def _(k=k):
+            for j in range(2):
+                source = small[1 + j] if k == 0 else totals[1 + j]
+                boxes[j][k, 0] = source[...].astype(BF16)
+            for copy in copies(k):
+                copy.start()
+
+
+def exchange_steps(nz):
+    return 3 + (nz - 1).bit_length()
+
+
+def reduce_kernel(pick, nz, grads, small0, small1, small2, out, total0, total1, total2, *rest):
+    n_comm = len(reduce_scratch(nz))
+    comm, (box0, box1, mod_box, sems) = rest[:n_comm], rest[n_comm:]
+    skip, n = pick
     where = place(4 * nz)
+    clip, z, y, c, x = where
     greet_reduce(nz, where)
 
     def step(t, carry):
-        reduce_tick(t, n, nz, where, sources, out, *rest)
+        exchange_tick(
+            t, nz, where, (small0, small1, small2), (total0, total1, total2), (box0, box1), mod_box, sems
+        )
+        reduce_tick(t, n, nz, where, [(grads, skip, n)], out, *comm)
         return carry
 
     lax.fori_loop(0, n + REDUCE_TAIL, step, 0)
 
 
 def reduce_scratch(nz):
-    half, quarter = COLS // 2, COLS // 4
+    half = ROWS // 2
+    rest = COLS - Y_FIRST
     dma = pltpu.SemaphoreType.DMA
     one = dma((NBUF,))
     regular = pltpu.SemaphoreType.REGULAR
     return [
         pltpu.VMEM((NACC, nz, 2, ROWS, COLS), BF16),
         pltpu.VMEM((NBUF, nz, 2, ROWS, COLS), BF16),
-        pltpu.VMEM((NBUF, nz, ROWS, half), BF16),
-        pltpu.VMEM((NBUF, nz, 2, ROWS, quarter), BF16),
-        pltpu.VMEM((NBUF, nz, ROWS, quarter), BF16),
-        pltpu.VMEM((NBUF, nz, ROWS, quarter), BF16),
-        pltpu.VMEM((NBUF, nz, ROWS, half), BF16),
-        pltpu.VMEM((NBUF, nz - 1, ROWS, half), BF16),
-        pltpu.VMEM((NBUF, ROWS, half), BF16),
-        pltpu.VMEM((NBUF, ROWS, half), BF16),
+        pltpu.VMEM((NBUF, nz, ROWS, Y_FIRST), BF16),
+        pltpu.VMEM((NBUF, nz, 2, half, rest), BF16),
+        pltpu.VMEM((NBUF, nz, half, rest), BF16),
+        pltpu.VMEM((NBUF, nz, half, Y_FIRST), BF16),
+        pltpu.VMEM((NBUF, nz, half, COLS), BF16),
+        pltpu.VMEM((NBUF, nz - 1, half, COLS), BF16),
+        pltpu.VMEM((NBUF, half, COLS), BF16),
+        pltpu.VMEM((NBUF, half, COLS), BF16),
         pltpu.VMEM((NBUF, ROWS, COLS), F32),
         one, one, one, one, one, one, one, one, one, one, one,
         dma((NBUF, nz - 1)), dma((NBUF, nz - 1)),
         one, one, one,
-        regular, regular, regular, pltpu.SemaphoreType.REGULAR((nz - 1,)), regular,
+        regular, regular, regular, regular((nz - 1,)), regular,
     ]
 
 
-def reduce_all(grads, picks, nz, cid):
-    n = sum(count for _, count in picks)
+def reduce_last(grads, pick, small, nz, cid):
+    n = pick[1]
+    steps = exchange_steps(nz)
+    vmem = pl.BlockSpec(memory_space=pltpu.VMEM)
     return pl.pallas_call(
-        functools.partial(reduce_kernel, picks, nz),
-        out_shape=jax.ShapeDtypeStruct((n, ROWS, COLS), F32),
-        in_specs=[pl.BlockSpec(memory_space=pl.ANY)] * len(grads),
-        out_specs=pl.BlockSpec(memory_space=pl.ANY),
-        scratch_shapes=reduce_scratch(nz),
+        functools.partial(reduce_kernel, pick, nz),
+        out_shape=[jax.ShapeDtypeStruct((n, ROWS, COLS), F32)]
+        + [jax.ShapeDtypeStruct(v.shape, F32) for v in small],
+        in_specs=[pl.BlockSpec(memory_space=pl.ANY), vmem, vmem, vmem],
+        out_specs=[pl.BlockSpec(memory_space=pl.ANY), vmem, vmem, vmem],
+        scratch_shapes=reduce_scratch(nz)
+        + [pltpu.VMEM((steps, 2) + v.shape, BF16) for v in small[1:]]
+        + [pltpu.VMEM(small[0].shape, F32), pltpu.SemaphoreType.DMA((3, 2, steps))],
         compiler_params=pltpu.CompilerParams(
             collective_id=cid, has_side_effects=True, vmem_limit_bytes=48 * 1024 * 1024
         ),
-        name="reduce_all",
-    )(*grads)
+        name="reduce_last",
+    )(grads, *small)
 
 
 CHUNK = 512
@@ -754,144 +740,301 @@
     lax.fori_loop(0, tokens // STEP_ROWS, step, 0)
 
 
-def qkv_body(s_ref, m_ref, w_ref, na_ref, q_ref):
-    @pl.when(pl.program_id(0) == 0)
-    def _():
-        def rows_of(rows):
-            normed, _ = norm_stats(s_ref[rows, :])
-            na_ref[rows, :] = (normed * (1.0 + m_ref[1:2, :]) + m_ref[0:1, :]).astype(BF16)
-
-        over_rows(s_ref.shape[0], rows_of)
-
-    q_ref[...] = dot_nn(na_ref[...], w_ref[0]).astype(BF16)
-
-
-def qkv_forward(stream, mods, weights, base):
+def down_rows(w_ref):
+    groups = w_ref.shape[1] // ROWS
+    return jnp.concatenate(
+        [w_ref[s, c * ROWS : (c + 1) * ROWS, :] for c in range(groups) for s in range(2)], axis=0
+    )
+
+
+FRONT_ROWS = 256
+GATHER_US = 8.5
+
+
+def forward_plan(tokens, width):
+    rows = tokens // FRONT_ROWS
+    sizes = (rows, 3, width // 128, 1, rows, 4, rows)
+    starts = [0]
+    for size in sizes:
+        starts.append(starts[-1] + size)
+    return starts
+
+
+def plan_gather(starts, spatial, need, n_items, nz):
+    takes = (1.0, 2.6, 1.9 if spatial else 3.6, 2.2, 1.3, 6.5, 0.8)
+    total = n_items + nz + 2
+    counts, done, clock, last = [], 0, 0.0, -GATHER_US
+    for section, (lo, hi) in enumerate(zip(starts, starts[1:])):
+        for step in range(lo, hi):
+            before = done
+            while done < total and (done < need.get(step, 0) or clock - last >= GATHER_US):
+                early = 4.0 if done < 7 else GATHER_US
+                clock = max(clock, last + early)
+                last = clock
+                done += 1
+            counts.append(done - before)
+            clock += takes[section]
+    return counts, total
+
+
+def forward_body(
+    spatial, shapes, n_own, own_first, counts, total, nz,
+    s_ref, m_ref, b_ref, ok_ref, shard_hbm, prev_hbm,
+    na_ref, qkv_ref, att_ref, p_ref, proj_ref, mid_ref, nm_ref, act_ref, dact_ref, down_ref, res_ref, full_hbm,
+    n_scr, q_scr, a_scr, acc_ref, mid_scr, bias_ref, w_scr, d_scr, w_sem, d_sem, *sems,
+):
+    n_win, n_query, n_key, chunk = shapes
+    tokens, width = acc_ref.shape
+    starts = forward_plan(tokens, width)
+    a0, a1, a2, a3, a4, a5, a6, end = starts
+    step = pl.program_id(0)
+    where = place(4 * nz)
+
+    @pl.when(step == 0)
+    def _():
+        greet_gather(nz, where)
+
+    lo = jnp.zeros((), jnp.int32)
+    hi = jnp.zeros((), jnp.int32)
+    for s, count in enumerate(counts):
+        if count:
+            lo = lo + count * (step > s).astype(jnp.int32)
+            hi = hi + count * (step >= s).astype(jnp.int32)
+
+    def tick(t, carry):
+        gather_tick(t, n_own, nz, where, shard_hbm, full_hbm, *sems)
+        return carry
+
+    lax.fori_loop(lo, hi, tick, 0)
+
+    def item_ref(item):
+        if item >= own_first:
+            return full_hbm.at[item - own_first]
+        return prev_hbm.at[PREV_ITEMS + item]
+
+    ready = []
+    done = 0
+    for count in counts:
+        done += count
+        ready.append(done)
+
+    def start_of(item, use):
+        if item < own_first:
+            return max(use - 1, 0)
+        for s in range(max(use - 1, 0), use + 1):
+            if ready[s] >= item - own_first + nz + 3:
+                return s
+        raise ValueError("late item")
+
+    jobs = []
+    uses = [(a1, 0), (a1 + 1, 1), (a1 + 2, 2), (a3, 3)] + [(a5 + i, UP_ITEMS[i]) for i in range(4)]
+    for k, (use, item) in enumerate(uses):
+        copy = pltpu.make_async_copy(item_ref(item), w_scr.at[k % 2], w_sem.at[k % 2])
+        jobs.append((start_of(item, use), use, copy))
+    for i in range(4):
+        items = (DOWN_ITEMS[2 * (i // 2)], DOWN_ITEMS[2 * (i // 2) + 1])
+        first = max(start_of(item, a5 + i) for item in items)
+        for k, item in enumerate(items):
+            source = item_ref(item).at[pl.ds((nz // 2) * (i % 2), nz // 2)]
+            copy = pltpu.make_async_copy(source, d_scr.at[i % 2, k], d_sem.at[i % 2, k])
+            jobs.append((first, a5 + i, copy))
+    for first, use, copy in jobs:
+        @pl.when(step == first)
+        def _(copy=copy):
+            copy.start()
+    for first, use, copy in jobs:
+        @pl.when(step == use)
+        def _(copy=copy):
+            copy.wait()
+
+    def weight(k):
+        return w_scr[k].reshape(width, width)
+
+    def rows_at(i):
+        return pl.ds(pl.multiple_of(i * FRONT_ROWS, FRONT_ROWS), FRONT_ROWS)
+
+    @pl.when(step < a1)
+    def _():
+        normed, _ = norm_stats(s_ref[...].astype(F32))
+        value = (normed * (1.0 + m_ref[1:2, :]) + m_ref[0:1, :]).astype(BF16)
+        n_scr[rows_at(step), :] = value
+        na_ref[...] = value
+
+    @pl.when(jnp.logical_and(step >= a1, step < a2))
+    def _():
+        i = step - a1
+        value = dot_nn(n_scr[...], weight(lax.rem(i, 2))).astype(BF16)
+        q_scr[:, pl.ds(pl.multiple_of(i * width, width), width)] = value
+        qkv_ref[...] = value
+
+    @pl.when(jnp.logical_and(step >= a2, step < a3))
+    def _():
+        def lanes(k):
+            return q_scr.at[:, pl.ds(pl.multiple_of(k * width + (step - a2) * 128, 128), 128)]
+
+        attend_forward(
+            spatial, n_win, n_query, n_key, chunk, lanes(0), lanes(1), lanes(2), b_ref, ok_ref, att_ref, p_ref, bias_ref
+        )
+        a_scr[:, pl.ds(pl.multiple_of((step - a2) * 128, 128), 128)] = att_ref[...]
+
+    @pl.when(step == a3)
+    def _():
+        acc_ref[...] = dot_nn(a_scr[...], weight(1))
+
+    @pl.when(jnp.logical_and(step >= a4, step < a5))
+    def _():
+        rows = rows_at(step - a4)
+        proj = acc_ref[rows, :]
+        proj_ref[...] = proj.astype(BF16)
+        mid = s_ref[...].astype(F32) + m_ref[2:3, :] * proj
+        mid_ref[...] = mid
+        mid_scr[rows, :] = mid
+        normed, _ = norm_stats(mid)
+        value = (normed * (1.0 + m_ref[4:5, :]) + m_ref[3:4, :]).astype(BF16)
+        n_scr[rows, :] = value
+        nm_ref[...] = value
+
+    @pl.when(jnp.logical_and(step >= a5, step < a6))
+    def _():
+        i = step - a5
+        slot = lax.rem(i, 2)
+        w_up = weight(slot)
+        first = d_scr[slot, 0].reshape(-1, ROWS, width)
+        second = d_scr[slot, 1].reshape(-1, ROWS, width)
+        w_down = jnp.concatenate(
+            [part for k in range(first.shape[0]) for part in (first[k], second[k])], axis=0
+        )
+        pieces = 4
+        each = tokens // pieces
+        ups = [dot_nn(n_scr[k * each : (k + 1) * each, :], w_up) for k in range(pieces)]
+        for k in range(pieces):
+            rows = slice(k * each, (k + 1) * each)
+            up = ups[k]
+            square = up * up
+            tanh = jnp.tanh(up * (GELU_C + (GELU_C * GELU_A) * square))
+            half = 0.5 + 0.5 * tanh
+            act = up * half
+            dact_ref[rows, :] = (
+                half + act * (1.0 - tanh) * (GELU_C + (3.0 * GELU_C * GELU_A) * square)
+            ).astype(BF16)
+            act = act.astype(BF16)
+            act_ref[rows, :] = act
+            acc_ref[rows, :] = jnp.where(i == 0, 0.0, acc_ref[rows, :]) + dot_nn(act, w_down)
+
+    @pl.when(step >= a6)
+    def _():
+        rows = rows_at(step - a6)
+        down = acc_ref[rows, :]
+        down_ref[...] = down.astype(BF16)
+        res_ref[...] = (mid_scr[rows, :] + m_ref[5:6, :] * down).astype(res_ref.dtype)
+
+    @pl.when(step == end - 1)
+    def _():
+        lax.fori_loop(sum(counts), total, tick, 0)
+
+
+DOWN_ITEMS = (4, 5, 8, 9)
+UP_ITEMS = (6, 7, 10, 11)
+PREV_ITEMS = 12
+
+
+def block_forward(stream, mods, shard, prev, own_first, spread, key_ok, spatial, result_type, nz, cid):
     tokens, width = stream.shape
-    per = width // CHUNK
-    return pl.pallas_call(
-        qkv_body,
-        grid=(3 * per,),
+    shapes = attention_shapes(spatial, tokens)
+    n_win, n_query, n_key, _ = shapes
+    pairs = width // 128
+    a0, a1, a2, a3, a4, a5, a6, end = starts = forward_plan(tokens, width)
+    n_own = shard.shape[0]
+    tail = spread.shape[1:]
+    zeros = (0,) * len(tail)
+    need = {}
+    for i in range(3):
+        need[a1 + i] = i
+    need[a3] = 3
+    for i in range(4):
+        need[a5 + i] = max(UP_ITEMS[i], DOWN_ITEMS[2 * (i // 2) + 1])
+    need = {s: item - own_first + nz + 3 for s, item in need.items() if item >= own_first}
+    counts, total = plan_gather(starts, spatial, need, n_own, nz)
+
+    def at(start, stop):
+        return lambda i: jnp.clip(i - start, 0, stop - start - 1)
+
+    def row_block(place_of):
+        return pl.BlockSpec((FRONT_ROWS, width), lambda i: (place_of(i), 0))
+
+    def s_at(i):
+        return jnp.where(i < a1, i, at(a4, a5)(i))
+
+    heads = at(a2, a3)
+    anywhere = pl.BlockSpec(memory_space=pl.ANY)
+    hidden = pl.BlockSpec((tokens, width), lambda i: (0, at(a5, a6)(i)))
+    body = functools.partial(forward_body, spatial, shapes, n_own, own_first, counts, total, nz)
+    extra = [] if prev is None else [prev]
+    if prev is None:
+        whole = body
+
+        def body(*refs):
+            return whole(*refs[:5], None, *refs[5:])
+
+    dma = pltpu.SemaphoreType.DMA
+    bf16_rows = jax.ShapeDtypeStruct((tokens, width), BF16)
+    outs = pl.pallas_call(
+        body,
+        grid=(end,),
         in_specs=[
-            fixed((tokens, width)),
+            row_block(s_at),
             fixed(mods.shape),
-            pl.BlockSpec((1, width, CHUNK), lambda i: (base + i // per, 0, i % per)),
-        ],
-        out_specs=[fixed((tokens, width)), pl.BlockSpec((tokens, CHUNK), lambda i: (0, i))],
-        out_shape=[
-            jax.ShapeDtypeStruct((tokens, width), BF16),
-            jax.ShapeDtypeStruct((tokens, 3 * width), BF16),
-        ],
-        compiler_params=pltpu.CompilerParams(vmem_limit_bytes=48 * MIB),
-        name="qkv_forward",
-    )(stream, mods, weights)
-
-
-def proj_body(att_ref, s_ref, m_ref, w_ref, proj_ref, mid_ref, nm_ref):
-    proj = dot_nn(att_ref[...], w_ref[0])
-    proj_ref[...] = proj.astype(BF16)
-    mid = s_ref[...] + m_ref[2:3, :] * proj
-    mid_ref[...] = mid
-    normed, _ = norm_stats(mid)
-    nm_ref[...] = (normed * (1.0 + m_ref[4:5, :]) + m_ref[3:4, :]).astype(BF16)
-
-
-def proj_forward(att, stream, mods, weights, base):
-    tokens, width = stream.shape
-    rows = 256
-    row = pl.BlockSpec((rows, width), lambda i: (i, 0))
-    return pl.pallas_call(
-        proj_body,
-        grid=(tokens // rows,),
-        in_specs=[row, row, fixed(mods.shape), pl.BlockSpec((1, width, width), lambda i: (base + 3, 0, 0))],
-        out_specs=[row, row, row],
-        out_shape=[
-            jax.ShapeDtypeStruct((tokens, width), BF16),
-            jax.ShapeDtypeStruct((tokens, width), F32),
-            jax.ShapeDtypeStruct((tokens, width), BF16),
-        ],
-        compiler_params=pltpu.CompilerParams(vmem_limit_bytes=48 * MIB),
-        name="proj_forward",
-    )(att, stream, mods, weights)
-
-
-def down_rows(w_ref):
-    return jnp.concatenate(
-        [w_ref[sub, c * 64 : (c + 1) * 64, :] for c in range(2) for sub in range(4)], axis=0
-    )
-
-
-def mlp_forward_body(n_steps, nm_ref, mid_ref, m_ref, up_ref, dn_ref, act_ref, dact_ref, down_ref, res_ref, acc_ref):
-    step = pl.program_id(0)
-    tokens = nm_ref.shape[0]
-    w_down = down_rows(dn_ref)
-    rows_each = 256
-
-    def part(k, carry):
-        rows = pl.ds(pl.multiple_of(k * rows_each, rows_each), rows_each)
-        up = dot_nn(nm_ref[rows, :], up_ref[0])
-        square = up * up
-        tanh = jnp.tanh(GELU_C * up * (1.0 + GELU_A * square))
-        half = 0.5 * (1.0 + tanh)
-        act = (up * half).astype(BF16)
-        slope = GELU_C * (1.0 + 3.0 * GELU_A * square)
-        act_ref[rows, :] = act
-        dact_ref[rows, :] = (half + 0.5 * up * (1.0 - tanh * tanh) * slope).astype(BF16)
-        down = dot_nn(act, w_down)
-
-        @pl.when(step == 0)
-        def _():
-            acc_ref[rows, :] = down
-
-        @pl.when(step > 0)
-        def _():
-            acc_ref[rows, :] += down
-
-        return carry
-
-    lax.fori_loop(0, tokens // rows_each, part, 0)
-
-    @pl.when(step == n_steps - 1)
-    def _():
-        def rows_of(rows):
-            down = acc_ref[rows, :]
-            down_ref[rows, :] = down.astype(BF16)
-            res_ref[rows, :] = (mid_ref[rows, :] + m_ref[5:6, :] * down).astype(res_ref.dtype)
-
-        over_rows(tokens, rows_of)
-
-
-def mlp_forward(normed_m, mid, mods, weights, base, result_type):
-    tokens, width = mid.shape
-    n_steps = 4 * width // CHUNK
-    per = width // CHUNK
-    hidden = 4 * width
-    return pl.pallas_call(
-        functools.partial(mlp_forward_body, n_steps),
-        grid=(n_steps,),
-        in_specs=[
-            fixed((tokens, width)),
-            fixed((tokens, width)),
-            fixed(mods.shape),
-            pl.BlockSpec((1, width, CHUNK), lambda i: (base + 4 + i // per, 0, i % per)),
-            pl.BlockSpec((4, 128, width), lambda i: (base // 4 + 2, i, 0)),
-        ],
+            pl.BlockSpec((2,) + tail, lambda i: (heads(i),) + zeros),
+            pl.BlockSpec((n_win, 1, n_key), lambda i: (0, 0, 0)),
+            anywhere,
+        ] + [anywhere] * len(extra),
         out_specs=[
-            pl.BlockSpec((tokens, CHUNK), lambda i: (0, i)),
-            pl.BlockSpec((tokens, CHUNK), lambda i: (0, i)),
-            fixed((tokens, width)),
-            fixed((tokens, width)),
+            row_block(at(a0, a1)),
+            pl.BlockSpec((tokens, width), lambda i: (0, at(a1, a2)(i))),
+            pl.BlockSpec((tokens, 128), lambda i: (0, heads(i))),
+            pl.BlockSpec((2, n_win, n_query, n_key), lambda i: (heads(i), 0, 0, 0)),
+            row_block(at(a4, a5)),
+            row_block(at(a4, a5)),
+            row_block(at(a4, a5)),
+            hidden,
+            hidden,
+            row_block(at(a6, end)),
+            row_block(at(a6, end)),
+            anywhere,
         ],
         out_shape=[
-            jax.ShapeDtypeStruct((tokens, hidden), BF16),
-            jax.ShapeDtypeStruct((tokens, hidden), BF16),
-            jax.ShapeDtypeStruct((tokens, width), BF16),
+            bf16_rows,
+            jax.ShapeDtypeStruct((tokens, 3 * width), BF16),
+            bf16_rows,
+            jax.ShapeDtypeStruct((2 * pairs, n_win, n_query, n_key), BF16),
+            bf16_rows,
+            jax.ShapeDtypeStruct((tokens, width), F32),
+            bf16_rows,
+            jax.ShapeDtypeStruct((tokens, 4 * width), BF16),
+            jax.ShapeDtypeStruct((tokens, 4 * width), BF16),
+            bf16_rows,
             jax.ShapeDtypeStruct((tokens, width), result_type),
+            jax.ShapeDtypeStruct((n_own, nz, 2, 2, ROWS, COLS), BF16),
         ],
-        scratch_shapes=[pltpu.VMEM((tokens, width), F32)],
-        compiler_params=pltpu.CompilerParams(vmem_limit_bytes=56 * MIB),
-        name="mlp_forward",
-    )(normed_m, mid, mods, weights, weights)
+        scratch_shapes=[
+            pltpu.VMEM((tokens, width), BF16),
+            pltpu.VMEM((tokens, 3 * width), BF16),
+            pltpu.VMEM((tokens, width), BF16),
+            pltpu.VMEM((tokens, width), F32),
+            pltpu.VMEM((tokens, width), F32),
+            pltpu.VMEM((2, n_query, n_key), F32),
+            pltpu.VMEM((2, nz, 2, 2, ROWS, COLS), BF16),
+            pltpu.VMEM((2, 2, nz // 2, 2, 2, ROWS, COLS), BF16),
+            dma((2,)),
+            dma((2, 2)),
+        ] + gather_sems(n_own, nz),
+        compiler_params=pltpu.CompilerParams(
+            collective_id=cid, has_side_effects=True, vmem_limit_bytes=64 * MIB
+        ),
+        name="block_forward",
+    )(stream, mods, spread, key_ok, shard, *extra)
+    normed_a, qkv, att, probs, proj, mid, normed_m, act, dact, down, result, full = outs
+    return result, (stream, normed_a, qkv, probs, att, proj, mid, normed_m, act, dact, down), full
 
 
 def norm_back_rows(values, scale_row, grad):
@@ -906,6 +1049,7 @@
 
 
 BLOCK_ROWS = 128
+TICK_US = 8.0
 
 
 def backward_plan(tokens, width):
@@ -922,7 +1066,7 @@
 
 def backward_body(
     spatial, shapes, n_prev, n_own, tick_steps, nz,
-    g_ref, down_ref, mid_ref, proj_ref, s_ref, m_ref, act_ref, dact_ref, w_ref, dn_ref,
+    g_ref, down_ref, mid_ref, proj_ref, s_ref, m_ref, act_ref, dact_ref, w_ref, up_ref, dn_ref,
     q_ref, k_ref, v_ref, p_ref, nm_hbm, att_hbm, na_hbm, prev_hbm,
     out_ref, dm_ref, rows_ref, grads_hbm, share_hbm,
     res_ref, gv_ref, e_ref, gm_ref, ga_ref, gq_ref, db_ref, gdb_ref, gub_ref,
@@ -959,7 +1103,7 @@
 
     def put_down(i):
         slot = lax.rem(i, 2)
-        target = grads_hbm.at[pl.ds(0, 4), i // 2, lax.rem(i, 2)]
+        target = grads_hbm.at[pl.ds(4 * (i // 4) + 2, 2), pl.ds(lax.rem(i, 4), 1)]
         return pltpu.make_async_copy(gdb_ref.at[slot], target, gd_sem.at[slot])
 
     def put_cols(i, item, half):
@@ -1017,14 +1161,12 @@
         gup = (grad_act * dact_ref[...].astype(F32)).astype(BF16)
         slot = lax.rem(i, 2)
         grad_down = dot_tn(act_ref[...], gdv).astype(BF16)
-        for c in range(2):
-            for sub in range(4):
-                first = (c * 4 + sub) * 64
-                gdb_ref[slot, sub, c] = grad_down[first : first + 64, :]
+        for k in range(CHUNK // ROWS):
+            gdb_ref[slot, k % 2, 0, k // 4, (k // 2) % 2] = grad_down[k * ROWS : (k + 1) * ROWS, :]
         put_down(i).start()
         keep_cols(i, dot_tn(res_ref[...], gup).astype(BF16))
-        put_cols(i, 4 + i // halves, lax.rem(i, halves)).start()
-        add_e(i == 0, gup, w_ref[0])
+        put_cols(i, 4 * (i // 4) + lax.rem(i // 2, 2), lax.rem(i, halves)).start()
+        add_e(i == 0, gup, up_ref[0])
 
     @pl.when(step == a2)
     def _():
@@ -1107,7 +1249,20 @@
         lax.fori_loop(len(tick_steps), n_items + REDUCE_TAIL, rest, 0)
 
 
-def block_backward(grad, saved, mods, weights, base, spread_shape, spatial, out_type, prev, n_own, tick_steps, nz, cid):
+def plan_ticks(starts, spatial, ready, spacing):
+    takes = (0.6, 5.0, 0.9, 2.5, 3.6 if spatial else 4.6, 3.0, 0.9)
+    steps, clock, last = [], 0.0, -spacing
+    for section, (lo, hi) in enumerate(zip(starts, starts[1:])):
+        for step in range(lo, hi):
+            clock += takes[section]
+            k = len(steps)
+            if (k >= len(ready) or step >= ready[k]) and clock - last >= spacing:
+                steps.append(step)
+                last = clock
+    return tuple(steps)
+
+
+def block_backward(grad, saved, mods, w_first, first_base, w_second, second_base, spread_shape, spatial, out_type, prev, n_own, nz, cid):
     stream, normed_a, qkv, probs, att, proj, mid, normed_m, act, dact, down = saved
     tokens, width = mid.shape
     shapes = attention_shapes(spatial, tokens)
@@ -1119,7 +1274,7 @@
     zeros = (0,) * len(tail)
 
     def at(start, stop):
-        return lambda i: jnp.clip(i - start, 0, stop - start - 1)
+        return lambda i: jnp.clip(i - start, 0, max(stop - start - 1, 0))
 
     def row_block(place_of):
         return pl.BlockSpec((BLOCK_ROWS, width), lambda i: (place_of(i), 0))
@@ -1127,26 +1282,36 @@
     def g_at(i):
         return jnp.where(i < a1, i, at(a2, a3)(i))
 
-    def weight_at(i):
-        up = at(a1, a2)(i)
-        proj_half = at(a3, a4)(i)
+    def first_at(i):
         third = at(a5, a6)(i)
-        item = jnp.where(i < a3, 4 + up // halves, jnp.where(i < a5, 3, third // halves))
-        half = jnp.where(i < a3, up % halves, jnp.where(i < a5, proj_half, third % halves))
-        return (base + item, 0, half)
+        item = jnp.where(i < a5, 3, third // halves)
+        half = jnp.where(i < a5, at(a3, a4)(i), third % halves)
+        return (first_base + item, 0, half)
+
+    def up_at(i):
+        k = at(a1, a2)(i)
+        return (second_base + 2 + 4 * (k // 4) + (k // 2) % 2, 0, k % 2)
+
+    def down_at(i):
+        k = at(a1, a2)(i)
+        return (second_base // 2 + 2 * (k // 4), k % 4, 0)
 
     heads = at(a4, a5)
     hidden = pl.BlockSpec((tokens, CHUNK), lambda i: (0, at(a1, a2)(i)))
     anywhere = pl.BlockSpec(memory_space=pl.ANY)
     n_prev = 0 if prev is None else 4
     n_items = n_prev + n_own
+    ready = [0] * n_prev
+    for done in (2, 4, 4, 4, 6, 8, 8, 8)[:n_own]:
+        ready.append(min(a1 + done + 1, a2))
+    tick_steps = plan_ticks((a0, a1, a2, a3, a4, a5, a6, end), spatial, ready, TICK_US)
     extra = [] if prev is None else [prev]
     body = functools.partial(backward_body, spatial, shapes, n_prev, n_own, tick_steps, nz)
     if prev is None:
         whole = body
 
         def body(*refs):
-            return whole(*refs[:17], None, *refs[17:])
+            return whole(*refs[:18], None, *refs[18:])
 
     dma = pltpu.SemaphoreType.DMA
     return pl.pallas_call(
@@ -1161,8 +1326,9 @@
             fixed(mods.shape),
             hidden,
             hidden,
-            pl.BlockSpec((1, width, CHUNK), weight_at),
-            pl.BlockSpec((4, 128, width), lambda i: (base // 4 + 2, at(a1, a2)(i), 0)),
+            pl.BlockSpec((1, width, CHUNK), first_at),
+            pl.BlockSpec((1, width, CHUNK), up_at),
+            pl.BlockSpec((2, CHUNK // 2, width), down_at),
             pl.BlockSpec((tokens, 128), lambda i: (0, heads(i))),
             pl.BlockSpec((tokens, 128), lambda i: (0, pairs + heads(i))),
             pl.BlockSpec((tokens, 128), lambda i: (0, 2 * pairs + heads(i))),
@@ -1191,7 +1357,7 @@
             pltpu.VMEM((tokens, width), BF16),
             pltpu.VMEM((tokens, 3 * width), BF16),
             pltpu.VMEM((2, n_query, n_key), F32),
-            pltpu.VMEM((2, 4, 2, ROWS, COLS), BF16),
+            pltpu.VMEM((2, 2, 1, 2, 2, ROWS, COLS), BF16),
             pltpu.VMEM((2, nz, 2, 2, ROWS, CHUNK), BF16),
             dma,
             dma((2,)),
@@ -1201,16 +1367,8 @@
             collective_id=cid, has_side_effects=True, vmem_limit_bytes=64 * MIB
         ),
         name="block_backward",
-    )(grad, down, mid, proj, stream, mods, act, dact, weights, weights, qkv, qkv, qkv, probs,
+    )(grad, down, mid, proj, stream, mods, act, dact, w_first, w_second, w_second, qkv, qkv, qkv, probs,
       normed_m, att, normed_a, *extra)
-
-
-def block_forward(stream, mods, weights, base, spread, key_ok, spatial, result_type):
-    normed_a, qkv = qkv_forward(stream, mods, weights, base)
-    att, probs = attention_forward(spatial, qkv, spread, key_ok)
-    proj, mid, normed_m = proj_forward(att, stream, mods, weights, base)
-    act, dact, down, result = mlp_forward(normed_m, mid, mods, weights, base, result_type)
-    return result, (stream, normed_a, qkv, probs, att, proj, mid, normed_m, act, dact, down)
 
 
 def swap_rows(values, me, swap):
@@ -1238,9 +1396,12 @@
 def pack_shards(shards, b):
     w_qkv, w_proj, w_up, w_down = [w[:, b] for w in shards]
     parts = []
-    for w in (w_qkv, w_proj, w_up):
+    for w in (w_qkv, w_proj):
         parts.append(w.reshape(ROWS, -1, COLS).transpose(1, 0, 2))
-    parts.append(w_down.reshape(-1, ROWS, COLS))
+    parts.append(w_up.reshape(ROWS, 2, 8, 2, 128).transpose(3, 1, 0, 2, 4).reshape(4, ROWS, COLS))
+    downs = w_down.reshape(-1, ROWS, COLS)
+    ups = parts.pop()
+    parts += [downs[0:2], ups[0:2], downs[2:4], ups[2:4]]
     return jnp.concatenate(parts, axis=0)
 
 
@@ -1254,8 +1415,8 @@
     nz = lax.axis_size("clip") // 4
     natural = (f_l, 2, TWIN, n_cw, TWIN, width)
     shards = (w_qkv, w_proj, w_up, w_down)
-    packed = jnp.concatenate([pack_shards(shards, b) for b in range(2)], axis=0)
-    full = gather_all(packed, nz, 1).reshape(24, 16 * ROWS, COLS)
+    packed = [pack_shards(shards, b) for b in range(2)]
+    early = jnp.concatenate([packed[0], packed[1][:4]], axis=0)
     limit = n_cols - 3 * (2 - size_group[0])
     wide = (jnp.arange(n_cols, dtype=jnp.int32) < limit).astype(F32)
     ok_sp = jnp.broadcast_to(wide[None, None, None, :], (f_l, 1, n_rows, n_cols))
@@ -1269,35 +1430,55 @@
     mods = jnp.pad(mods, ((0, 0), (0, 2), (0, 0)))
     cot = swap_rows(cotangent.reshape(natural), me, swap)
     stream0 = frames_in.reshape(-1, width).astype(F32)
-    mid_stream, saved0 = block_forward(stream0, mods[0], full, 0, spread0, ok_sp, True, F32)
+    mid_stream, saved0, full0 = block_forward(
+        stream0, mods[0], early, None, 0, spread0, ok_sp, True, F32, nz, 1
+    )
     stream1 = swap_rows(mid_stream.reshape(natural), me, swap)
-    end_stream, saved1 = block_forward(stream1, mods[1], full, 12, spread1, ok_st, False, BF16)
+    end_stream, saved1, full1 = block_forward(
+        stream1, mods[1], packed[1][4:], full0, 4, spread1, ok_st, False, BF16, nz, 5
+    )
+    full0 = full0.reshape(-1, width, width)
+    full1 = full1.reshape(-1, width, width)
     mixed = unswap_rows(end_stream, me, swap, n_cw, f_l).reshape(frames_in.shape)
-    starts = backward_plan(stream0.shape[0], width)
-    ticks1 = tuple(range(starts[2], starts[6] + 4, 2))
     grad1, gspread1, rows1, gw1, shares1 = block_backward(
-        cot, saved1, mods[1], full, 12, spread1.shape, False, F32, None, 8, ticks1, nz, 2
+        cot, saved1, mods[1], full0, 12, full1, 0, spread1.shape, False, F32, None, 8, nz, 2
     )
     grad_mid = unswap_rows(grad1, me, swap, n_cw, f_l)
-    ticks0 = (0,) + tuple(range(starts[1], starts[2], 3)) + tuple(range(starts[2], starts[6] + 4, 2))
     grad0, gspread0, rows0, gw0, shares0 = block_backward(
-        grad_mid, saved0, mods[0], full, 0, spread0.shape, True, BF16, gw1, 8, ticks0, nz, 3
-    )
-    last = reduce_all([gw0], [(8, 4)], nz, 4)
-    shares = jnp.stack([
-        jnp.concatenate([shares0[4:12], last], axis=0),
-        jnp.concatenate([shares1, shares0[0:4]], axis=0),
-    ])
-
-    def columns(lo, hi):
-        part = shares[:, lo:hi]
-        return part.transpose(2, 0, 1, 3).reshape(ROWS, 2, (hi - lo) * COLS)
-
-    g_down = shares[:, 0:4].reshape(2, 4 * ROWS, COLS).transpose(1, 0, 2)
-    outs = (columns(9, 12), columns(8, 9), columns(4, 8), g_down)
-    mod_grad = lax.psum(jnp.concatenate([rows0[:6], rows1[:6]], axis=0), "frame")[None]
-    g_sp = lax.psum(gather_sp(gspread0), ("clip", "frame"))
-    g_st = lax.psum(gather_st(gspread1), ("clip", "frame"))
+        grad_mid, saved0, mods[0], full0, 0, full0, 4, spread0.shape, True, BF16, gw1, 8, nz, 3
+    )
+    def wide_pad(table):
+        return jnp.pad(table, ((0, 0), (0, -table.shape[1] % 128)))
+
+    small = (
+        jnp.pad(jnp.concatenate([rows0[:6], rows1[:6]], axis=0), ((0, 4), (0, 0))),
+        wide_pad(gather_sp(gspread0)),
+        wide_pad(gather_st(gspread1)),
+    )
+    last, mods_sum, sp_sum, st_sum = reduce_last(gw0, (8, 4), small, nz, 4)
+    def pair(first, second):
+        return jnp.stack([first, second], axis=1)
+
+    def qkv_of(items):
+        return jnp.concatenate([items[0], items[1], items[2]], axis=-1)
+
+    def up_of(items):
+        parts = jnp.stack([items[0], items[1], items[4], items[5]]).reshape(2, 2, ROWS, 8, 128)
+        return parts.transpose(2, 1, 3, 0, 4).reshape(ROWS, 4 * COLS)
+
+    def down_of(items):
+        return jnp.concatenate([items[2], items[3], items[6], items[7]], axis=0)
+
+    own0 = shares0[4:]
+    outs = (
+        pair(qkv_of(last[1:]), qkv_of(shares0[1:4])),
+        pair(last[0], shares0[0]),
+        pair(up_of(own0), up_of(shares1)),
+        pair(down_of(own0), down_of(shares1)),
+    )
+    mod_grad = mods_sum[:12][None]
+    g_sp = sp_sum[:, : table_sp.shape[1]]
+    g_st = st_sum[:, : table_st.shape[1]]
     grad_in = grad0.reshape(frames_in.shape)
     return (mixed, grad_in, mod_grad, outs[0], outs[1], outs[2], outs[3], g_sp, g_st)
 

time: 1030 us -> 822 us (0.80)
  Pallas kernels: 821 us -> 691 us
  blocking collectives: 48.3 us -> 0 us
  waiting for transfers between devices: 35.3 us -> 20.9 us
  between operations: 16.2 us -> 3.01 us
    pallas_call x10 -> x3, Pallas kernels: 471 us -> 377 us  [the longest x2 317 us: block_forward(): pl.pallas_call(body, grid=(end,), in_specs=[row_block(s_at), fixed(mods.s...]
    psum x2 -> x0, blocking collectives: 48.3 us -> none  [the longest x1 40 us: on_device(): g_sp = lax.psum(gather_sp(gspread0), ('clip', 'frame'))]
    pallas_call x2, Pallas kernels: 350 us -> 314 us  [block_backward(): pl.pallas_call(body, grid=(end,), in_specs=[row_block(g_at), row_block(at...]
    unnamed x180 -> x187, local copies, waits for them, and re-layouts: 38.2 us -> 19.5 us
  transfers between devices with their start and end apart: 5 -> 4, of which waited for: 2 -> 2; matrix products, arithmetic and copies ran while one was open for 5% -> 5% of each run, Pallas kernels for 32% -> 55%
where the time goes in v2:
time: 822 us; the launch traced here: 816 us
  Pallas kernels  691 us (84%)
  local copies, waits for them, and re-layouts  64.9 us (8%)
  other arithmetic  26.6 us (3%)
  waiting for transfers between devices  20.9 us (3%)
    pallas_call x2, Pallas kernels, block_forward(): pl.pallas_call(body, grid=(end,), in_specs=[row_block(s_at), fixed(mods.s...  317 us
    pallas_call x2, Pallas kernels, block_backward(): pl.pallas_call(body, grid=(end,), in_specs=[row_block(g_at), row_block(at...  314 us
    pallas_call x1, Pallas kernels, reduce_last(): pl.pallas_call(functools.partial(reduce_kernel, pick, nz), out_shape=[jax...  59.8 us
    unnamed x187, local copies, waits for them, and re-layouts  19.5 us
  transfers between devices with their start and end apart: 4, of which 2 were waited for; matrix products, arithmetic and copies ran while one was open for 5% of the time, Pallas kernels for 55%

profile of v2, /device:TPU:0, one launch (start us, length us, event | category | flops | bytes accessed | tf_op | source)
XLA Modules:
  0.0 815.6 jit_solution(10608965489842606736)
XLA Ops:
  1.9 4.2 bitcast_convert_fusion.refs_0_.s_ref
  9.9 3.3 slice_reduce_fusion.2
  14.4 2.5 fusion.64
  16.9 5.6 slice_reduce_fusion
  22.9 2.8 slice_reduce_fusion.6
  31.7 180.9 %block_forward.2 = (bf16[1024,1024]{1,0:T(8,128)(2,1)}, bf16[1024,3072]{1,0:T(8,128)(2,1)}, bf16[1024,1024]{1,0:T(8,128)(2,1)}, bf16[16,4,256,256]{3,2,1,0:T(8,1...) custom-call(f32[1024,1024]{1,0:T(8,128)} %bitcast_convert_fusion.ref, ...), custom_call_target="tpu_custom_call" | custom-call | tf_op jit(solution)/shard_map/block_forward/pallas_call | solution.py:981
  212.5 1.9 fusion.9
  221.3 2.7 slice_reduce_fusion.5
  224.2 1.7 convolution_bitcast_fusion
  226.1 2.4 copy.91
  233.3 7.4 collective-permute-done
  240.6 2.5 convert_select_fusion.3
  243.1 2.6 pad_maximum_fusion
  245.7 136.1 %block_forward.3 = (bf16[1024,1024]{1,0:T(8,128)(2,1)}, bf16[1024,3072]{1,0:T(8,128)(2,1)}, bf16[1024,1024]{1,0:T(8,128)(2,1)}, bf16[16,2,512,384]{3,2,1,0:T(8,1...) custom-call(f32[1024,1024]{1,0:T(8,128)} %bitcast.229, ...), custom_call_target="tpu_custom_call" | custom-call | tf_op jit(solution)/shard_map/block_forward/pallas_call | solution.py:981
  381.8 2.7 constant_dynamic-slice_fusion.5
  386.1 1.4 bitcast_select_fusion.1
  387.4 1.5 pad_maximum_fusion.2
  388.9 148.0 %block_backward.2 = (f32[1024,1024]{1,0:T(8,128)}, f32[16,15,8,128]{3,2,1,0:T(8,128)}, f32[8,1024]{1,0:T(8,128)}, bf16[12,4,2,2,64,1024]{5,4,3,2,1,0:T(8,128)(2,1)}, f32[8,64,1024]{2,1,0:T(8,128)}) custom-call(bf16[1024,1024]{1,0:T(8,128)(2,1)} %bitcast.232, bf16[1024,1024]{1,0:T(8,128)(2,1)} %get-tuple-element.50.refs_1_, ...), custom_call_target="tpu_custom_call" | custom-call | tf_op jit(solution)/shard_map/block_backward/pallas_call | solution.py:1317
  537.1 1.8 fusion.10
  540.3 1.6 fusion.41
  544.1 1.8 copy.67
  547.1 13.6 %collective-permute-done.3 = bf16[2,4,8,8,1024]{4,3,0,2,1:T(8,128)(2,1)} collective-permute-done((bf16[2,4,8,8,1024]{4,3,0,2,1:T(8,128)(2,1)S(1)}, bf16[2,4,8,8,1024]{4,3,0,2,1:T(8,128)(2,1)}, u32[]{:S(2)}, u32[]{:S(2)}) %collective-permute-start.3) | collective-permute-done | bytes 1048608 | tf_op jit(solution)/shard_map/ppermute | solution.py:1389
  560.6 2.0 fusion
  562.6 2.6 pad_maximum_fusion.1
  565.2 166.2 %block_backward.3 = (bf16[1024,1024]{1,0:T(8,128)(2,1)}, f32[16,4,16,128]{3,2,1,0:T(8,128)}, f32[8,1024]{1,0:T(8,128)}, bf16[12,4,2,2,64,1024]{5,4,3,2,1,0:T(8,128)(2,1)}, f32[12,64,1024]{2,1,0:T(8,128)}) custom-call(f32[1024,1024]{1,0:T(8,128)} %bitcast.231, bf16[1024,1024]{1,0:T(8,128)(2,1)} %get-tuple-element.62.down_ref, ...), custom_call_target="tpu_custom_call" | custom-call | tf_op jit(solution)/shard_map/block_backward/pallas_call | solution.py:1317
  732.6 1.7 slice_bitcast_fusion.7
  736.2 1.5 copy.59
  737.8 1.4 fusion.5
  740.2 59.8 %reduce_last.1 = (f32[4,64,1024]{2,1,0:T(8,128)S(1)}, f32[16,1024]{1,0:T(8,128)S(1)}, f32[16,1024]{1,0:T(8,128)S(1)}, f32[16,3456]{1,0:T(8,128)S(1)}) custom-call(bf16[12,4,2,2,64,1024]{5,4,3,2,1,0:T(8,128)(2,1)} %get-tuple-element.74.grads, f32[16,1024]{1,0:T(8,128)S(1)} %select_maximum_fusion.small0, f32[16,1024]{1,0:T(8,128)S(1)} %pad.23.small1, ...), custom_call_target="tpu_custom_call" | custom-call | tf_op jit(solution)/shard_map/reduce_last/pallas_call | solution.py:707
  801.0 2.4 copy.69
  806.4 2.9 copy.71
  809.3 3.4 pad_maximum_fusion.3
  (272 shorter events, 40.0 us)
Async XLA Ops:
  0.7 6.4 copy-start.55
  0.7 6.4 copy-start.61
  0.7 6.3 copy-start.53
  0.7 6.3 copy-start.57
  0.7 6.3 copy-start.59
  0.7 6.3 copy-start.37
  0.7 6.3 copy-start.39
  0.8 6.3 copy-start.41
  0.8 6.3 copy-start.43
  0.8 6.3 copy-start.75
  0.8 6.3 copy-start.77
  1.3 5.8 copy-start.63
  1.9 5.3 copy-start.65
  1.9 4.9 copy-start.17
  8.2 5.8 copy-start.15
  9.9 4.4 copy-start.4
  214.5 26.2 %collective-permute-start = (bf16[4,8,2,8,1024]{4,3,1,0,2:T(8,128)(2,1)S(1)}, bf16[4,8,2,8,1024]{4,3,1,0,2:T(8,128)(2,1)}, u32[]{:S(2)}, u32[]{:S(2)}) collective-permute-start(bf16[4,8,2,8,1024]{4,3,1,0,2:T(8,128)(2,1)S(1)} %fusion.9), channel_id=1, source_target_pairs={{0,1},{1,0},{2,3},{3,2},{4,5},{5,4},{6,7},{7,6},{8,9},{9,8},{10,11... | collective-permute-start | bytes 3145736 | tf_op jit(solution)/shard_map/ppermute | solution.py:1377
  217.8 167.8 %collective-permute-start.2 = (bf16[4,8,2,8,1024]{4,3,1,0,2:T(8,128)(2,1)}, bf16[4,8,2,8,1024]{4,3,1,0,2:T(8,128)(2,1)}, u32[]{:S(2)}, u32[]{:S(2)}) collective-permute-start(bf16[4,8,2,8,1024]{4,3,1,0,2:T(8,128)(2,1)} %bitcast.215), channel_id=1, source_target_pairs={{0,1},{1,0},{2,3},{3,2},{4,5},{5,4},{6,7},{7,6},{8,9},{9,8},{10,11... | collective-permute-start | bytes 3145736 | tf_op jit(solution)/shard_map/ppermute | solution.py:1377
  218.8 7.1 copy-start.45
  218.8 7.1 copy-start.47
  218.9 7.1 copy-start.49
  218.9 7.1 copy-start.51
  218.9 7.1 copy-start.79
  218.9 7.1 copy-start.81
  220.8 5.2 copy-start.25
  220.9 5.1 copy-start.69
  220.9 5.1 copy-start.71
  224.1 4.4 copy-start.27
  224.1 4.4 copy-start.29
  385.5 348.8 %collective-permute-start.1 = (bf16[2,4,8,8,1024]{4,3,0,2,1:T(8,128)(2,1)}, bf16[2,4,8,8,1024]{4,3,0,2,1:T(8,128)(2,1)}, u32[]{:S(2)}, u32[]{:S(2)}) collective-permute-start(bf16[2,4,8,8,1024]{4,3,0,2,1:T(8,128)(2,1)} %bitcast.216), channel_id=1, source_target_pairs={{0,1},{1,0},{2,3},{3,2},{4,5},{5,4},{6,7},{7,6},{8,9},{9,8},{10,11... | collective-permute-start | bytes 3145736 | tf_op jit(solution)/shard_map/ppermute | solution.py:1389
  538.9 21.7 %collective-permute-start.3 = (bf16[2,4,8,8,1024]{4,3,0,2,1:T(8,128)(2,1)S(1)}, bf16[2,4,8,8,1024]{4,3,0,2,1:T(8,128)(2,1)}, u32[]{:S(2)}, u32[]{:S(2)}) collective-permute-start(bf16[2,4,8,8,1024]{4,3,0,2,1:T(8,128)(2,1)S(1)} %fusion.10), channel_id=1, source_target_pairs={{0,1},{1,0},{2,3},{3,2},{4,5},{5,4},{6,7},{7,6},{8,9},{9,8},{10,11... | collective-permute-start | bytes 3145736 | tf_op jit(solution)/shard_map/ppermute | solution.py:1389
  545.9 14.7 %copy-start.8 = (f32[1024,1024]{1,0:T(8,128)S(1)}, f32[1024,1024]{1,0:T(8,128)}, u32[]{:S(2)}) copy-start(f32[1024,1024]{1,0:T(8,128)} %get-tuple-element.61) | copy-start | bytes 12582916
  (55 other events, 146.7 us)

commit v3 on v2

--- a/solution.py
+++ b/solution.py
@@ -2,6 +2,7 @@
 
 import jax
 import jax.numpy as jnp
+import numpy as np
 from jax import lax
 from jax.experimental import pallas as pl
 from jax.experimental.pallas import tpu as pltpu
@@ -42,23 +43,16 @@
 
 def pick_sp():
     span = 2 * SWIN - 1
-    shape = (8 * span, SWIN, 128)
-    source = lax.broadcasted_iota(jnp.int32, shape, 0)
-    ci = lax.broadcasted_iota(jnp.int32, shape, 1)
-    lane = lax.broadcasted_iota(jnp.int32, shape, 2)
-    hit = (source // span == 7 - lane // SWIN) & (source % span == SWIN - 1 + ci - lane % SWIN)
-    return hit.astype(F32).reshape(8 * span, SWIN * 128)
+    k, b, ci, lane = np.ogrid[0:8, 0:span, 0:SWIN, 0:128]
+    hit = (k == 7 - lane // SWIN) & (b == SWIN - 1 + ci - lane % SWIN)
+    return hit.reshape(8 * span, SWIN * 128).astype(np.float32)
 
 
 def pick_st():
     span = 2 * TWIN - 1
-    shape = (span * span, TWIN, 128)
-    source = lax.broadcasted_iota(jnp.int32, shape, 0)
-    ci = lax.broadcasted_iota(jnp.int32, shape, 1)
-    lane = lax.broadcasted_iota(jnp.int32, shape, 2)
-    row = span - 1 - lane // TWIN
-    hit = (source // span == row) & (source % span == TWIN - 1 + ci - lane % TWIN)
-    return hit.astype(F32).reshape(span * span, TWIN * 128)
+    r, b, ci, lane = np.ogrid[0:span, 0:span, 0:TWIN, 0:128]
+    hit = (r == span - 1 - lane // TWIN) & (b == TWIN - 1 + ci - lane % TWIN)
+    return hit.reshape(span * span, TWIN * 128).astype(np.float32)
 
 
 def spread_sp(table):
@@ -310,7 +304,7 @@
 GATHER_TAIL = 6
 
 
-def gather_tick(t, n, nz, where, shard, full, local, up_s, up_r, dn_s, dn_r, y_s, y_r, x_s, x_r, c_s, c_r):
+def gather_tick(t, n, nz, where, wide, shard, full, local, up_s, up_r, dn_s, dn_r, y_s, y_r, x_s, x_r, c_s, c_r):
     clip, z, y, c, x = where
     last = nz - 1
     steps = nz - 1
@@ -407,8 +401,8 @@
     for k in range(steps + 4):
         i = t - k
         valid = jnp.logical_and(i >= 0, i < n)
-        third = lax.rem(i + 3, 3) == 2
-        for hi, chosen in ((640, jnp.logical_not(third)), (768, third)):
+        larger = lax.rem(i + 3, 3) < wide
+        for hi, chosen in ((640, jnp.logical_not(larger)), (768, larger)):
             @pl.when(jnp.logical_and(valid, chosen))
             def _(i=i, hi=hi, k=k):
                 phases(i, hi)[k]()
@@ -748,7 +742,7 @@
 
 
 FRONT_ROWS = 256
-GATHER_US = 8.5
+GATHER_US = 6.0
 
 
 def forward_plan(tokens, width):
@@ -768,7 +762,7 @@
         for step in range(lo, hi):
             before = done
             while done < total and (done < need.get(step, 0) or clock - last >= GATHER_US):
-                early = 4.0 if done < 7 else GATHER_US
+                early = 3.0 if done < 6 else GATHER_US
                 clock = max(clock, last + early)
                 last = clock
                 done += 1
@@ -778,10 +772,10 @@
 
 
 def forward_body(
-    spatial, shapes, n_own, own_first, counts, total, nz,
+    spatial, shapes, wide, n_own, own_first, counts, total, nz,
     s_ref, m_ref, b_ref, ok_ref, shard_hbm, prev_hbm,
-    na_ref, qkv_ref, att_ref, p_ref, proj_ref, mid_ref, nm_ref, act_ref, dact_ref, down_ref, res_ref, full_hbm,
-    n_scr, q_scr, a_scr, acc_ref, mid_scr, bias_ref, w_scr, d_scr, w_sem, d_sem, *sems,
+    na_ref, qkv_ref, att_ref, p_ref, proj_ref, mid_ref, nm_ref, act_ref, dact_ref, down_ref, res_ref, full_hbm, peer_hbm,
+    n_scr, q_scr, a_scr, acc_ref, mid_scr, bias_ref, w_scr, d_scr, w_sem, d_sem, send_ref, send_sem, peer_sem, *sems,
 ):
     n_win, n_query, n_key, chunk = shapes
     tokens, width = acc_ref.shape
@@ -802,7 +796,7 @@
             hi = hi + count * (step >= s).astype(jnp.int32)
 
     def tick(t, carry):
-        gather_tick(t, n_own, nz, where, shard_hbm, full_hbm, *sems)
+        gather_tick(t, n_own, nz, where, wide, shard_hbm, full_hbm, *sems)
         return carry
 
     lax.fori_loop(lo, hi, tick, 0)
@@ -928,9 +922,25 @@
         down_ref[...] = down.astype(BF16)
         res_ref[...] = (mid_scr[rows, :] + m_ref[5:6, :] * down).astype(res_ref.dtype)
 
+    clip, _, _, _, x = where
+
+    def to_peer(k):
+        return remote(send_ref.at[k], peer_hbm.at[k], send_sem.at[k], peer_sem.at[k], clip, 1 - x)
+
+    if spatial:
+        @pl.when(step >= a6)
+        def _():
+            half = FRONT_ROWS // 2
+            theirs = pl.ds(pl.multiple_of((1 - x) * half, half), half)
+            send_ref[step - a6] = res_ref[theirs, :].astype(BF16)
+            to_peer(step - a6).start()
+
     @pl.when(step == end - 1)
     def _():
         lax.fori_loop(sum(counts), total, tick, 0)
+        if spatial:
+            for k in range(send_ref.shape[0]):
+                to_peer(k).wait()
 
 
 DOWN_ITEMS = (4, 5, 8, 9)
@@ -938,13 +948,13 @@
 PREV_ITEMS = 12
 
 
-def block_forward(stream, mods, shard, prev, own_first, spread, key_ok, spatial, result_type, nz, cid):
+def block_forward(stream, mods, shard, wide, n_own, prev, own_first, spread, key_ok, spatial, result_type, nz, cid):
     tokens, width = stream.shape
     shapes = attention_shapes(spatial, tokens)
     n_win, n_query, n_key, _ = shapes
     pairs = width // 128
     a0, a1, a2, a3, a4, a5, a6, end = starts = forward_plan(tokens, width)
-    n_own = shard.shape[0]
+    n_send = tokens // FRONT_ROWS
     tail = spread.shape[1:]
     zeros = (0,) * len(tail)
     need = {}
@@ -968,7 +978,7 @@
     heads = at(a2, a3)
     anywhere = pl.BlockSpec(memory_space=pl.ANY)
     hidden = pl.BlockSpec((tokens, width), lambda i: (0, at(a5, a6)(i)))
-    body = functools.partial(forward_body, spatial, shapes, n_own, own_first, counts, total, nz)
+    body = functools.partial(forward_body, spatial, shapes, wide, n_own, own_first, counts, total, nz)
     extra = [] if prev is None else [prev]
     if prev is None:
         whole = body
@@ -1001,6 +1011,7 @@
             row_block(at(a6, end)),
             row_block(at(a6, end)),
             anywhere,
+            anywhere,
         ],
         out_shape=[
             bf16_rows,
@@ -1015,6 +1026,7 @@
             bf16_rows,
             jax.ShapeDtypeStruct((tokens, width), result_type),
             jax.ShapeDtypeStruct((n_own, nz, 2, 2, ROWS, COLS), BF16),
+            jax.ShapeDtypeStruct((n_send, FRONT_ROWS // 2, width), BF16),
         ],
         scratch_shapes=[
             pltpu.VMEM((tokens, width), BF16),
@@ -1027,14 +1039,18 @@
             pltpu.VMEM((2, 2, nz // 2, 2, 2, ROWS, COLS), BF16),
             dma((2,)),
             dma((2, 2)),
+            pltpu.VMEM((n_send, FRONT_ROWS // 2, width), BF16),
+            dma((n_send,)),
+            dma((n_send,)),
         ] + gather_sems(n_own, nz),
         compiler_params=pltpu.CompilerParams(
             collective_id=cid, has_side_effects=True, vmem_limit_bytes=64 * MIB
         ),
         name="block_forward",
     )(stream, mods, spread, key_ok, shard, *extra)
-    normed_a, qkv, att, probs, proj, mid, normed_m, act, dact, down, result, full = outs
-    return result, (stream, normed_a, qkv, probs, att, proj, mid, normed_m, act, dact, down), full
+    normed_a, qkv, att, probs, proj, mid, normed_m, act, dact, down, result, full, peer = outs
+    saved = (stream, normed_a, qkv, probs, att, proj, mid, normed_m, act, dact, down)
+    return result, saved, full, peer
 
 
 def norm_back_rows(values, scale_row, grad):
@@ -1049,7 +1065,7 @@
 
 
 BLOCK_ROWS = 128
-TICK_US = 8.0
+TICK_US = (5.5, 6.5)
 
 
 def backward_plan(tokens, width):
@@ -1057,7 +1073,7 @@
     chunks = 4 * width // CHUNK
     halves = width // CHUNK
     pairs = width // 128
-    sizes = (rows, chunks, rows, halves, pairs, 3 * halves, rows)
+    sizes = (rows, chunks, rows, halves, pairs, 3 * halves, rows, 3 * halves)
     starts = [0]
     for size in sizes:
         starts.append(starts[-1] + size)
@@ -1067,22 +1083,20 @@
 def backward_body(
     spatial, shapes, n_prev, n_own, tick_steps, nz,
     g_ref, down_ref, mid_ref, proj_ref, s_ref, m_ref, act_ref, dact_ref, w_ref, up_ref, dn_ref,
-    q_ref, k_ref, v_ref, p_ref, nm_hbm, att_hbm, na_hbm, prev_hbm,
-    out_ref, dm_ref, rows_ref, grads_hbm, share_hbm,
+    q_ref, k_ref, v_ref, p_ref, nm_hbm, att_hbm, na_hbm, mixed_hbm, prev_hbm,
+    out_ref, dm_ref, rows_ref, grads_hbm, share_hbm, peer_hbm, swap_hbm,
     res_ref, gv_ref, e_ref, gm_ref, ga_ref, gq_ref, db_ref, gdb_ref, gub_ref,
-    res_sem, gd_sem, gu_sem, *comm,
+    res_sem, gd_sem, gu_sem, send_ref, send_sem, peer_sem, mix_sem, swap_sem, *comm,
 ):
     n_win, n_query, n_key, chunk = shapes
     tokens, width = e_ref.shape
     starts = backward_plan(tokens, width)
-    a0, a1, a2, a3, a4, a5, a6, end = starts
+    a0, a1, a2, a3, a4, a5, a6, a7, end = starts
     halves = width // CHUNK
     step = pl.program_id(0)
     where = place(4 * nz)
     n_items = n_prev + n_own
-    sources = []
-    if n_prev:
-        sources.append((prev_hbm, 8, n_prev))
+    sources = [(prev_hbm, 9, n_prev)] if n_prev else []
     sources.append((grads_hbm, 0, n_own))
 
     @pl.when(step == 0)
@@ -1202,6 +1216,8 @@
     def _():
         resident(na_hbm).start()
         ga_ref[...] = e_ref[...].astype(BF16)
+        for k in range(2):
+            put_cols(k, 8, 0).wait()
 
     @pl.when(jnp.logical_and(step >= a4, step < a5))
     def _():
@@ -1212,20 +1228,28 @@
             q_ref, k_ref, v_ref, ga_ref.at[:, lanes], p_ref, gq_ref, dm_ref, db_ref,
         )
 
-    @pl.when(step == a5)
-    def _():
-        resident(na_hbm).wait()
-
     @pl.when(jnp.logical_and(step >= a5, step < a6))
     def _():
         i = step - a5
-        put_cols(i, 8, 0).wait()
-        part = gq_ref[:, pl.ds(pl.multiple_of(i * CHUNK, CHUNK), CHUNK)]
-        keep_cols(i, dot_tn(res_ref[...], part).astype(BF16))
-        put_cols(i, 9 + i // halves, lax.rem(i, halves)).start()
-        add_e(i == 0, part, w_ref[0])
-
-    @pl.when(step >= a6)
+        add_e(i == 0, gq_ref[:, pl.ds(pl.multiple_of(i * CHUNK, CHUNK), CHUNK)], w_ref[0])
+
+    clip, _, _, _, x = where
+
+    def to_peer(k):
+        return remote(send_ref.at[k], peer_hbm.at[k], send_sem.at[k], peer_sem.at[k], clip, 1 - x)
+
+    def mixed_to_peer(k):
+        block = 4 * (k // 2) + 2 * (1 - x) + k % 2
+        rows = pl.ds(pl.multiple_of(block * BLOCK_ROWS, BLOCK_ROWS), BLOCK_ROWS)
+        return remote(mixed_hbm.at[rows], swap_hbm.at[k], mix_sem.at[k], swap_sem.at[k], clip, 1 - x)
+
+    if not spatial:
+        @pl.when(step == 0)
+        def _():
+            for k in range(send_ref.shape[0]):
+                mixed_to_peer(k).start()
+
+    @pl.when(jnp.logical_and(step >= a6, step < a7))
     def _():
         rows = rows_at(step - a6)
         out, shift, scale = norm_back_rows(s_ref[...].astype(F32), m_ref[1:2, :], e_ref[rows, :])
@@ -1233,6 +1257,32 @@
         rows_ref[0:1, :] += shift
         rows_ref[1:2, :] += scale
 
+    if not spatial:
+        block = step - a6
+        half = lax.rem(block, 4) // 2
+
+        @pl.when(jnp.logical_and(jnp.logical_and(step >= a6, step < a7), half == 1 - x))
+        def _():
+            k = 2 * (block // 4) + lax.rem(block, 2)
+            send_ref[k] = out_ref[...].astype(BF16)
+            to_peer(k).start()
+
+    @pl.when(step == a7)
+    def _():
+        resident(na_hbm).wait()
+
+    @pl.when(step >= a7)
+    def _():
+        i = step - a7
+
+        @pl.when(i >= 2)
+        def _():
+            put_cols(i, 8, 0).wait()
+
+        part = gq_ref[:, pl.ds(pl.multiple_of(i * CHUNK, CHUNK), CHUNK)]
+        keep_cols(i, dot_tn(res_ref[...], part).astype(BF16))
+        put_cols(i, 9 + i // halves, lax.rem(i, halves)).start()
+
     @pl.when(due)
     def _():
         tick(passed)
@@ -1247,10 +1297,14 @@
             return carry
 
         lax.fori_loop(len(tick_steps), n_items + REDUCE_TAIL, rest, 0)
+        if not spatial:
+            for k in range(send_ref.shape[0]):
+                to_peer(k).wait()
+                mixed_to_peer(k).wait()
 
 
 def plan_ticks(starts, spatial, ready, spacing):
-    takes = (0.6, 5.0, 0.9, 2.5, 3.6 if spatial else 4.6, 3.0, 0.9)
+    takes = (0.6, 5.0, 0.9, 2.5, 3.6 if spatial else 4.6, 1.7, 0.9, 1.7)
     steps, clock, last = [], 0.0, -spacing
     for section, (lo, hi) in enumerate(zip(starts, starts[1:])):
         for step in range(lo, hi):
@@ -1262,14 +1316,14 @@
     return tuple(steps)
 
 
-def block_backward(grad, saved, mods, w_first, first_base, w_second, second_base, spread_shape, spatial, out_type, prev, n_own, nz, cid):
+def block_backward(grad, saved, mods, w_first, first_base, w_second, second_base, spread_shape, spatial, out_type, mixed, prev, nz, cid):
     stream, normed_a, qkv, probs, att, proj, mid, normed_m, act, dact, down = saved
     tokens, width = mid.shape
     shapes = attention_shapes(spatial, tokens)
     n_win, n_query, n_key, _ = shapes
     pairs = width // 128
     halves = width // CHUNK
-    a0, a1, a2, a3, a4, a5, a6, end = backward_plan(tokens, width)
+    a0, a1, a2, a3, a4, a5, a6, a7, end = backward_plan(tokens, width)
     tail = spread_shape[1:]
     zeros = (0,) * len(tail)
 
@@ -1299,19 +1353,19 @@
     heads = at(a4, a5)
     hidden = pl.BlockSpec((tokens, CHUNK), lambda i: (0, at(a1, a2)(i)))
     anywhere = pl.BlockSpec(memory_space=pl.ANY)
-    n_prev = 0 if prev is None else 4
+    n_own = 9
+    n_prev = 0 if prev is None else 3
     n_items = n_prev + n_own
-    ready = [0] * n_prev
-    for done in (2, 4, 4, 4, 6, 8, 8, 8)[:n_own]:
-        ready.append(min(a1 + done + 1, a2))
-    tick_steps = plan_ticks((a0, a1, a2, a3, a4, a5, a6, end), spatial, ready, TICK_US)
     extra = [] if prev is None else [prev]
+    n_send = tokens // (2 * BLOCK_ROWS)
+    ready = [0] * n_prev + [a1 + 3, a1 + 5, a1 + 5, a1 + 5, a1 + 7, a2, a2, a2, a4]
+    tick_steps = plan_ticks((a0, a1, a2, a3, a4, a5, a6, a7, end), spatial, ready, TICK_US[spatial])
     body = functools.partial(backward_body, spatial, shapes, n_prev, n_own, tick_steps, nz)
     if prev is None:
         whole = body
 
         def body(*refs):
-            return whole(*refs[:18], None, *refs[18:])
+            return whole(*refs[:19], None, *refs[19:])
 
     dma = pltpu.SemaphoreType.DMA
     return pl.pallas_call(
@@ -1322,7 +1376,7 @@
             row_block(at(a0, a1)),
             row_block(at(a2, a3)),
             row_block(at(a2, a3)),
-            row_block(at(a6, end)),
+            row_block(at(a6, a7)),
             fixed(mods.shape),
             hidden,
             hidden,
@@ -1333,12 +1387,14 @@
             pl.BlockSpec((tokens, 128), lambda i: (0, pairs + heads(i))),
             pl.BlockSpec((tokens, 128), lambda i: (0, 2 * pairs + heads(i))),
             pl.BlockSpec((2, n_win, n_query, n_key), lambda i: (heads(i), 0, 0, 0)),
-            anywhere, anywhere, anywhere,
+            anywhere, anywhere, anywhere, anywhere,
         ] + [anywhere] * len(extra),
         out_specs=[
-            row_block(at(a6, end)),
+            row_block(at(a6, a7)),
             pl.BlockSpec((2,) + tail, lambda i: (heads(i),) + zeros),
             pl.BlockSpec((8, width), lambda i: (0, 0)),
+            anywhere,
+            anywhere,
             anywhere,
             anywhere,
         ],
@@ -1348,6 +1404,8 @@
             jax.ShapeDtypeStruct((8, width), F32),
             jax.ShapeDtypeStruct((12, nz, 2, 2, ROWS, COLS), BF16),
             jax.ShapeDtypeStruct((n_items, ROWS, COLS), F32),
+            jax.ShapeDtypeStruct((n_send, BLOCK_ROWS, width), BF16),
+            jax.ShapeDtypeStruct((n_send, BLOCK_ROWS, width), BF16),
         ],
         scratch_shapes=[
             pltpu.VMEM((tokens, width), BF16),
@@ -1362,31 +1420,40 @@
             dma,
             dma((2,)),
             dma((2,)),
+            pltpu.VMEM((n_send, BLOCK_ROWS, width), BF16),
+            dma((n_send,)),
+            dma((n_send,)),
+            dma((n_send,)),
+            dma((n_send,)),
         ] + reduce_scratch(nz),
         compiler_params=pltpu.CompilerParams(
             collective_id=cid, has_side_effects=True, vmem_limit_bytes=64 * MIB
         ),
         name="block_backward",
     )(grad, down, mid, proj, stream, mods, act, dact, w_first, w_second, w_second, qkv, qkv, qkv, probs,
-      normed_m, att, normed_a, *extra)
-
-
-def swap_rows(values, me, swap):
+      normed_m, att, normed_a, mixed, *extra)
+
+
+def swap_rows(values, me, swap, recv=None):
     keep = lax.dynamic_index_in_dim(values, me, 1, keepdims=False)
-    send = lax.dynamic_index_in_dim(values, 1 - me, 1, keepdims=False)
-    recv = lax.ppermute(send.astype(BF16), "frame", swap).astype(values.dtype)
+    if recv is None:
+        send = lax.dynamic_index_in_dim(values, 1 - me, 1, keepdims=False)
+        recv = lax.ppermute(send.astype(BF16), "frame", swap)
+    recv = recv.reshape(keep.shape).astype(values.dtype)
     first = jnp.where(me == 0, keep, recv)
     second = jnp.where(me == 0, recv, keep)
     full = jnp.concatenate([first, second], axis=0)
     return full.transpose(2, 0, 1, 3, 4).reshape(-1, values.shape[-1])
 
 
-def unswap_rows(values, me, swap, n_cw, f_l):
+def unswap_rows(values, me, swap, n_cw, f_l, recv=None):
     depth = values.shape[-1]
     full = values.reshape(n_cw, 2, f_l, TWIN, TWIN, depth)
     keep = lax.dynamic_index_in_dim(full, me, 1, keepdims=False)
-    send = lax.dynamic_index_in_dim(full, 1 - me, 1, keepdims=False)
-    recv = lax.ppermute(send.astype(BF16), "frame", swap).astype(values.dtype)
+    if recv is None:
+        send = lax.dynamic_index_in_dim(full, 1 - me, 1, keepdims=False)
+        recv = lax.ppermute(send.astype(BF16), "frame", swap)
+    recv = recv.reshape(keep.shape).astype(values.dtype)
     first = jnp.where(me == 0, keep, recv)
     second = jnp.where(me == 0, recv, keep)
     both = jnp.stack([first, second], axis=0)
@@ -1395,14 +1462,10 @@
 
 def pack_shards(shards, b):
     w_qkv, w_proj, w_up, w_down = [w[:, b] for w in shards]
-    parts = []
-    for w in (w_qkv, w_proj):
-        parts.append(w.reshape(ROWS, -1, COLS).transpose(1, 0, 2))
-    parts.append(w_up.reshape(ROWS, 2, 8, 2, 128).transpose(3, 1, 0, 2, 4).reshape(4, ROWS, COLS))
+    first = w_qkv.reshape(ROWS, 3, COLS).transpose(1, 0, 2)
+    ups = w_up.reshape(ROWS, 2, 8, 2, 128).transpose(3, 1, 0, 2, 4).reshape(4, ROWS, COLS)
     downs = w_down.reshape(-1, ROWS, COLS)
-    ups = parts.pop()
-    parts += [downs[0:2], ups[0:2], downs[2:4], ups[2:4]]
-    return jnp.concatenate(parts, axis=0)
+    return [first, w_proj[None]], [downs[0:2], ups[0:2], downs[2:4], ups[2:4]]
 
 
 def on_device(
@@ -1416,7 +1479,8 @@
     natural = (f_l, 2, TWIN, n_cw, TWIN, width)
     shards = (w_qkv, w_proj, w_up, w_down)
     packed = [pack_shards(shards, b) for b in range(2)]
-    early = jnp.concatenate([packed[0], packed[1][:4]], axis=0)
+    early = jnp.concatenate(packed[0][0] + packed[0][1] + packed[1][0], axis=0)
+    late = jnp.concatenate(packed[1][1], axis=0)
     limit = n_cols - 3 * (2 - size_group[0])
     wide = (jnp.arange(n_cols, dtype=jnp.int32) < limit).astype(F32)
     ok_sp = jnp.broadcast_to(wide[None, None, None, :], (f_l, 1, n_rows, n_cols))
@@ -1429,24 +1493,25 @@
     mods = modulation[0].reshape(2, 6, width)
     mods = jnp.pad(mods, ((0, 0), (0, 2), (0, 0)))
     cot = swap_rows(cotangent.reshape(natural), me, swap)
-    stream0 = frames_in.reshape(-1, width).astype(F32)
-    mid_stream, saved0, full0 = block_forward(
-        stream0, mods[0], early, None, 0, spread0, ok_sp, True, F32, nz, 1
-    )
-    stream1 = swap_rows(mid_stream.reshape(natural), me, swap)
-    end_stream, saved1, full1 = block_forward(
-        stream1, mods[1], packed[1][4:], full0, 4, spread1, ok_st, False, BF16, nz, 5
+    stream0 = frames_in.reshape(-1, width)
+    mid_stream, saved0, full0, peer0 = block_forward(
+        stream0, mods[0], early, 2, 16, None, 0, spread0, ok_sp, True, F32, nz, 1
+    )
+    stream1 = swap_rows(mid_stream.reshape(natural), me, swap, peer0)
+    end_stream, saved1, full1, _ = block_forward(
+        stream1, mods[1], late, 1, 8, full0, 4, spread1, ok_st, False, BF16, nz, 5
     )
     full0 = full0.reshape(-1, width, width)
     full1 = full1.reshape(-1, width, width)
-    mixed = unswap_rows(end_stream, me, swap, n_cw, f_l).reshape(frames_in.shape)
-    grad1, gspread1, rows1, gw1, shares1 = block_backward(
-        cot, saved1, mods[1], full0, 12, full1, 0, spread1.shape, False, F32, None, 8, nz, 2
-    )
-    grad_mid = unswap_rows(grad1, me, swap, n_cw, f_l)
-    grad0, gspread0, rows0, gw0, shares0 = block_backward(
-        grad_mid, saved0, mods[0], full0, 0, full0, 4, spread0.shape, True, BF16, gw1, 8, nz, 3
-    )
+    grad1, gspread1, rows1, gw1, shares1, peer1, mixed1 = block_backward(
+        cot, saved1, mods[1], full0, 12, full1, 0, spread1.shape, False, F32, end_stream, None, nz, 2
+    )
+    mixed = unswap_rows(end_stream, me, swap, n_cw, f_l, mixed1).reshape(frames_in.shape)
+    grad_mid = unswap_rows(grad1, me, swap, n_cw, f_l, peer1)
+    grad0, gspread0, rows0, gw0, shares0, _, _ = block_backward(
+        grad_mid, saved0, mods[0], full0, 0, full0, 4, spread0.shape, True, BF16, end_stream, gw1, nz, 3
+    )
+
     def wide_pad(table):
         return jnp.pad(table, ((0, 0), (0, -table.shape[1] % 128)))
 
@@ -1455,7 +1520,8 @@
         wide_pad(gather_sp(gspread0)),
         wide_pad(gather_st(gspread1)),
     )
-    last, mods_sum, sp_sum, st_sum = reduce_last(gw0, (8, 4), small, nz, 4)
+    last, mods_sum, sp_sum, st_sum = reduce_last(gw0, (9, 3), small, nz, 4)
+
     def pair(first, second):
         return jnp.stack([first, second], axis=1)
 
@@ -1469,10 +1535,10 @@
     def down_of(items):
         return jnp.concatenate([items[2], items[3], items[6], items[7]], axis=0)
 
-    own0 = shares0[4:]
+    own0 = shares0[3:]
     outs = (
-        pair(qkv_of(last[1:]), qkv_of(shares0[1:4])),
-        pair(last[0], shares0[0]),
+        pair(qkv_of(last), qkv_of(shares0[0:3])),
+        pair(own0[8], shares1[8]),
         pair(up_of(own0), up_of(shares1)),
         pair(down_of(own0), down_of(shares1)),
     )

time: 822 us -> 797 us (0.970)
  waiting for transfers between devices: 20.9 us -> 0.01 us
  local copies, waits for them, and re-layouts: 64.9 us -> 56 us
    ppermute x4 -> x1, waiting for transfers between devices: 20.9 us -> 0.01 us  [swap_rows(): recv = lax.ppermute(send.astype(BF16), 'frame', swap)]
    pallas_call x2, Pallas kernels: 314 us -> 328 us  [block_backward(): pl.pallas_call(body, grid=(end,), in_specs=[row_block(g_at), row_block(at...]
    unnamed x187 -> x72, local copies, waits for them, and re-layouts: 19.5 us -> 18.8 us
  transfers between devices with their start and end apart: 4 -> 1, of which waited for: 2 -> 0; matrix products, arithmetic and copies ran while one was open for 5% -> 5% of each run, Pallas kernels for 55% -> 40%
where the time goes in v3:
time: 797 us; the launch traced here: 789 us
  Pallas kernels  699 us (88%)
  local copies, waits for them, and re-layouts  56 us (7%)
  other arithmetic  21.5 us (3%)
    pallas_call x2, Pallas kernels, block_backward(): pl.pallas_call(body, grid=(end,), in_specs=[row_block(g_at), row_block(at...  328 us
    pallas_call x2, Pallas kernels, block_forward(): pl.pallas_call(body, grid=(end,), in_specs=[row_block(s_at), fixed(mods.s...  318 us
    pallas_call x1, Pallas kernels, reduce_last(): pl.pallas_call(functools.partial(reduce_kernel, pick, nz), out_shape=[jax...  53.1 us
    unnamed x72, local copies, waits for them, and re-layouts  18.8 us
  transfers between devices with their start and end apart: 1, of which 0 were waited for; matrix products, arithmetic and copies ran while one was open for 5% of the time, Pallas kernels for 40%

profile of v3, /device:TPU:0, one launch (start us, length us, event | category | flops | bytes accessed | tf_op | source)
XLA Modules:
  0.0 789.5 jit_solution(11368968168245011829)
XLA Ops:
  0.7 2.8 constant_dynamic-slice_fusion.2
  4.5 2.9 collective-permute-start
  9.7 1.4 fusion.11
  13.5 1.2 copy.143
  14.8 3.3 slice_reduce_fusion.2
  18.1 5.2 slice_reduce_fusion
  23.6 2.7 slice_reduce_fusion.5
  28.4 2.8 slice_reduce_fusion.6
  32.1 1.5 fusion.17
  41.7 192.2 %block_forward.2 = (bf16[1024,1024]{1,0:T(8,128)(2,1)}, bf16[1024,3072]{1,0:T(8,128)(2,1)}, bf16[1024,1024]{1,0:T(8,128)(2,1)}, bf16[16,4,256,256]{3,2,1,0:T(8,1...) custom-call(bf16[1024,1024]{1,0:T(8,128)(2,1)} %bitcast.192, ...), custom_call_target="tpu_custom_call" | custom-call | tf_op jit(solution)/shard_map/block_forward/pallas_call | solution.py:991
  234.0 2.4 pad_maximum_fusion.7.shard_hbm
  236.3 2.2 bitcast_select_fusion.3
  238.5 2.5 pad_maximum_fusion
  241.0 125.8 %block_forward.3 = (bf16[1024,1024]{1,0:T(8,128)(2,1)}, bf16[1024,3072]{1,0:T(8,128)(2,1)}, bf16[1024,1024]{1,0:T(8,128)(2,1)}, bf16[16,2,512,384]{3,2,1,0:T(8,1...) custom-call(f32[1024,1024]{1,0:T(8,128)} %bitcast.188, ...), custom_call_target="tpu_custom_call" | custom-call | tf_op jit(solution)/shard_map/block_forward/pallas_call | solution.py:991
  366.8 1.7 bitcast_select_fusion.5
  368.5 1.5 pad_maximum_fusion.2
  370.0 167.3 %block_backward.2 = (f32[1024,1024]{1,0:T(8,128)}, f32[16,15,8,128]{3,2,1,0:T(8,128)}, f32[8,1024]{1,0:T(8,128)}, bf16[12,4,2,2,64,1024]{5,4,3,2,1,0:T(8,128)(2,...) custom-call(bf16[1024,1024]{1,0:T(8,128)(2,1)} %bitcast.194, ...), custom_call_target="tpu_custom_call" | custom-call | tf_op jit(solution)/shard_map/block_backward/pallas_call | solution.py:1371
  537.3 2.4 bitcast_select_fusion.1
  539.8 2.3 pad_maximum_fusion.1
  542.1 160.7 %block_backward.3 = (bf16[1024,1024]{1,0:T(8,128)(2,1)}, f32[16,4,16,128]{3,2,1,0:T(8,128)}, f32[8,1024]{1,0:T(8,128)}, bf16[12,4,2,2,64,1024]{5,4,3,2,1,0:T(8,1...) custom-call(f32[1024,1024]{1,0:T(8,128)} %bitcast.190, ...), custom_call_target="tpu_custom_call" | custom-call | tf_op jit(solution)/shard_map/block_backward/pallas_call | solution.py:1371
  702.7 1.3 fusion.15
  704.0 2.7 slice_bitcast_fusion.7
  708.8 2.0 fusion.3
  711.0 3.2 fusion
  714.2 1.8 reshape.221
  716.9 53.1 %reduce_last.1 = (f32[3,64,1024]{2,1,0:T(8,128)S(1)}, f32[16,1024]{1,0:T(8,128)S(1)}, f32[16,1024]{1,0:T(8,128)S(1)}, f32[16,3456]{1,0:T(8,128)S(1)}) custom-call(bf16[12,4,2,2,64,1024]{5,4,3,2,1,0:T(8,128)(2,1)} %get-tuple-element.80.grads, f32[16,1024]{1,0:T(8,128)S(1)} %select_maximum_fusion.small0, f32[16,1024]{1,0:T(8,128)S(1)} %pad.23.small1, ...), custom_call_target="tpu_custom_call" | custom-call | tf_op jit(solution)/shard_map/reduce_last/pallas_call | solution.py:701
  772.3 2.4 copy.79
  776.3 2.9 copy.81
  779.2 1.2 copy.80
  781.5 1.5 pad_maximum_fusion.3
  783.1 3.4 pad_maximum_fusion.4
  786.5 1.3 copy.155
  (116 shorter events, 25.8 us)
Async XLA Ops:
  0.6 8.3 %copy-start.23 = (f32[1,12,1024]{2,0,1:T(1,128)S(1)}, f32[1,12,1024]{2,0,1:T(1,128)}, u32[]{:S(2)}) copy-start(f32[1,12,1024]{2,0,1:T(1,128)} %param.16) | copy-start | bytes 147460
  3.4 5.7 copy-start.22
  3.4 5.9 copy-start.21
  3.4 6.2 copy-start.7
  4.5 362.4 %collective-permute-start = (bf16[4,8,2,8,1024]{4,3,1,0,2:T(8,128)(2,1)}, bf16[4,8,2,8,1024]{4,3,1,0,2:T(8,128)(2,1)}, u32[]{:S(2)}, u32[]{:S(2)}) collective-permute-start(bf16[4,8,2,8,1024]{4,3,1,0,2:T(8,128)(2,1)} %bitcast.174), channel_id=1, source_target_pairs={{0,1},{1,0},{2,3},{3,2},{4,5},{5,4},{6,7},{7,6},{8,9},{9,8},{10,11... | collective-permute-start | bytes 3145736 | tf_op jit(solution)/shard_map/ppermute | solution.py:1441
  9.3 2.7 copy-start.15
  9.7 2.7 copy-start.19
  12.4 2.4 copy-start.3
  13.5 4.5 copy-start.1
  28.0 4.1 copy-start.2
  233.9 2.4 copy-start.18
  704.0 2.7 copy-start.4
  706.7 1.9 copy-start.6
  706.7 2.0 copy-start.20
  710.9 6.0 copy-start.24
  710.9 6.0 copy-start.25
  770.9 1.1 copy-start.12
  770.9 1.1 copy-start.13
  770.9 1.1 copy-start.14
  774.7 1.1 copy-start.9
  774.7 1.1 copy-start.10
  774.8 1.1 copy-start.11
  776.2 3.0 copy-start.16
  776.2 3.0 copy-start.17
  776.3 4.2 copy-start.8
  779.2 1.8 copy-start
  783.0 3.4 copy-start.5

commit v4 on v3

--- a/solution.py
+++ b/solution.py
@@ -742,7 +742,7 @@
 
 
 FRONT_ROWS = 256
-GATHER_US = 6.0
+GATHER_US = 5.0
 
 
 def forward_plan(tokens, width):
@@ -1310,7 +1310,8 @@
         for step in range(lo, hi):
             clock += takes[section]
             k = len(steps)
-            if (k >= len(ready) or step >= ready[k]) and clock - last >= spacing:
+            busy = section == 7 and not spatial
+            if not busy and (k >= len(ready) or step >= ready[k]) and clock - last >= spacing:
                 steps.append(step)
                 last = clock
     return tuple(steps)

time: 797 us -> 794 us (level)
  no operation moved by 1% of the time
where the time goes in v4:
time: 794 us; the launch traced here: 786 us
  Pallas kernels  696 us (88%)
  local copies, waits for them, and re-layouts  56 us (7%)
  other arithmetic  21.5 us (3%)
    pallas_call x2, Pallas kernels, block_backward(): pl.pallas_call(body, grid=(end,), in_specs=[row_block(g_at), row_block(at...  326 us
    pallas_call x2, Pallas kernels, block_forward(): pl.pallas_call(body, grid=(end,), in_specs=[row_block(s_at), fixed(mods.s...  316 us
    pallas_call x1, Pallas kernels, reduce_last(): pl.pallas_call(functools.partial(reduce_kernel, pick, nz), out_shape=[jax...  53.3 us
    unnamed x72, local copies, waits for them, and re-layouts  18.8 us
  transfers between devices with their start and end apart: 1, of which 0 were waited for; matrix products, arithmetic and copies ran while one was open for 5% of the time, Pallas kernels for 40%

profile of v4, /device:TPU:0, one launch (start us, length us, event | category | flops | bytes accessed | tf_op | source)
XLA Modules:
  0.0 786.3 jit_solution(13873170326437272009)
XLA Ops:
  0.7 2.8 constant_dynamic-slice_fusion.2
  4.5 2.9 collective-permute-start
  9.7 1.4 fusion.11
  13.5 1.2 copy.143
  14.8 3.3 slice_reduce_fusion.2
  18.1 5.2 slice_reduce_fusion
  23.6 2.7 slice_reduce_fusion.5
  28.4 2.8 slice_reduce_fusion.6
  32.1 1.5 fusion.17
  41.7 193.8 %block_forward.2 = (bf16[1024,1024]{1,0:T(8,128)(2,1)}, bf16[1024,3072]{1,0:T(8,128)(2,1)}, bf16[1024,1024]{1,0:T(8,128)(2,1)}, bf16[16,4,256,256]{3,2,1,0:T(8,1...) custom-call(bf16[1024,1024]{1,0:T(8,128)(2,1)} %bitcast.192, ...), custom_call_target="tpu_custom_call" | custom-call | tf_op jit(solution)/shard_map/block_forward/pallas_call | solution.py:991
  235.6 2.4 pad_maximum_fusion.7.shard_hbm
  238.0 2.2 bitcast_select_fusion.3
  240.1 2.5 pad_maximum_fusion
  242.6 122.4 %block_forward.3 = (bf16[1024,1024]{1,0:T(8,128)(2,1)}, bf16[1024,3072]{1,0:T(8,128)(2,1)}, bf16[1024,1024]{1,0:T(8,128)(2,1)}, bf16[16,2,512,384]{3,2,1,0:T(8,1...) custom-call(f32[1024,1024]{1,0:T(8,128)} %bitcast.188, ...), custom_call_target="tpu_custom_call" | custom-call | tf_op jit(solution)/shard_map/block_forward/pallas_call | solution.py:991
  365.0 1.7 bitcast_select_fusion.5
  366.7 1.5 pad_maximum_fusion.2
  368.2 165.4 %block_backward.2 = (f32[1024,1024]{1,0:T(8,128)}, f32[16,15,8,128]{3,2,1,0:T(8,128)}, f32[8,1024]{1,0:T(8,128)}, bf16[12,4,2,2,64,1024]{5,4,3,2,1,0:T(8,128)(2,...) custom-call(bf16[1024,1024]{1,0:T(8,128)(2,1)} %bitcast.194, ...), custom_call_target="tpu_custom_call" | custom-call | tf_op jit(solution)/shard_map/block_backward/pallas_call | solution.py:1372
  533.6 2.4 bitcast_select_fusion.1
  536.0 2.3 pad_maximum_fusion.1
  538.3 160.9 %block_backward.3 = (bf16[1024,1024]{1,0:T(8,128)(2,1)}, f32[16,4,16,128]{3,2,1,0:T(8,128)}, f32[8,1024]{1,0:T(8,128)}, bf16[12,4,2,2,64,1024]{5,4,3,2,1,0:T(8,1...) custom-call(f32[1024,1024]{1,0:T(8,128)} %bitcast.190, ...), custom_call_target="tpu_custom_call" | custom-call | tf_op jit(solution)/shard_map/block_backward/pallas_call | solution.py:1372
  699.3 1.3 fusion.15
  700.6 2.7 slice_bitcast_fusion.7
  705.3 2.0 fusion.3
  707.5 3.2 fusion
  710.7 1.8 reshape.221
  713.5 53.3 %reduce_last.1 = (f32[3,64,1024]{2,1,0:T(8,128)S(1)}, f32[16,1024]{1,0:T(8,128)S(1)}, f32[16,1024]{1,0:T(8,128)S(1)}, f32[16,3456]{1,0:T(8,128)S(1)}) custom-call(bf16[12,4,2,2,64,1024]{5,4,3,2,1,0:T(8,128)(2,1)} %get-tuple-element.80.grads, f32[16,1024]{1,0:T(8,128)S(1)} %select_maximum_fusion.small0, f32[16,1024]{1,0:T(8,128)S(1)} %pad.23.small1, ...), custom_call_target="tpu_custom_call" | custom-call | tf_op jit(solution)/shard_map/reduce_last/pallas_call | solution.py:701
  769.0 2.4 copy.79
  773.0 2.9 copy.81
  776.0 1.2 copy.80
  778.3 1.5 pad_maximum_fusion.3
  779.8 3.4 pad_maximum_fusion.4
  783.2 1.3 copy.155
  (116 shorter events, 25.8 us)
Async XLA Ops:
  0.6 8.3 %copy-start.23 = (f32[1,12,1024]{2,0,1:T(1,128)S(1)}, f32[1,12,1024]{2,0,1:T(1,128)}, u32[]{:S(2)}) copy-start(f32[1,12,1024]{2,0,1:T(1,128)} %param.16) | copy-start | bytes 147460
  3.4 5.7 copy-start.22
  3.4 5.9 copy-start.21
  3.4 6.2 copy-start.7
  4.5 360.5 %collective-permute-start = (bf16[4,8,2,8,1024]{4,3,1,0,2:T(8,128)(2,1)}, bf16[4,8,2,8,1024]{4,3,1,0,2:T(8,128)(2,1)}, u32[]{:S(2)}, u32[]{:S(2)}) collective-permute-start(bf16[4,8,2,8,1024]{4,3,1,0,2:T(8,128)(2,1)} %bitcast.174), channel_id=1, source_target_pairs={{0,1},{1,0},{2,3},{3,2},{4,5},{5,4},{6,7},{7,6},{8,9},{9,8},{10,11... | collective-permute-start | bytes 3145736 | tf_op jit(solution)/shard_map/ppermute | solution.py:1442
  9.3 2.7 copy-start.15
  9.7 2.7 copy-start.19
  12.4 2.4 copy-start.3
  13.5 4.5 copy-start.1
  28.0 4.1 copy-start.2
  235.6 2.4 copy-start.18
  700.6 2.7 copy-start.4
  703.3 1.9 copy-start.6
  703.3 2.0 copy-start.20
  707.5 6.0 copy-start.24
  707.5 6.0 copy-start.25
  767.6 1.1 copy-start.12
  767.7 1.1 copy-start.13
  767.7 1.1 copy-start.14
  771.5 1.1 copy-start.9
  771.5 1.1 copy-start.10
  771.5 1.1 copy-start.11
  773.0 3.0 copy-start.16
  773.0 3.0 copy-start.17
  773.0 4.2 copy-start.8
  776.0 1.8 copy-start
  779.8 3.4 copy-start.5
